TPU v7x, 32 devices: a whole 2x2x4 slice. The times are simulated.
32 devices in a mesh: row: 4 (over z), col: 8 (over y, x, core).
Axes of the slice: x: 2, y: 2, z: 4, core: 2. Of those that a mesh axis runs over, the one named last changes fastest.
Arguments:
- tile_u: bfloat16 [32, 8, 2048, 128], P('row', 'col'), may hold values from -6 to 6
- tile_v: bfloat16 [32, 8, 2048, 128], P('row', 'col'), may hold values from -0.5 to 0.5
- tile_rank: int32 [32, 8], P('row', 'col'), may hold values from 16 to 128, as said below
- listed: int32 [32, 8], P('row', 'col'), may hold values from 0 to 1, as said below
- row_u: bfloat16 [32, 2048, 128], P('row', 'col'), may hold values from -6 to 6
- row_v: bfloat16 [32, 2048, 128], P('row', 'col'), may hold values from -0.5 to 0.5
- row_rank: int32 [32], P('row'), may hold values from 16 to 128
- col_u: bfloat16 [8, 2048, 128], P('col', 'row'), may hold values from -6 to 6
- col_v: bfloat16 [8, 2048, 128], P('col', 'row'), may hold values from -0.5 to 0.5
- col_rank: int32 [8], P('col'), may hold values from 16 to 112
- sketch: bfloat16 [2048, 128], replicated, may hold values from -0.125 to 0.125
Outputs:
- out_u: bfloat16 [32, 8, 2048, 128], P('row', 'col')
- out_v: bfloat16 [32, 8, 2048, 128], P('row', 'col')
Inputs may be any that keep to these rules, and one draw needn't show every extreme that they name: A tile with listed 0 has tile_rank plus the col_rank of its column at most 128; a tile with listed 1 has more than 128. The tiles of one device are tile rows a * 8 to a * 8 + 7 and tile columns b * 1 to b + 1 - 1 for its indices a along row and b along col. Two devices of the same row index whose col indices differ by 4 hold together at most 8 listed tiles; some device holds 8.
All inputs are finite; a program needn't handle non-finite values.
Results may differ from a plain program's by a relative error of at most 0.0072.
Values may be sent and summed in bfloat16 or wider, within the bound.
No kernel may reach another device: no remote copies, remote signals or barrier semaphores. Data moves between devices by JAX's collectives and lax.ppermute only.
A program may use at most 192 MiB of HBM per device.

v0:
```python
import jax
import jax.numpy as jnp
from jax import lax
from jax.sharding import PartitionSpec as P


def masked(factor, rank):
    width = factor.shape[-1]
    keep = lax.broadcasted_iota(jnp.int32, (width,), 0) < rank[..., None]
    return factor * keep[..., None, :].astype(factor.dtype)


def recompress(unew, vnew, sketch):
    f32 = jnp.float32
    proj = jnp.einsum("nbq,bs->nqs", vnew, sketch, preferred_element_type=f32).astype(jnp.bfloat16)
    span = jnp.einsum("nbq,nqs->nbs", unew, proj, preferred_element_type=f32)
    gram = jnp.einsum("nbs,nbt->nst", span, span, precision=lax.Precision.HIGHEST)
    columns = gram.shape[-1]
    level = jnp.trace(gram, axis1=1, axis2=2) / columns
    eye = jnp.eye(columns, dtype=jnp.float32)
    gram = gram + (0.01 * level + 1e-06)[:, None, None] * eye
    factor = jnp.linalg.cholesky(gram)
    basis = lax.linalg.triangular_solve(factor, span, left_side=False, lower=True, transpose_a=True)
    order = span.shape[1]
    new_u = (basis * jnp.sqrt(jnp.float32(order))).astype(jnp.bfloat16)
    coef = (jnp.einsum("nbq,nbs->nqs", unew, new_u, preferred_element_type=f32) / order).astype(
        jnp.bfloat16
    )
    new_v = jnp.einsum("nbq,nqs->nbs", vnew, coef, preferred_element_type=f32).astype(jnp.bfloat16)
    return (new_u, new_v)


def on_device(
    tile_u, tile_v, tile_rank, listed, row_u, row_v, row_rank, col_u, col_v, col_rank, sketch
):
    f32 = jnp.float32
    bf16 = jnp.bfloat16
    pan_u, pan_v = (
        lax.all_gather(row_u, "col", axis=1, tiled=True),
        lax.all_gather(row_v, "col", axis=1, tiled=True),
    )
    side_u, side_v = (
        lax.all_gather(col_u, "row", axis=1, tiled=True),
        lax.all_gather(col_v, "row", axis=1, tiled=True),
    )
    tile_u = masked(tile_u, tile_rank)
    tile_v = masked(tile_v, tile_rank)
    pan_u = masked(pan_u, row_rank)
    pan_v = masked(pan_v, row_rank)
    side_u = masked(side_u, col_rank)
    side_v = masked(side_v, col_rank)
    core = jnp.einsum("ibr,jbs->ijrs", pan_v, side_v, preferred_element_type=f32).astype(bf16)
    left = jnp.einsum("ibr,ijrs->ijbs", pan_u, core, preferred_element_type=f32).astype(bf16)
    rows_here, cols_here, order, width = tile_u.shape
    target = lax.broadcasted_iota(jnp.int32, (width, width), 1)
    source = lax.broadcasted_iota(jnp.int32, (width, width), 0)
    shift = (target == source + tile_rank[:, :, None, None]).astype(bf16)
    plain_u = (
        tile_u.astype(f32) + jnp.einsum("ijbr,ijrc->ijbc", left, shift, preferred_element_type=f32)
    ).astype(bf16)
    plain_v = (
        tile_v.astype(f32) - jnp.einsum("jbr,ijrc->ijbc", side_u, shift, preferred_element_type=f32)
    ).astype(bf16)
    minus_side = jnp.broadcast_to(-side_u[None], (rows_here,) + side_u.shape)
    count = rows_here * cols_here
    unew = jnp.concatenate([tile_u, left], axis=-1).reshape(count, order, 2 * width)
    vnew = jnp.concatenate([tile_v, minus_side], axis=-1).reshape(count, order, 2 * width)
    done_u, done_v = recompress(unew, vnew, sketch)
    out_width = done_u.shape[-1]
    done_u = done_u.reshape(rows_here, cols_here, order, out_width)
    done_v = done_v.reshape(rows_here, cols_here, order, out_width)
    pick = listed[:, :, None, None] == 1
    return (jnp.where(pick, done_u, plain_u), jnp.where(pick, done_v, plain_v))


def solution(mesh):
    return jax.shard_map(
        on_device,
        mesh=mesh,
        in_specs=(
            P("row", "col", None, None),
            P("row", "col", None, None),
            P("row", "col"),
            P("row", "col"),
            P("row", "col", None),
            P("row", "col", None),
            P("row"),
            P("col", "row", None),
            P("col", "row", None),
            P("col"),
            P(),
        ),
        out_specs=(P("row", "col", None, None), P("row", "col", None, None)),
        check_vma=False,
    )
```

profile of v0, /device:TPU:0, one launch (start us, length us, event | category | flops | bytes accessed | tf_op | source)
XLA Modules:
  0.0 353.4 jit_solution(7592447937317604411)
XLA Ops:
  7.2 0.7 all-gather.3.cloned.1.call-update
  7.9 0.0 all-gather.5.cloned.1.call-start
  8.0 0.7 all-gather.5.cloned.1.call-update
  8.7 6.4 %copy.29 = bf16[8,1,2048,128]{2,3,0,1:T(8,128)(2,1)} copy(bf16[8,1,2048,128]{3,2,1,0:T(8,128)(2,1)} %param.11) | data formatting | bytes 8388608 | tf_op args[0]
  15.1 6.6 %copy.31 = bf16[8,1,2048,128]{2,3,0,1:T(8,128)(2,1)} copy(bf16[8,1,2048,128]{3,2,1,0:T(8,128)(2,1)} %param.12) | data formatting | bytes 8388608 | tf_op args[1]
  22.4 17.3 %all_gather.15 = bf16[1,2048,128]{2,1,0:T(8,128)(2,1)S(1)} all-gather(bf16[1,512,128]{2,1,0:T(8,128)(2,1)S(1)} %copy-done.6), channel_id=1, replica_groups=mesh['row'=4,'col'=8] {'row'}, dimensions={1}, use_global_device_ids=true | all-gather | bytes 655360 | tf_op jit(solution)/shard_map/all_gather | solution.py:43
  39.7 0.1 bitcast_negate_fusion
  39.8 0.2 copy.32
  40.1 16.1 %all_gather.12 = bf16[1,2048,128]{2,1,0:T(8,128)(2,1)S(1)} all-gather(bf16[1,512,128]{2,1,0:T(8,128)(2,1)S(1)} %copy-done.7), channel_id=1, replica_groups=mesh['row'=4,'col'=8] {'row'}, dimensions={1}, use_global_device_ids=true | all-gather | bytes 655360 | tf_op jit(solution)/shard_map/all_gather | solution.py:44
  56.2 0.1 fusion.48
  56.3 0.1 fusion.49
  56.4 5.8 %broadcast_multiply_fusion = (bf16[8,1,2048,128]{2,3,0,1:T(8,128)(2,1)S(1)}, bf16[8,1,2048,128]{2,3,0,1:T(8,128)(2,1)}) fusion(bf16[8,1,2048,128]{2,3,0,1:T(8,128)(2,1)} %copy.31, bf16[8,128]{1,0:T(8,128)(2,1)S(1)} %fusion.48, bf16[8,1,2048,128]{2,3,0,1:T(8,128)(2,1)} %copy.29), kind=kLoop, calls=%fused_computation.21 | loop fusion | flops 4194304 | bytes 16779264 | tf_op jit(solution)/shard_map/mul | solution.py:10
  62.2 2.0 copy-done.2
  64.1 3.3 fusion
  67.4 20.6 %all-gather.5.cloned.1.call-done = bf16[8,2048,128]{2,1,0:T(8,128)(2,1)} async-done(((bf16[8,256,128]{2,1,0:T(8,128)(2,1)}), bf16[8,2048,128]{2,1,0:T(8,128)(2,1)}) %all-gather.5.cloned.1.call-update) | async-done | bytes 4194320 | tf_op jit(solution)/shard_map/all_gather | solution.py:39
  88.0 7.7 %fusion.11 = bf16[8,128,2048]{2,1,0:T(8,128)(2,1)} fusion(bf16[8,2048,128]{2,1,0:T(8,128)(2,1)} %all-gather.5.cloned.1.call-done, bf16[8,128]{1,0:T(8,128)(2,1)S(1)} %fusion.49, bf16[8,2048,128]{2,1,0:T(8,128)(2,1)} %all-gather.3.cloned.1.call-done, bf16[1,2048,128]{2,1,0:T(8,128)(2,1)S(1)} %all_gather.12, bf16[128]{0:T(256)(128)(2,1)S(1)} %compare_convert_fusion), kind=kOutput, calls=%fused_computation.18 | convolution fusion | flops 1087504384 | bytes 13109504 | tf_op jit(solution)/shard_map/ibr,ijrs->ijbs/dot_general | solution.py:53
  95.7 2.5 broadcast_in_dim.21
  98.2 14.2 %fusion.5 = f32[8,2048,128]{2,1,0:T(8,128)} fusion(bf16[8,1,2048,128]{2,3,0,1:T(8,128)(2,1)} %bitcast.88, bf16[8,1,2048,128]{2,3,0,1:T(8,128)(2,1)} %get-tuple-element.7, bf16[8,1,2048,128]{2,3,0,1:T(8,128)(2,1)} %broadcast_in_dim.21, bf16[8,1,2048,128]{2,3,0,1:T(8,128)(2,1)} %copy-done.2, bf16[2048,128]{1,0:T(8,128)(2,1)S(1)} %copy-done), kind=kOutput, calls=%fused_computation.10 | convolution fusion | flops 2181300224 | bytes 25690112 | tf_op jit(solution)/shard_map/nbq,nqs->nbs/dot_general | solution.py:16
  112.4 19.3 %select_reduce_fusion.1 = (f32[8]{0:T(128)S(1)}, f32[8,128,128]{2,1,0:T(8,128)S(1)}) fusion(pred[128,128]{1,0:T(8,128)(4,1)S(1)} %iota_compare_fusion.1, f32[8,2048,128]{2,1,0:T(8,128)} %fusion.5), kind=kOutput, calls=%fused_computation.40 | convolution fusion | flops 3221487616 | bytes 8929312 | tf_op jit(solution)/shard_map/nbs,nbt->nst/dot_general | solution.py:17
  131.7 0.2 copy.35
  132.0 0.2 fusion.34
  132.1 93.8 %custom-call.7 = f32[8,128,128]{2,1,0:T(8,128)S(1)} custom-call(f32[8,128,128]{2,1,0:T(8,128)S(1)} %fusion.34), custom_call_target="Cholesky" | custom-call | tf_op jit(solution)/shard_map/jit(cholesky)/cholesky | solution.py:22
  225.9 0.1 select_reduce_fusion
  226.0 0.1 compare_reduce_fusion
  226.1 0.1 select_bitcast_fusion
  226.2 78.8 %custom-call.8 = f32[8,1,128,128]{2,3,1,0:T(8,128)S(1)} custom-call(f32[8,1,128,128]{3,2,1,0:T(8,128)S(1)} %select_bitcast_fusion), custom_call_target="InvertDiagBlocksLowerTriangular" | custom-call | tf_op jit(solution)/shard_map/triangular_solve | solution.py:23
  305.1 10.4 %multiply_convert_fusion = bf16[8,2048,128]{1,2,0:T(8,128)(2,1)S(1)} fusion(f32[8,2048,128]{2,1,0:T(8,128)} %fusion.5, f32[8,1,128,128]{2,3,1,0:T(8,128)S(1)} %custom-call.8), kind=kOutput, calls=%fused_computation.6 | convolution fusion | flops 3225419776 | bytes 13107200 | tf_op jit(solution)/shard_map/triangular_solve | solution.py:23
  315.5 2.0 copy-done.5
  317.4 3.9 %bitcast_select_fusion.1 = bf16[8,1,2048,128]{2,3,0,1:T(8,128)(2,1)} fusion(bf16[8,2048,128]{1,2,0:T(8,128)(2,1)S(1)} %multiply_convert_fusion, pred[8]{0:T(512)(128)(4,1)S(1)} %compare_bitcast_fusion, bf16[8,128,2048]{2,1,0:T(8,128)(2,1)S(1)} %copy-done.4, bf16[8,1,2048,128]{2,3,0,1:T(8,128)(2,1)S(1)} %copy-done.3, s32[8]{0:T(128)S(1)} %bitcast.92), kind=kOutput, calls=%fused_computation.13 | convolution fusion | flops 545521664 | bytes 16777256 | tf_op jit(solution)/shard_map/ijbr,ijrc->ijbc/dot_general | solution.py:59
  321.3 12.3 %bitcast_select_fusion = bf16[8,1,2048,128]{2,3,0,1:T(8,128)(2,1)} fusion(bf16[8,1,2048,128]{2,3,0,1:T(8,128)(2,1)} %fusion, pred[8]{0:T(512)(128)(4,1)S(1)} %compare_bitcast_fusion, bf16[8,1,2048,128]{2,3,0,1:T(8,128)(2,1)} %broadcast_in_dim.21, bf16[8,1,2048,128]{2,3,0,1:T(8,128)(2,1)} %copy-done.2, bf16[8,2048,128]{1,2,0:T(8,128)(2,1)} %copy-done.5, ...), kind=kOutput, calls=%fused_computation.12 | convolution fusion | flops 2185756672 | bytes 29360136 | tf_op jit(solution)/shard_map/nbq,nqs->nbs/dot_general | solution.py:29
  333.7 6.5 %copy.44 = bf16[8,1,2048,128]{3,2,1,0:T(8,128)(2,1)} copy(bf16[8,1,2048,128]{2,3,0,1:T(8,128)(2,1)} %bitcast_select_fusion) | data formatting | bytes 8388608
  340.2 6.4 %copy.43 = bf16[8,1,2048,128]{3,2,1,0:T(8,128)(2,1)} copy(bf16[8,1,2048,128]{2,3,0,1:T(8,128)(2,1)} %bitcast_select_fusion.1) | data formatting | bytes 8388608
  (28 shorter events, 0.2 us)
Async XLA Ops:
  7.2 91.1 %copy-start = (bf16[2048,128]{1,0:T(8,128)(2,1)S(1)}, bf16[2048,128]{1,0:T(8,128)(2,1)}, u32[]{:S(2)}) copy-start(bf16[2048,128]{1,0:T(8,128)(2,1)} %param.21) | copy-start | bytes 1572868
  7.2 60.2 %all-gather.3.cloned.1.call-start = ((), (), s32[]{:S(2)}) async-start(), calls=%async_computation | async-start | bytes 4718592 | tf_op jit(solution)/shard_map/all_gather | solution.py:40
  7.9 80.1 %all-gather.5.cloned.1.call-start = ((), (), s32[]{:S(2)}) async-start(), calls=%async_computation.1 | async-start | bytes 4718592 | tf_op jit(solution)/shard_map/all_gather | solution.py:39
  15.1 7.2 %copy-start.6 = (bf16[1,512,128]{2,1,0:T(8,128)(2,1)S(1)}, bf16[1,512,128]{2,1,0:T(8,128)(2,1)}, u32[]{:S(2)}) copy-start(bf16[1,512,128]{2,1,0:T(8,128)(2,1)} %param.18) | copy-start | bytes 393220
  15.1 25.0 %copy-start.7 = (bf16[1,512,128]{2,1,0:T(8,128)(2,1)S(1)}, bf16[1,512,128]{2,1,0:T(8,128)(2,1)}, u32[]{:S(2)}) copy-start(bf16[1,512,128]{2,1,0:T(8,128)(2,1)} %param.19) | copy-start | bytes 393220
  15.1 41.1 %copy-start.10 = (s32[8,1]{0,1:T(1,128)S(1)}, s32[8,1]{0,1:T(1,128)}, u32[]{:S(2)}) copy-start(s32[8,1]{0,1:T(1,128)} %param.14) | copy-start | bytes 100
  15.1 41.1 %copy-start.8 = (s32[8,1]{0,1:T(1,128)S(1)}, s32[8,1]{0,1:T(1,128)}, u32[]{:S(2)}) copy-start(s32[8,1]{0,1:T(1,128)} %param.13) | copy-start | bytes 100
  15.1 41.2 %copy-start.9 = (s32[8]{0:T(128)S(1)}, s32[8]{0:T(128)}, u32[]{:S(2)}) copy-start(s32[8]{0:T(128)} %param.17) | copy-start | bytes 100
  62.2 2.0 copy-start.2
  305.1 12.4 %copy-start.3 = (bf16[8,1,2048,128]{2,3,0,1:T(8,128)(2,1)S(1)}, bf16[8,1,2048,128]{2,3,0,1:T(8,128)(2,1)}, u32[]{:S(2)}) copy-start(bf16[8,1,2048,128]{2,3,0,1:T(8,128)(2,1)} %get-tuple-element.7) | copy-start | bytes 12582916
  305.1 12.4 %copy-start.4 = (bf16[8,128,2048]{2,1,0:T(8,128)(2,1)S(1)}, bf16[8,128,2048]{2,1,0:T(8,128)(2,1)}, u32[]{:S(2)}) copy-start(bf16[8,128,2048]{2,1,0:T(8,128)(2,1)} %fusion.11) | copy-start | bytes 12582916
  315.5 2.0 copy-start.5
  333.7 12.9 %copy-start.1 = (bf16[2048,128]{1,0:T(8,128)(2,1)S(1)}, bf16[2048,128]{1,0:T(8,128)(2,1)}, u32[]{:S(2)}) copy-start(bf16[2048,128]{1,0:T(8,128)(2,1)} %param.21) | copy-start | bytes 1572868
Sparse Core Ops, SparseCore 0:
  9.9 39.4 all-gather.2
  51.3 36.7 all-gather.4
where the time goes:
time: 354 us; the launch traced here: 353 us
  other arithmetic  179 us (51%)
  matrix products  71.1 us (20%)
  blocking collectives  33.5 us (9%)
  local copies, waits for them, and re-layouts  32.8 us (9%)
  waiting for transfers between devices  22 us (6%)
  between operations  14.9 us (4%)
    another operation x4, other arithmetic, recompress(): factor = jnp.linalg.cholesky(gram)  94 us
    another operation x3, other arithmetic, recompress(): lax.linalg.triangular_solve(factor, span, left_side=False, lower=True, tr...  79 us
    unnamed x26, local copies, waits for them, and re-layouts  29.9 us
    all_gather x1, waiting for transfers between devices, on_device(): lax.all_gather(row_u, 'col', axis=1, tiled=True)  20.6 us
    dot_general x1, matrix products, recompress(): jnp.einsum('nbs,nbt->nst', span, span, precision=lax.Precision.HIGHEST)  19.3 us
    all_gather x1, blocking collectives, on_device(): lax.all_gather(col_u, 'row', axis=1, tiled=True)  17.3 us
    all_gather x1, blocking collectives, on_device(): lax.all_gather(col_v, 'row', axis=1, tiled=True)  16.1 us
    dot_general x1, matrix products, recompress(): span = jnp.einsum('nbq,nqs->nbs', unew, proj, preferred_element_type=f32)  14.2 us
  transfers between devices with their start and end apart: 2, of which 1 were waited for; matrix products, arithmetic and copies ran while one was open for 6% of the time, Pallas kernels for 0%

commit v1 on v0

v1 whole, which is shorter than its diff:
```python
import functools

import jax
import jax.numpy as jnp
from jax import lax
from jax.experimental import pallas as pl
from jax.experimental.pallas import tpu as pltpu
from jax.sharding import PartitionSpec as P

F32 = jnp.float32
BF16 = jnp.bfloat16
ANY = pl.BlockSpec(memory_space=pl.ANY)
SMEM = pl.BlockSpec(memory_space=pltpu.SMEM)
VMEM = pl.BlockSpec(memory_space=pltpu.VMEM)
MIB = 2**20


def dot(a, b, ca=1, cb=0):
    return lax.dot_general(a, b, (((ca,), (cb,)), ((), ())), preferred_element_type=F32)


def halves(x):
    high = x.astype(BF16)
    return high, (x - high.astype(F32)).astype(BF16)


def lanes(shape):
    return lax.broadcasted_iota(jnp.int32, shape, len(shape) - 1)


def rows_of(shape):
    return lax.broadcasted_iota(jnp.int32, shape, len(shape) - 2)


def local_kernel(rank_ref, u_ref, v_ref, st_ref, proj_ref, uu_ref):
    t = pl.program_id(0)
    proj = dot(st_ref[...], v_ref[0])
    keep = lanes(proj.shape) < rank_ref[t]
    proj_ref[0] = jnp.where(keep, proj, 0.0).astype(BF16)
    u = u_ref[0]
    uu_ref[0] = dot(u, u, 0, 0)


def core_kernel(masks, pos_ref, *refs):
    q_refs = refs[: len(masks)]
    mine_ref, other_ref, own_out, other_out = refs[len(masks) :]
    count, chunk, width = q_refs[0].shape
    depth = mine_ref.shape[2]
    sides = []
    for mask in masks:
        start = jnp.bitwise_xor(pos_ref[1], mask) * chunk
        piece = jnp.bitwise_xor(start // depth, pos_ref[0])
        inner = pl.multiple_of(start % depth, chunk)
        both = [ref[piece, 1, pl.ds(inner, chunk), :] for ref in (mine_ref, other_ref)]
        sides.append(jnp.concatenate(both, axis=1).astype(F32).T.astype(BF16))
    for t in range(0, count, 2):
        total = None
        for q_ref, side in zip(q_refs, sides):
            pair = jnp.concatenate([q_ref[t], q_ref[t + 1]], axis=1)
            part = dot(side, pair)
            total = part if total is None else total + part
        for k in range(2):
            block = total[:, k * width : (k + 1) * width]
            own_out[t + k] = block[:width]
            other_out[t + k] = block[width:]


def left_kernel(
    masks, pos_ref, row_rank_ref, col_rank_ref, own_ref, other_ref, u_ref, x_ref, st_ref, *refs
):
    p_refs = refs[: 2 * len(masks)]
    left_ref, gram_ref, core_ref, proj_ref = refs[2 * len(masks) :]
    t = pl.program_id(0)
    chunk = p_refs[0].shape[1]
    core = own_ref[0] + other_ref[0]
    keep = (lanes(core.shape) < row_rank_ref[t]) & (rows_of(core.shape) < col_rank_ref[0])
    core = jnp.where(keep, core, 0.0).astype(BF16)
    core_ref[0] = core
    total = None
    for k, mask in enumerate(masks):
        start = jnp.bitwise_xor(pos_ref[1] // 2, mask // 2) * (2 * chunk)
        start = pl.multiple_of(start, 2 * chunk)
        odd = pos_ref[1] % 2 == 1
        first, second = p_refs[2 * k][0], p_refs[2 * k + 1][0]
        panel = jnp.concatenate(
            [jnp.where(odd, second, first), jnp.where(odd, first, second)], axis=0
        )
        left = dot(panel, core, 1, 1).astype(BF16)
        left_ref[0, pl.ds(start, 2 * chunk), :] = left
        both = jnp.concatenate([u_ref[0, pl.ds(start, 2 * chunk), :], left], axis=1)
        part = dot(left, both, 0, 0)
        total = part if total is None else total + part
    gram_ref[0] = total

    @pl.when(t == 0)
    def _():
        pieces, depth = x_ref.shape[0], x_ref.shape[2]
        proj = None
        for k in range(pieces):
            start = jnp.bitwise_xor(pos_ref[0], k) * depth
            start = pl.multiple_of(start, depth)
            part = dot(st_ref[:, pl.ds(start, depth)], x_ref[k, 0])
            proj = part if proj is None else proj + part
        keep = lanes(proj.shape) < col_rank_ref[0]
        proj_ref[...] = jnp.where(keep, -proj, 0.0).astype(BF16)


def final_kernel(
    pos_ref,
    rank_ref,
    listed_ref,
    col_rank_ref,
    first_ref,
    second_ref,
    u_hbm,
    v_hbm,
    left_hbm,
    x_hbm,
    uu_ref,
    gram_ref,
    core_ref,
    vproj_ref,
    xproj_ref,
    out_u,
    out_v,
    u_buf,
    v_buf,
    left_buf,
    x_buf,
    to_u,
    to_v,
    gs,
    rs,
    ts,
    scales,
    sem_in,
    sem_x,
    sem_out,
    *,
    last_mask,
    block,
):
    count, order, width = u_hbm.shape
    chunk = first_ref.shape[1]
    pieces, depth = x_hbm.shape[0], x_hbm.shape[2]

    def fetch(which, t):
        src = (u_hbm, left_hbm, v_hbm)[which]
        dst = (u_buf, left_buf, v_buf)[which]
        return pltpu.make_async_copy(src.at[t], dst.at[t], sem_in.at[which, t])

    def fetch_x(k):
        start = jnp.bitwise_xor(pos_ref[0], k) * depth
        start = pl.multiple_of(start, depth)
        return pltpu.make_async_copy(x_hbm.at[k, 0], x_buf.at[pl.ds(start, depth), :], sem_x.at[k])

    def send(which, t):
        src = (to_u, to_v)[which]
        dst = (out_u, out_v)[which]
        return pltpu.make_async_copy(src.at[t], dst.at[t], sem_out.at[which, t])

    for t in range(count):
        fetch(0, t).start()
        fetch(1, t).start()
    for t in range(count):
        fetch(2, t).start()
    for k in range(pieces):
        fetch_x(k).start()

    odd = pos_ref[1] % 2 == 1
    start = jnp.bitwise_xor(pos_ref[1] // 2, last_mask // 2) * (2 * chunk)
    start = pl.multiple_of(start, 2 * chunk)
    square = (width, width)
    eye = rows_of(square) == lanes(square)

    def assemble(t, carry):
        fetch(0, t).wait()
        fetch(1, t).wait()
        first, second = first_ref[t], second_ref[t]
        panel = jnp.concatenate(
            [jnp.where(odd, second, first), jnp.where(odd, first, second)], axis=0
        )
        left = dot(panel, core_ref[t], 1, 1).astype(BF16)
        left_buf[t, pl.ds(start, 2 * chunk), :] = left
        both = jnp.concatenate([u_buf[t, pl.ds(start, 2 * chunk), :], left], axis=1)
        low = gram_ref[t] + dot(left, both, 0, 0)
        lu_h, lu_l = halves(low[:, :width])
        ll_h, ll_l = halves(low[:, width:])
        uu_h, uu_l = halves(uu_ref[t])
        a, b = vproj_ref[t], xproj_ref[...]
        left_part = dot(a, uu_h) + dot(a, uu_l) + dot(b, lu_h) + dot(b, lu_l)
        right_part = dot(a, lu_h, 1, 1) + dot(a, lu_l, 1, 1) + dot(b, ll_h) + dot(b, ll_l)
        moved = jnp.concatenate([left_part, right_part], axis=1)
        ts[t] = moved
        moved_h, moved_l = halves(moved)
        weights = jnp.concatenate([a, b], axis=1)
        gram = dot(moved_h, weights, 1, 1) + dot(moved_l, weights, 1, 1)
        diag = jnp.where(eye, gram, 0.0)
        trace = jnp.sum(jnp.sum(diag, axis=1, keepdims=True), axis=0, keepdims=True)
        scale = trace / width + 0.0001
        inverse = 1.0 / scale
        gs[pl.ds(pl.multiple_of(t * width, width), width), :] = gram * inverse + jnp.where(
            eye, 0.01, 0.0
        )
        scales[t] = jnp.broadcast_to(lax.rsqrt(scale), scales.shape[1:])
        return carry

    lax.fori_loop(0, count, assemble, 0)

    lane = lanes((count, width))
    for k0 in range(0, width, block):
        rows = [gs[pl.ds(k0 + r, count, stride=width), :] for r in range(block)]
        for k in range(block):
            at = k0 + k
            pivot = jnp.broadcast_to(rows[k][:, at : at + 1], (count, width))
            root = lax.rsqrt(pivot)
            inverse = root * root
            here = lane == at
            rs[pl.ds(at, count, stride=width), :] = jnp.where(here, 1.0, rows[k]) * root
            scaled = jnp.where(here, 1.0 + inverse, rows[k] * inverse)
            for r in range(k + 1, block):
                rows[r] = rows[r] - rows[r][:, at : at + 1] * scaled
        end = k0 + block
        if end < width:
            strip = (block, width)
            strip_lane = lanes(strip)
            own = k0 + rows_of(strip)
            for n in range(count):
                done = rs[pl.ds(n * width + k0, block), :]
                ahead = jnp.where(strip_lane >= end, done, 0.0)
                use = jnp.where((strip_lane > own) & (strip_lane < end), 0.0, done)
                a_h, a_l = halves(ahead)
                b_h, b_l = halves(use)
                a = jnp.concatenate([a_h, a_l, a_h], axis=0)
                b = jnp.concatenate([b_h, b_h, b_l], axis=0)
                change = dot(a, b, 0, 0)
                rest = pl.ds(n * width + end, width - end)
                old = gs[rest, :]
                gone = lanes(old.shape)
                old = jnp.where((gone >= k0) & (gone < end), 0.0, old)
                gs[rest, :] = old - change[end:]

    for k in range(pieces):
        fetch_x(k).wait()

    def finish(t, carry):
        tile_rank = rank_ref[t]
        picked = listed_ref[t] == 1
        inverse = rs[pl.ds(pl.multiple_of(t * width, width), width), :]
        inverse = jnp.where(lanes(square) <= rows_of(square), inverse, 0.0)
        inverse = inverse * (scales[t][:1, :1] * (float(order) ** 0.5))
        inv_h, inv_l = halves(inverse)
        weights = jnp.concatenate([vproj_ref[t], xproj_ref[...]], axis=1)
        mixed = dot(inv_h, weights) + dot(inv_l, weights)
        mixed_h, mixed_l = halves(mixed)
        moved_h, moved_l = halves(ts[t])
        coef = dot(inv_h, moved_h) + dot(inv_h, moved_l) + dot(inv_l, moved_h)
        coef = coef * (1.0 / order)
        wide = coef.shape
        col = lanes(wide)
        row = rows_of(wide)
        in_u = col < width
        keep = (col == row) & (col < tile_rank)
        moved_to = (col >= width) & (row == col - width + tile_rank)
        exact_u = jnp.where(keep | moved_to, 1.0, 0.0)
        moved_to = moved_to & (col - width < col_rank_ref[0])
        exact_v = jnp.where(keep, 1.0, jnp.where(moved_to, -1.0, 0.0))
        coef = jnp.where(in_u, jnp.where(col < tile_rank, coef, 0.0), -coef)
        coef = jnp.where(picked, coef, exact_v).astype(BF16)
        mixed_h = jnp.where(picked, mixed_h.astype(F32), exact_u).astype(BF16)
        mixed_l = jnp.where(picked, mixed_l.astype(F32), 0.0).astype(BF16)
        both = jnp.concatenate([mixed_h, mixed_l], axis=0)
        pair = jnp.concatenate([u_buf[t], left_buf[t]], axis=1)
        result = dot(pair, both, 1, 1)
        to_u[t] = (result[:, :width] + result[:, width:]).astype(BF16)
        send(0, t).start()
        fetch(2, t).wait()
        pair = jnp.concatenate([v_buf[t], x_buf[...]], axis=1)
        to_v[t] = dot(pair, coef, 1, 1).astype(BF16)
        send(1, t).start()
        return carry

    lax.fori_loop(0, count, finish, 0)

    def drain(t, carry):
        send(0, t).wait()
        send(1, t).wait()
        return carry

    lax.fori_loop(0, count, drain, 0)


def swap(x, axis, size, mask):
    return lax.ppermute(x, axis, [(c, c ^ mask) for c in range(size)])


def on_device(
    n_row,
    n_col,
    tile_u,
    tile_v,
    tile_rank,
    listed,
    row_u,
    row_v,
    row_rank,
    col_u,
    col_v,
    col_rank,
    sketch,
):
    rows_here, cols_here, order, width = tile_u.shape
    assert cols_here == 1 and width == sketch.shape[1]
    count = rows_here * cols_here
    chunk = row_u.shape[1]
    half = count // 2
    tile_u = tile_u.reshape(count, order, width)
    tile_v = tile_v.reshape(count, order, width)
    tile_rank = tile_rank.reshape(count)
    listed = listed.reshape(count)
    pos = jnp.stack([lax.axis_index("row"), lax.axis_index("col")]).astype(jnp.int32)
    col_swap = lambda x, mask: swap(x, "col", n_col, mask)
    dims = []
    mask = 2
    while mask < n_col:
        dims.append(mask)
        mask *= 2

    def spread(own, after=None):
        pieces = {0: own}
        first = [col_swap(own, m) for m in dims]
        for m, got in zip(dims, first):
            pieces[m] = got
        return pieces

    def spread_rest(pieces):
        if len(dims) == 2:
            low, high = dims
            a = col_swap(pieces[low][:half], high)
            b = col_swap(pieces[high][half:], low)
            pieces[low | high] = (a, b)
            return pieces
        for mask in range(2, n_col, 2):
            if mask not in pieces:
                bit = mask & -mask
                pieces[mask] = col_swap(pieces[mask ^ bit], bit)
        return pieces

    q = spread(row_v)
    sides = jnp.stack([col_u[0], col_v[0]])[None]
    mask = 1
    while mask < n_row:
        sides = jnp.concatenate([sides, swap(sides, "row", n_row, mask)], axis=0)
        mask *= 2
    sides_other = col_swap(sides, 1)
    turned = sketch.T

    vproj, uu = pl.pallas_call(
        local_kernel,
        grid_spec=pltpu.PrefetchScalarGridSpec(
            num_scalar_prefetch=1,
            grid=(count,),
            in_specs=[
                pl.BlockSpec((1, order, width), lambda t, r: (t, 0, 0)),
                pl.BlockSpec((1, order, width), lambda t, r: (t, 0, 0)),
                pl.BlockSpec((width, order), lambda t, r: (0, 0)),
            ],
            out_specs=[
                pl.BlockSpec((1, width, width), lambda t, r: (t, 0, 0)),
                pl.BlockSpec((1, width, width), lambda t, r: (t, 0, 0)),
            ],
        ),
        out_shape=[
            jax.ShapeDtypeStruct((count, width, width), BF16),
            jax.ShapeDtypeStruct((count, width, width), F32),
        ],
        compiler_params=pltpu.CompilerParams(vmem_limit_bytes=24 * MIB),
        cost_estimate=pl.CostEstimate(
            flops=4 * count * order * width * width,
            bytes_accessed=4 * count * order * width,
            transcendentals=0,
        ),
        name="local_products",
    )(tile_rank, tile_u, tile_v, turned)

    p_own, _ = lax.optimization_barrier((row_u, q[dims[-1]]))
    q = spread_rest(q)
    p = spread(p_own)
    masks = tuple(sorted(q))
    q_args = [
        jnp.concatenate(q[m], axis=0) if isinstance(q[m], tuple) else q[m] for m in masks
    ]
    part_shape = jax.ShapeDtypeStruct((count, width, width), F32)
    core_own, core_other = pl.pallas_call(
        functools.partial(core_kernel, masks),
        in_specs=[SMEM] + [VMEM] * (len(masks) + 2),
        out_specs=[VMEM, VMEM],
        out_shape=[part_shape, part_shape],
        compiler_params=pltpu.CompilerParams(vmem_limit_bytes=32 * MIB),
        cost_estimate=pl.CostEstimate(
            flops=2 * count * order * width * width,
            bytes_accessed=count * order * width,
            transcendentals=0,
        ),
        name="core_products",
    )(pos, *q_args, sides, sides_other)
    core_got = col_swap(core_other, 1)

    p = spread_rest(p)
    last = masks[-1]
    early = masks[:-1]
    mates = {m: col_swap(p[m], 1) for m in early}
    p_early = [x for m in early for x in (p[m], mates[m])]
    tile_spec = pl.BlockSpec((1, order, width), lambda t, *_: (t, 0, 0))
    small_spec = pl.BlockSpec((1, width, width), lambda t, *_: (t, 0, 0))
    piece_spec = pl.BlockSpec((1, chunk, width), lambda t, *_: (t, 0, 0))
    left, low, core, xproj = pl.pallas_call(
        functools.partial(left_kernel, early),
        grid_spec=pltpu.PrefetchScalarGridSpec(
            num_scalar_prefetch=3,
            grid=(count,),
            in_specs=[
                small_spec,
                small_spec,
                tile_spec,
                pl.BlockSpec(sides.shape, lambda t, *_: (0, 0, 0, 0)),
                pl.BlockSpec((width, order), lambda t, *_: (0, 0)),
            ]
            + [piece_spec] * len(p_early),
            out_specs=[
                tile_spec,
                pl.BlockSpec((1, width, 2 * width), lambda t, *_: (t, 0, 0)),
                small_spec,
                pl.BlockSpec((width, width), lambda t, *_: (0, 0)),
            ],
        ),
        out_shape=[
            jax.ShapeDtypeStruct((count, order, width), BF16),
            jax.ShapeDtypeStruct((count, width, 2 * width), F32),
            jax.ShapeDtypeStruct((count, width, width), BF16),
            jax.ShapeDtypeStruct((width, width), BF16),
        ],
        compiler_params=pltpu.CompilerParams(vmem_limit_bytes=32 * MIB),
        cost_estimate=pl.CostEstimate(
            flops=6 * count * order * width * width,
            bytes_accessed=6 * count * order * width,
            transcendentals=0,
        ),
        name="left_products",
    )(pos, row_rank, col_rank, core_own, core_got, tile_u, sides, turned, *p_early)

    tail = p[last]
    if isinstance(tail, tuple):
        mate = jnp.concatenate([col_swap(x, 1) for x in tail], axis=0)
        tail = jnp.concatenate(tail, axis=0)
    else:
        mate = col_swap(tail, 1)
    out_shape = jax.ShapeDtypeStruct((count, order, width), BF16)
    out_u, out_v = pl.pallas_call(
        functools.partial(final_kernel, last_mask=last, block=32),
        in_specs=[SMEM] * 4 + [VMEM] * 2 + [ANY] * 4 + [VMEM] * 5,
        out_specs=[ANY, ANY],
        out_shape=[out_shape, out_shape],
        scratch_shapes=[
            pltpu.VMEM((count, order, width), BF16),
            pltpu.VMEM((count, order, width), BF16),
            pltpu.VMEM((count, order, width), BF16),
            pltpu.VMEM((order, width), BF16),
            pltpu.VMEM((count, order, width), BF16),
            pltpu.VMEM((count, order, width), BF16),
            pltpu.VMEM((count * width, width), F32),
            pltpu.VMEM((count * width, width), F32),
            pltpu.VMEM((count, width, 2 * width), F32),
            pltpu.VMEM((count, 8, width), F32),
            pltpu.SemaphoreType.DMA((3, count)),
            pltpu.SemaphoreType.DMA((sides.shape[0],)),
            pltpu.SemaphoreType.DMA((2, count)),
        ],
        compiler_params=pltpu.CompilerParams(vmem_limit_bytes=48 * MIB),
        cost_estimate=pl.CostEstimate(
            flops=16 * count * order * width * width,
            bytes_accessed=10 * count * order * width,
            transcendentals=0,
        ),
        name="recompress_store",
    )(
        pos,
        tile_rank,
        listed,
        col_rank,
        tail,
        mate,
        tile_u,
        tile_v,
        left,
        sides,
        uu,
        low,
        core,
        vproj,
        xproj,
    )
    shape = (rows_here, cols_here, order, width)
    return out_u.reshape(shape), out_v.reshape(shape)


def solution(mesh):
    return jax.shard_map(
        functools.partial(on_device, mesh.shape["row"], mesh.shape["col"]),
        mesh=mesh,
        in_specs=(
            P("row", "col", None, None),
            P("row", "col", None, None),
            P("row", "col"),
            P("row", "col"),
            P("row", "col", None),
            P("row", "col", None),
            P("row"),
            P("col", "row", None),
            P("col", "row", None),
            P("col"),
            P(),
        ),
        out_specs=(P("row", "col", None, None), P("row", "col", None, None)),
        check_vma=False,
    )
```

time: 354 us -> 140 us (0.40)
  other arithmetic: 179 us -> 4.38 us
  matrix products: 71.1 us -> 0 us
  Pallas kernels: 0 us -> 49.6 us
  blocking collectives: 33.5 us -> 0 us
  waiting for transfers between devices: 22 us -> 55.3 us
  local copies, waits for them, and re-layouts: 32.8 us -> 10.9 us
  starting transfers between devices: 0.08 us -> 17.3 us
  between operations: 14.9 us -> 1.48 us
    another operation x7 -> x1, other arithmetic: 173 us -> 0.07 us  [on_device(): jnp.stack([lax.axis_index('row'), lax.axis_index('col')]).astype(jnp.int32)]
    dot_general x6 -> x0, matrix products: 60.8 us -> none  [the longest x1 19.3 us: recompress(): jnp.einsum('nbs,nbt->nst', span, span, precision=lax.Precision.HIGHEST)]
    ppermute x0 -> x17, waiting for transfers between devices: none -> 55.3 us  [swap(): return lax.ppermute(x, axis, [(c, c ^ mask) for c in range(size)])]
    pallas_call x0 -> x4, Pallas kernels: none -> 49.6 us  [the longest x1 35 us: on_device(): pl.pallas_call(functools.partial(final_kernel, last_mask=last, block=32),...]
    all_gather x2 -> x0, blocking collectives: 33.5 us -> none  [the longest x1 17.3 us: on_device(): lax.all_gather(col_u, 'row', axis=1, tiled=True)]
    all_gather x2 -> x0, waiting for transfers between devices: 20.6 us -> none  [the longest x1 20.6 us: on_device(): lax.all_gather(row_u, 'col', axis=1, tiled=True)]
    unnamed x26 -> x23, local copies, waits for them, and re-layouts: 29.9 us -> 9.44 us
    ppermute x0 -> x17, starting transfers between devices: none -> 17.3 us  [swap(): return lax.ppermute(x, axis, [(c, c ^ mask) for c in range(size)])]
  transfers between devices with their start and end apart: 2 -> 17, of which waited for: 1 -> 6; matrix products, arithmetic and copies ran while one was open for 6% -> 4% of each run, Pallas kernels for 0% -> 5%
where the time goes in v1:
time: 140 us; the launch traced here: 139 us
  waiting for transfers between devices  55.3 us (40%)
  Pallas kernels  49.6 us (35%)
  starting transfers between devices  17.3 us (12%)
  local copies, waits for them, and re-layouts  10.9 us (8%)
  other arithmetic  4.38 us (3%)
  between operations  1.48 us (1%)
    ppermute x17, waiting for transfers between devices, swap(): return lax.ppermute(x, axis, [(c, c ^ mask) for c in range(size)])  55.3 us
    pallas_call x1, Pallas kernels, on_device(): pl.pallas_call(functools.partial(final_kernel, last_mask=last, block=32),...  35 us
    ppermute x17, starting transfers between devices, swap(): return lax.ppermute(x, axis, [(c, c ^ mask) for c in range(size)])  17.3 us
    unnamed x23, local copies, waits for them, and re-layouts  9.44 us
    pallas_call x1, Pallas kernels, on_device(): pl.pallas_call(functools.partial(left_kernel, early), grid_spec=pltpu.Pre...  7.7 us
    pallas_call x1, Pallas kernels, on_device(): pl.pallas_call(local_kernel, grid_spec=pltpu.PrefetchScalarGridSpec(num_s...  4.08 us
    pallas_call x1, Pallas kernels, on_device(): pl.pallas_call(functools.partial(core_kernel, masks), in_specs=[SMEM] + [...  2.81 us
  transfers between devices with their start and end apart: 17, of which 6 were waited for; matrix products, arithmetic and copies ran while one was open for 4% of the time, Pallas kernels for 5%

profile of v1, /device:TPU:0, one launch (start us, length us, event | category | flops | bytes accessed | tf_op | source)
XLA Modules:
  0.0 139.0 jit_solution(3119665705497249990)
XLA Ops:
  0.6 1.0 maximum_bitcast_fusion
  1.6 3.1 %collective-permute-start.10 = (bf16[1,2,512,128]{3,2,1,0:T(8,128)(2,1)S(1)}, bf16[1,2,512,128]{3,2,1,0:T(8,128)(2,1)S(1)}, u32[]{:S(2)}, u32[]{:S(2)}) collective-permute-start(bf16[1,2,512,128]{3,2,1,0:T(8,128)(2,1)S(1)} %maximum_bitcast_fusion), channel_id=1, source_target_pairs={{0,8},{8,0},{16,24},{24,16},{1,9},{9,1},{17,25},{25,17},{2,10},{10... | collective-permute-start | bytes 786440 | tf_op jit(solution)/shard_map/ppermute | solution.py:294
  4.7 6.3 %collective-permute-done.10 = bf16[1,2,512,128]{3,2,1,0:T(8,128)(2,1)S(1)} collective-permute-done((bf16[1,2,512,128]{3,2,1,0:T(8,128)(2,1)S(1)}, bf16[1,2,512,128]{3,2,1,0:T(8,128)(2,1)S(1)}, u32[]{:S(2)}, u32[]{:S(2)}) %collective-permute-start.10) | collective-permute-done | bytes 262176 | tf_op jit(solution)/shard_map/ppermute | solution.py:294
  11.1 2.8 %collective-permute-start.11 = (bf16[2,2,512,128]{3,2,1,0:T(8,128)(2,1)S(1)}, bf16[2,2,512,128]{3,2,1,0:T(8,128)(2,1)S(1)}, u32[]{:S(2)}, u32[]{:S(2)}) collective-permute-start(bf16[2,2,512,128]{3,2,1,0:T(8,128)(2,1)S(1)} %pad_maximum_fusion.4), channel_id=1, source_target_pairs={{0,16},{8,24},{16,0},{24,8},{1,17},{9,25},{17,1},{25,9},{2,18},{10... | collective-permute-start | bytes 1572872 | tf_op jit(solution)/shard_map/ppermute | solution.py:294
  13.9 1.5 %collective-permute-start = (bf16[8,256,128]{2,1,0:T(8,128)(2,1)}, bf16[8,256,128]{2,1,0:T(8,128)(2,1)S(1)}, u32[]{:S(2)}, u32[]{:S(2)}) collective-permute-start(bf16[8,256,128]{2,1,0:T(8,128)(2,1)} %refs_0_.1), channel_id=1, source_target_pairs={{0,4},{1,5},{2,6},{3,7},{4,0},{5,1},{6,2},{7,3},{8,12},{9,13},{10,... | collective-permute-start | bytes 1572872 | tf_op jit(solution)/shard_map/ppermute | solution.py:294
  15.4 21.0 %collective-permute-done.11 = bf16[2,2,512,128]{3,2,1,0:T(8,128)(2,1)S(1)} collective-permute-done((bf16[2,2,512,128]{3,2,1,0:T(8,128)(2,1)S(1)}, bf16[2,2,512,128]{3,2,1,0:T(8,128)(2,1)S(1)}, u32[]{:S(2)}, u32[]{:S(2)}) %collective-permute-start.11) | collective-permute-done | bytes 524320 | tf_op jit(solution)/shard_map/ppermute | solution.py:294
  36.6 1.4 %collective-permute-start.3 = (bf16[8,256,128]{2,1,0:T(8,128)(2,1)}, bf16[8,256,128]{2,1,0:T(8,128)(2,1)S(1)}, u32[]{:S(2)}, u32[]{:S(2)}) collective-permute-start(bf16[8,256,128]{2,1,0:T(8,128)(2,1)} %refs_0_.2), channel_id=1, source_target_pairs={{0,4},{1,5},{2,6},{3,7},{4,0},{5,1},{6,2},{7,3},{8,12},{9,13},{10,... | collective-permute-start | bytes 1572872 | tf_op jit(solution)/shard_map/ppermute | solution.py:294
  38.0 1.5 %collective-permute-start.7 = (bf16[8,256,128]{2,1,0:T(8,128)(2,1)}, bf16[8,256,128]{2,1,0:T(8,128)(2,1)S(1)}, u32[]{:S(2)}, u32[]{:S(2)}) collective-permute-start(bf16[8,256,128]{2,1,0:T(8,128)(2,1)} %refs_0_.1), channel_id=1, source_target_pairs={{0,2},{1,3},{2,0},{3,1},{4,6},{5,7},{6,4},{7,5},{8,10},{9,11},{10,... | collective-permute-start | bytes 1572872 | tf_op jit(solution)/shard_map/ppermute | solution.py:294
  40.1 1.6 %collective-permute-start.9 = (bf16[4,256,128]{2,1,0:T(8,128)(2,1)S(1)}, bf16[4,256,128]{2,1,0:T(8,128)(2,1)}, u32[]{:S(2)}, u32[]{:S(2)}) collective-permute-start(bf16[4,256,128]{2,1,0:T(8,128)(2,1)S(1)} %slice.19), channel_id=1, source_target_pairs={{0,2},{1,3},{2,0},{3,1},{4,6},{5,7},{6,4},{7,5},{8,10},{9,11},{10,... | collective-permute-start | bytes 786440 | tf_op jit(solution)/shard_map/ppermute | solution.py:294
  41.6 9.5 %collective-permute-done.3.refs_4_ = bf16[8,256,128]{2,1,0:T(8,128)(2,1)S(1)} collective-permute-done((bf16[8,256,128]{2,1,0:T(8,128)(2,1)}, bf16[8,256,128]{2,1,0:T(8,128)(2,1)S(1)}, u32[]{:S(2)}, u32[]{:S(2)}) %collective-permute-start.3) | collective-permute-done | bytes 524320 | tf_op jit(solution)/shard_map/ppermute | solution.py:294
  51.1 0.7 slice.17
  51.9 1.3 collective-permute-start.4
  53.2 0.7 slice.18
  53.9 1.5 %collective-permute-start.8 = (bf16[4,256,128]{2,1,0:T(8,128)(2,1)}, bf16[4,256,128]{2,1,0:T(8,128)(2,1)}, u32[]{:S(2)}, u32[]{:S(2)}) collective-permute-start(bf16[4,256,128]{2,1,0:T(8,128)(2,1)} %slice.18), channel_id=1, source_target_pairs={{0,4},{1,5},{2,6},{3,7},{4,0},{5,1},{6,2},{7,3},{8,12},{9,13},{10,... | collective-permute-start | bytes 786440 | tf_op jit(solution)/shard_map/ppermute | solution.py:294
  55.4 8.8 %collective-permute-done.1.refs_2_ = bf16[8,256,128]{2,1,0:T(8,128)(2,1)S(1)} collective-permute-done((bf16[8,256,128]{2,1,0:T(8,128)(2,1)}, bf16[8,256,128]{2,1,0:T(8,128)(2,1)S(1)}, u32[]{:S(2)}, u32[]{:S(2)}) %collective-permute-start.1) | collective-permute-done | bytes 524320 | tf_op jit(solution)/shard_map/ppermute | solution.py:294
  64.3 0.7 collective-permute-start.2
  65.1 4.9 %collective-permute-done.9 = bf16[4,256,128]{2,1,0:T(8,128)(2,1)} collective-permute-done((bf16[4,256,128]{2,1,0:T(8,128)(2,1)S(1)}, bf16[4,256,128]{2,1,0:T(8,128)(2,1)}, u32[]{:S(2)}, u32[]{:S(2)}) %collective-permute-start.9) | collective-permute-done | bytes 262176 | tf_op jit(solution)/shard_map/ppermute | solution.py:294
  70.0 4.8 %collective-permute-done.4 = bf16[4,256,128]{2,1,0:T(8,128)(2,1)} collective-permute-done((bf16[4,256,128]{2,1,0:T(8,128)(2,1)}, bf16[4,256,128]{2,1,0:T(8,128)(2,1)}, u32[]{:S(2)}, u32[]{:S(2)}) %collective-permute-start.4) | collective-permute-done | bytes 262176 | tf_op jit(solution)/shard_map/ppermute | solution.py:294
  74.8 1.1 pad_maximum_fusion.3.refs_3_
  75.9 0.6 collective-permute-start.16
  76.6 1.0 copy-done.4
  77.6 2.8 %core_products.1 = (f32[8,128,128]{2,1,0:T(8,128)S(1)}, f32[8,128,128]{2,1,0:T(8,128)}) custom-call(s32[2]{0:T(128)S(1)} %pad_add_fusion.pos_ref, bf16[8,256,128]{2,1,0:T(8,128)(2,1)S(1)} %copy-done.4, bf16[8,256,128]{2,1,0:T(8,128)(2,1)S(1)} %collective-permute-done.7.refs_1_, bf16[8,256,128]{2,1,0:T(8,128)(2,1)S(1)} %collective-permute-done.refs_2_, ...), custom_call_target="tpu_custom_call" | custom-call | flops 536870912 | bytes 2097152 | tf_op jit(solution)/shard_map/core_products/pallas_call | solution.py:394
  80.4 0.8 copy-done.6
  82.4 1.2 copy.13
  83.6 2.2 %copy-done = bf16[8,1,2048,128]{3,2,1,0:T(8,128)(2,1)S(1)} copy-done((bf16[8,1,2048,128]{3,2,1,0:T(8,128)(2,1)S(1)}, bf16[8,1,2048,128]{3,2,1,0:T(8,128)(2,1)}, u32[]{:S(2)}) %copy-start) | copy-done | bytes 4194328
  85.8 2.2 %copy-done.2 = bf16[8,1,2048,128]{3,2,1,0:T(8,128)(2,1)S(1)} copy-done((bf16[8,1,2048,128]{3,2,1,0:T(8,128)(2,1)S(1)}, bf16[8,1,2048,128]{3,2,1,0:T(8,128)(2,1)}, u32[]{:S(2)}) %copy-start.2) | copy-done | bytes 4194328
  88.0 4.1 %local_products.1 = (bf16[8,128,128]{2,1,0:T(8,128)(2,1)S(1)}, f32[8,128,128]{2,1,0:T(8,128)S(1)}) custom-call(s32[8]{0:T(128)S(1)} %bitcast.22, bf16[8,2048,128]{2,1,0:T(8,128)(2,1)S(1)} %bitcast.16, bf16[8,2048,128]{2,1,0:T(8,128)(2,1)S(1)} %bitcast.19, bf16[128,2048]{1,0:T(8,128)(2,1)S(1)} %bitcast.20), custom_call_target="tpu_custom_call" | custom-call | flops 1073741824 | bytes 8388608 | tf_op jit(solution)/shard_map/local_products/pallas_call | solution.py:358
  92.1 1.1 pad_maximum_fusion.1.first_ref
  93.2 1.0 pad_maximum_fusion.2.second_ref
  94.3 7.7 %left_products.1 = (bf16[8,2048,128]{2,1,0:T(8,128)(2,1)S(1)}, f32[8,128,256]{2,1,0:T(8,128)S(1)}, bf16[8,128,128]{2,1,0:T(8,128)(2,1)S(1)}, bf16[128,128]{1,0:T(8,128)(2,1)S(1)}) custom-call(s32[2]{0:T(128)S(1)} %pad_add_fusion.pos_ref, s32[8]{0:T(128)S(1)} %copy-done.10, s32[1]{0:T(128)S(6)} %copy.16.col_rank_ref, f32[8,128,128]{2,1,0:T(8,128)S(1)} %copy-done.7, ...), custom_call_target="tpu_custom_call" | custom-call | flops 1610612736 | bytes 12582912 | tf_op jit(solution)/shard_map/left_products/pallas_call | solution.py:417
  102.0 2.0 %copy-done.3 = bf16[8,2048,128]{2,1,0:T(8,128)(2,1)} copy-done((bf16[8,2048,128]{2,1,0:T(8,128)(2,1)}, bf16[8,2048,128]{2,1,0:T(8,128)(2,1)S(1)}, u32[]{:S(2)}) %copy-start.3) | copy-done | bytes 4194328
  104.0 35.0 %recompress_store.1 = (bf16[8,2048,128]{2,1,0:T(8,128)(2,1)}, bf16[8,2048,128]{2,1,0:T(8,128)(2,1)}) custom-call(s32[2]{0:T(128)S(1)} %pad_add_fusion.pos_ref, s32[8]{0:T(128)S(1)} %bitcast.23, s32[8]{0:T(128)S(1)} %bitcast.24, s32[1]{0:T(128)S(6)} %copy.16.col_rank_ref, bf16[8,256,128]{2,1,0:T(8,128)(2,1)S(1)} %pad_maximum_fusion.1.first_ref, ...), custom_call_target="tpu_custom_call" | custom-call | flops 4294967296 | bytes 20971520 | tf_op jit(solution)/shard_map/recompress_store/pallas_call | solution.py:459
  (40 shorter events, 1.5 us)
Async XLA Ops:
  1.6 9.4 %collective-permute-start.10 = (bf16[1,2,512,128]{3,2,1,0:T(8,128)(2,1)S(1)}, bf16[1,2,512,128]{3,2,1,0:T(8,128)(2,1)S(1)}, u32[]{:S(2)}, u32[]{:S(2)}) collective-permute-start(bf16[1,2,512,128]{3,2,1,0:T(8,128)(2,1)S(1)} %maximum_bitcast_fusion), channel_id=1, source_target_pairs={{0,8},{8,0},{16,24},{24,16},{1,9},{9,1},{17,25},{25,17},{2,10},{10... | collective-permute-start | bytes 786440 | tf_op jit(solution)/shard_map/ppermute | solution.py:294
  11.1 25.3 %collective-permute-start.11 = (bf16[2,2,512,128]{3,2,1,0:T(8,128)(2,1)S(1)}, bf16[2,2,512,128]{3,2,1,0:T(8,128)(2,1)S(1)}, u32[]{:S(2)}, u32[]{:S(2)}) collective-permute-start(bf16[2,2,512,128]{3,2,1,0:T(8,128)(2,1)S(1)} %pad_maximum_fusion.4), channel_id=1, source_target_pairs={{0,16},{8,24},{16,0},{24,8},{1,17},{9,25},{17,1},{25,9},{2,18},{10... | collective-permute-start | bytes 1572872 | tf_op jit(solution)/shard_map/ppermute | solution.py:294
  13.9 22.7 %collective-permute-start = (bf16[8,256,128]{2,1,0:T(8,128)(2,1)}, bf16[8,256,128]{2,1,0:T(8,128)(2,1)S(1)}, u32[]{:S(2)}, u32[]{:S(2)}) collective-permute-start(bf16[8,256,128]{2,1,0:T(8,128)(2,1)} %refs_0_.1), channel_id=1, source_target_pairs={{0,4},{1,5},{2,6},{3,7},{4,0},{5,1},{6,2},{7,3},{8,12},{9,13},{10,... | collective-permute-start | bytes 1572872 | tf_op jit(solution)/shard_map/ppermute | solution.py:294
  36.5 47.1 %copy-start.8 = (s32[8,1]{0,1:T(1,128)S(1)}, s32[8,1]{0,1:T(1,128)}, u32[]{:S(2)}) copy-start(s32[8,1]{0,1:T(1,128)} %param.13) | copy-start | bytes 100
  36.5 40.0 %collective-permute-start.12 = (bf16[4,2,512,128]{3,2,1,0:T(8,128)(2,1)S(1)}, bf16[4,2,512,128]{3,2,1,0:T(8,128)(2,1)}, u32[]{:S(2)}, u32[]{:S(2)}) collective-permute-start(bf16[4,2,512,128]{3,2,1,0:T(8,128)(2,1)S(1)} %pad_maximum_fusion.refs_4_.x_ref.x_hbm), channel_id=1, source_target_pairs={{0,1},{1,0},{2,3},{3,2},{4,5},{5,4},{6,7},{7,6},{8,9},{9,8},{10,11... | collective-permute-start | bytes 3145736 | tf_op jit(solution)/shard_map/ppermute | solution.py:294
  36.6 14.5 %collective-permute-start.3 = (bf16[8,256,128]{2,1,0:T(8,128)(2,1)}, bf16[8,256,128]{2,1,0:T(8,128)(2,1)S(1)}, u32[]{:S(2)}, u32[]{:S(2)}) collective-permute-start(bf16[8,256,128]{2,1,0:T(8,128)(2,1)} %refs_0_.2), channel_id=1, source_target_pairs={{0,4},{1,5},{2,6},{3,7},{4,0},{5,1},{6,2},{7,3},{8,12},{9,13},{10,... | collective-permute-start | bytes 1572872 | tf_op jit(solution)/shard_map/ppermute | solution.py:294
  38.0 15.2 %collective-permute-start.7 = (bf16[8,256,128]{2,1,0:T(8,128)(2,1)}, bf16[8,256,128]{2,1,0:T(8,128)(2,1)S(1)}, u32[]{:S(2)}, u32[]{:S(2)}) collective-permute-start(bf16[8,256,128]{2,1,0:T(8,128)(2,1)} %refs_0_.1), channel_id=1, source_target_pairs={{0,2},{1,3},{2,0},{3,1},{4,6},{5,7},{6,4},{7,5},{8,10},{9,11},{10,... | collective-permute-start | bytes 1572872 | tf_op jit(solution)/shard_map/ppermute | solution.py:294
  39.5 24.7 %collective-permute-start.1 = (bf16[8,256,128]{2,1,0:T(8,128)(2,1)}, bf16[8,256,128]{2,1,0:T(8,128)(2,1)S(1)}, u32[]{:S(2)}, u32[]{:S(2)}) collective-permute-start(bf16[8,256,128]{2,1,0:T(8,128)(2,1)} %refs_0_.2), channel_id=1, source_target_pairs={{0,2},{1,3},{2,0},{3,1},{4,6},{5,7},{6,4},{7,5},{8,10},{9,11},{10,... | collective-permute-start | bytes 1572872 | tf_op jit(solution)/shard_map/ppermute | solution.py:294
  40.1 29.9 %collective-permute-start.9 = (bf16[4,256,128]{2,1,0:T(8,128)(2,1)S(1)}, bf16[4,256,128]{2,1,0:T(8,128)(2,1)}, u32[]{:S(2)}, u32[]{:S(2)}) collective-permute-start(bf16[4,256,128]{2,1,0:T(8,128)(2,1)S(1)} %slice.19), channel_id=1, source_target_pairs={{0,2},{1,3},{2,0},{3,1},{4,6},{5,7},{6,4},{7,5},{8,10},{9,11},{10,... | collective-permute-start | bytes 786440 | tf_op jit(solution)/shard_map/ppermute | solution.py:294
  51.9 22.9 %collective-permute-start.4 = (bf16[4,256,128]{2,1,0:T(8,128)(2,1)}, bf16[4,256,128]{2,1,0:T(8,128)(2,1)}, u32[]{:S(2)}, u32[]{:S(2)}) collective-permute-start(bf16[4,256,128]{2,1,0:T(8,128)(2,1)} %slice.17), channel_id=1, source_target_pairs={{0,2},{1,3},{2,0},{3,1},{4,6},{5,7},{6,4},{7,5},{8,10},{9,11},{10,... | collective-permute-start | bytes 786440 | tf_op jit(solution)/shard_map/ppermute | solution.py:294
  53.9 20.9 %collective-permute-start.8 = (bf16[4,256,128]{2,1,0:T(8,128)(2,1)}, bf16[4,256,128]{2,1,0:T(8,128)(2,1)}, u32[]{:S(2)}, u32[]{:S(2)}) collective-permute-start(bf16[4,256,128]{2,1,0:T(8,128)(2,1)} %slice.18), channel_id=1, source_target_pairs={{0,4},{1,5},{2,6},{3,7},{4,0},{5,1},{6,2},{7,3},{8,12},{9,13},{10,... | collective-permute-start | bytes 786440 | tf_op jit(solution)/shard_map/ppermute | solution.py:294
  64.3 16.9 %collective-permute-start.2 = (bf16[4,256,128]{2,1,0:T(8,128)(2,1)S(1)}, bf16[4,256,128]{2,1,0:T(8,128)(2,1)}, u32[]{:S(2)}, u32[]{:S(2)}) collective-permute-start(bf16[4,256,128]{2,1,0:T(8,128)(2,1)S(1)} %slice.16), channel_id=1, source_target_pairs={{0,4},{1,5},{2,6},{3,7},{4,0},{5,1},{6,2},{7,3},{8,12},{9,13},{10,... | collective-permute-start | bytes 786440 | tf_op jit(solution)/shard_map/ppermute | solution.py:294
  70.0 24.2 %collective-permute-start.14 = (bf16[8,256,128]{2,1,0:T(8,128)(2,1)}, bf16[8,256,128]{2,1,0:T(8,128)(2,1)}, u32[]{:S(2)}, u32[]{:S(2)}) collective-permute-start(bf16[8,256,128]{2,1,0:T(8,128)(2,1)} %refs_0_.2), channel_id=1, source_target_pairs={{0,1},{1,0},{2,3},{3,2},{4,5},{5,4},{6,7},{7,6},{8,9},{9,8},{10,11... | collective-permute-start | bytes 1572872 | tf_op jit(solution)/shard_map/ppermute | solution.py:294
  74.8 6.8 %collective-permute-start.6 = (bf16[4,256,128]{2,1,0:T(8,128)(2,1)}, bf16[4,256,128]{2,1,0:T(8,128)(2,1)S(1)}, u32[]{:S(2)}, u32[]{:S(2)}) collective-permute-start(bf16[4,256,128]{2,1,0:T(8,128)(2,1)} %collective-permute-done.4), channel_id=1, source_target_pairs={{0,1},{1,0},{2,3},{3,2},{4,5},{5,4},{6,7},{7,6},{8,9},{9,8},{10,11... | collective-permute-start | bytes 786440 | tf_op jit(solution)/shard_map/ppermute | solution.py:294
  75.9 18.3 %collective-permute-start.16 = (bf16[8,256,128]{2,1,0:T(8,128)(2,1)S(1)}, bf16[8,256,128]{2,1,0:T(8,128)(2,1)}, u32[]{:S(2)}, u32[]{:S(2)}) collective-permute-start(bf16[8,256,128]{2,1,0:T(8,128)(2,1)S(1)} %collective-permute-done.3.refs_4_), channel_id=1, source_target_pairs={{0,1},{1,0},{2,3},{3,2},{4,5},{5,4},{6,7},{7,6},{8,9},{9,8},{10,11... | collective-permute-start | bytes 1572872 | tf_op jit(solution)/shard_map/ppermute | solution.py:294
  76.5 17.8 %collective-permute-start.15 = (bf16[8,256,128]{2,1,0:T(8,128)(2,1)S(1)}, bf16[8,256,128]{2,1,0:T(8,128)(2,1)}, u32[]{:S(2)}, u32[]{:S(2)}) collective-permute-start(bf16[8,256,128]{2,1,0:T(8,128)(2,1)S(1)} %collective-permute-done.1.refs_2_), channel_id=1, source_target_pairs={{0,1},{1,0},{2,3},{3,2},{4,5},{5,4},{6,7},{7,6},{8,9},{9,8},{10,11... | collective-permute-start | bytes 1572872 | tf_op jit(solution)/shard_map/ppermute | solution.py:294
  76.5 1.0 copy-start.4
  80.4 0.8 copy-start.6
  81.2 13.0 %collective-permute-start.13 = (f32[8,128,128]{2,1,0:T(8,128)}, f32[8,128,128]{2,1,0:T(8,128)S(1)}, u32[]{:S(2)}, u32[]{:S(2)}) collective-permute-start(f32[8,128,128]{2,1,0:T(8,128)} %get-tuple-element.15), channel_id=1, source_target_pairs={{0,1},{1,0},{2,3},{3,2},{4,5},{5,4},{6,7},{7,6},{8,9},{9,8},{10,11... | collective-permute-start | bytes 1572872 | tf_op jit(solution)/shard_map/ppermute | solution.py:294
  81.6 11.6 %collective-permute-start.5 = (bf16[4,256,128]{2,1,0:T(8,128)(2,1)}, bf16[4,256,128]{2,1,0:T(8,128)(2,1)}, u32[]{:S(2)}, u32[]{:S(2)}) collective-permute-start(bf16[4,256,128]{2,1,0:T(8,128)(2,1)} %collective-permute-done.2), channel_id=1, source_target_pairs={{0,1},{1,0},{2,3},{3,2},{4,5},{5,4},{6,7},{7,6},{8,9},{9,8},{10,11... | collective-permute-start | bytes 786440 | tf_op jit(solution)/shard_map/ppermute | solution.py:294
  83.6 2.2 %copy-start = (bf16[8,1,2048,128]{3,2,1,0:T(8,128)(2,1)S(1)}, bf16[8,1,2048,128]{3,2,1,0:T(8,128)(2,1)}, u32[]{:S(2)}) copy-start(bf16[8,1,2048,128]{3,2,1,0:T(8,128)(2,1)} %param.11) | copy-start | bytes 12582916
  85.8 2.2 %copy-start.2 = (bf16[8,1,2048,128]{3,2,1,0:T(8,128)(2,1)S(1)}, bf16[8,1,2048,128]{3,2,1,0:T(8,128)(2,1)}, u32[]{:S(2)}) copy-start(bf16[8,1,2048,128]{3,2,1,0:T(8,128)(2,1)} %param.12) | copy-start | bytes 12582916
  88.0 6.2 %copy-start.1 = (bf16[8,1,2048,128]{3,2,1,0:T(8,128)(2,1)S(1)}, bf16[8,1,2048,128]{3,2,1,0:T(8,128)(2,1)}, u32[]{:S(2)}) copy-start(bf16[8,1,2048,128]{3,2,1,0:T(8,128)(2,1)} %param.11) | copy-start | bytes 12582916
  88.0 6.2 %copy-start.5 = (bf16[8,256,128]{2,1,0:T(8,128)(2,1)S(1)}, bf16[8,256,128]{2,1,0:T(8,128)(2,1)}, u32[]{:S(2)}) copy-start(bf16[8,256,128]{2,1,0:T(8,128)(2,1)} %refs_0_.2) | copy-start | bytes 1572868
  88.0 6.2 %copy-start.7 = (f32[8,128,128]{2,1,0:T(8,128)S(1)}, f32[8,128,128]{2,1,0:T(8,128)}, u32[]{:S(2)}) copy-start(f32[8,128,128]{2,1,0:T(8,128)} %copy-done.6) | copy-start | bytes 1572868
  88.0 6.3 %copy-start.10 = (s32[8]{0:T(128)S(1)}, s32[8]{0:T(128)}, u32[]{:S(2)}) copy-start(s32[8]{0:T(128)} %row_rank_ref.1) | copy-start | bytes 100
  94.3 9.7 %copy-start.9 = (s32[8,1]{0,1:T(1,128)S(1)}, s32[8,1]{0,1:T(1,128)}, u32[]{:S(2)}) copy-start(s32[8,1]{0,1:T(1,128)} %param.14) | copy-start | bytes 100
  102.0 2.0 %copy-start.3 = (bf16[8,2048,128]{2,1,0:T(8,128)(2,1)}, bf16[8,2048,128]{2,1,0:T(8,128)(2,1)S(1)}, u32[]{:S(2)}) copy-start(bf16[8,2048,128]{2,1,0:T(8,128)(2,1)S(1)} %get-tuple-element.16.left_hbm) | copy-start | bytes 12582916

commit v2 on v0

v2 whole, which is shorter than its diff:
```python
import functools

import jax
import jax.numpy as jnp
from jax import lax
from jax.experimental import pallas as pl
from jax.experimental.pallas import tpu as pltpu
from jax.sharding import PartitionSpec as P

F32 = jnp.float32
BF16 = jnp.bfloat16
HBM = pl.BlockSpec(memory_space=pltpu.HBM)
SMEM = pl.BlockSpec(memory_space=pltpu.SMEM)
VMEM = pl.BlockSpec(memory_space=pltpu.VMEM)
MIB = 2**20


def dot(a, b, ca=1, cb=0):
    return lax.dot_general(a, b, (((ca,), (cb,)), ((), ())), preferred_element_type=F32)


def halves(x):
    high = x.astype(BF16)
    return high, (x - high.astype(F32)).astype(BF16)


def lanes(shape):
    return lax.broadcasted_iota(jnp.int32, shape, len(shape) - 1)


def rows_of(shape):
    return lax.broadcasted_iota(jnp.int32, shape, len(shape) - 2)


def local_kernel(rank_ref, st_ref, u_ref, v_ref, proj_ref, uu_ref):
    for t in range(u_ref.shape[0]):
        proj = dot(st_ref[...], v_ref[t])
        keep = lanes(proj.shape) < rank_ref[t]
        proj_ref[t] = jnp.where(keep, proj, 0.0).astype(BF16)
        u = u_ref[t]
        uu_ref[t] = dot(u, u, 0, 0)


def core_kernel(pos_ref, *refs, masks, pieces, more):
    q_refs, refs = refs[: len(masks)], refs[len(masks) :]
    mine_refs, refs = refs[:pieces], refs[pieces:]
    other_ref, refs = refs[0], refs[1:]
    before, (own_out, other_out) = refs[:-2], refs[-2:]
    count, chunk, width = q_refs[0].shape
    depth = other_ref.shape[1]
    sides = []
    for mask in masks:
        start = jnp.bitwise_xor(pos_ref[1], mask) * chunk
        piece = lax.rem(pos_ref[0] + pieces - start // depth, pieces)
        inner = pl.multiple_of(start % depth, chunk)
        mine = mine_refs[0][0, pl.ds(inner, chunk), :]
        for k in range(1, pieces):
            mine = jnp.where(piece == k, mine_refs[k][0, pl.ds(inner, chunk), :], mine)
        both = [mine, other_ref[piece, pl.ds(inner, chunk), :]]
        sides.append(jnp.concatenate(both, axis=1).astype(F32).T.astype(BF16))
    for t in range(0, count, 2):
        total = None
        for q_ref, side in zip(q_refs, sides):
            pair = jnp.concatenate([q_ref[t], q_ref[t + 1]], axis=1)
            part = dot(side, pair)
            total = part if total is None else total + part
        for k in range(2):
            block = total[:, k * width : (k + 1) * width]
            own, other = block[:width], block[width:]
            if more:
                own, other = own + before[0][t + k], other + before[1][t + k]
            own_out[t + k] = own
            other_out[t + k] = other


def final_kernel(
    pos_ref,
    rank_ref,
    listed_ref,
    row_rank_ref,
    col_rank_ref,
    u_hbm,
    v_hbm,
    uu_ref,
    own_ref,
    other_ref,
    vproj_ref,
    st_ref,
    *refs,
    masks,
    block,
    pieces,
):
    x_refs, refs = refs[:pieces], refs[pieces:]
    panel_refs, refs = refs[: 2 * len(masks)], refs[2 * len(masks) :]
    (
        out_u,
        out_v,
        u_buf,
        v_buf,
        left_buf,
        x_buf,
        to_u,
        to_v,
        gs,
        rs,
        ts,
        scales,
        to_mix,
        to_coef,
        sem_u,
        sem_v,
        sem_out,
    ) = refs
    count, order, width = u_hbm.shape
    chunk = panel_refs[0].shape[1]
    depth = x_refs[0].shape[1]
    def rows_at(k):
        start = jnp.bitwise_xor(pos_ref[1], masks[k // 2] + k % 2) * chunk
        return pl.ds(pl.multiple_of(start, chunk), chunk)

    spans = [pl.ds(k * chunk, chunk) for k in range(len(panel_refs))]
    loads = [
        pltpu.make_async_copy(u_hbm.at[:, rows_at(k), :], u_buf.at[:, span, :], sem_u.at[k])
        for k, span in enumerate(spans)
    ]
    for copy in loads:
        copy.start()
    load_v = pltpu.make_async_copy(v_hbm, v_buf, sem_v)
    load_v.start()
    for k in range(pieces):
        start = lax.rem(pos_ref[0] + pieces - k, pieces) * depth
        rows = pl.ds(pl.multiple_of(start, depth), depth)
        x_buf[rows, :] = x_refs[k][0]

    def send_u(t, k):
        src = to_u.at[t, spans[k], :]
        return pltpu.make_async_copy(src, out_u.at[t, rows_at(k), :], sem_out.at[0])

    def send_v(t):
        return pltpu.make_async_copy(to_v.at[t], out_v.at[t], sem_out.at[1])

    square = (width, width)
    eye = rows_of(square) == lanes(square)
    xproj = dot(st_ref[...], x_buf[...])
    xproj = jnp.where(lanes(square) < col_rank_ref[0], -xproj, 0.0).astype(BF16)

    for t in range(count):
        core = own_ref[t] + other_ref[t]
        keep = (lanes(square) < row_rank_ref[t]) & (rows_of(square) < col_rank_ref[0])
        core = jnp.where(keep, core, 0.0).astype(BF16)
        panel = jnp.concatenate([ref[t] for ref in panel_refs], axis=0)
        left_buf[t] = dot(panel, core, 1, 1).astype(BF16)
    for copy in loads:
        copy.wait()

    def assemble(t):
        left = left_buf[t]
        low = dot(left, jnp.concatenate([u_buf[t], left], axis=1), 0, 0)
        lu_h, lu_l = halves(low[:, :width])
        ll_h, ll_l = halves(low[:, width:])
        uu_h, uu_l = halves(uu_ref[t])
        a, b = vproj_ref[t], xproj
        left_part = dot(a, uu_h) + dot(a, uu_l) + dot(b, lu_h) + dot(b, lu_l)
        right_part = dot(a, lu_h, 1, 1) + dot(a, lu_l, 1, 1) + dot(b, ll_h) + dot(b, ll_l)
        moved = jnp.concatenate([left_part, right_part], axis=1)
        ts[t] = moved
        moved_h, moved_l = halves(moved)
        weights = jnp.concatenate([a, b], axis=1)
        gram = dot(moved_h, weights, 1, 1) + dot(moved_l, weights, 1, 1)
        diag = jnp.where(eye, gram, 0.0)
        trace = jnp.sum(jnp.sum(diag, axis=1, keepdims=True), axis=0, keepdims=True)
        scale = trace / width + 0.0001
        inverse = 1.0 / scale
        gs[pl.ds(t * width, width), :] = gram * inverse + jnp.where(
            eye, 0.01, 0.0
        )
        scales[t] = jnp.broadcast_to(lax.rsqrt(scale), scales.shape[1:])

    for t in range(count):
        assemble(t)

    lane = lanes((count, width))
    small = 8
    for k0 in range(0, width, block):
        end = k0 + block
        taken = jnp.stack([gs[pl.ds(n * width + k0, block), :] for n in range(count)])
        taken = jnp.swapaxes(taken, 0, 1)
        rows = [taken[r] for r in range(block)]
        ready = []
        for b0 in range(0, block, small):
            first = k0 + b0
            inside = (lane >= first) & (lane < first + small)
            part = rows[b0 : b0 + small]
            a = [
                [part[i][:, first + j : first + j + 1] for j in range(i + 1)]
                for i in range(small)
            ]
            a = [[jnp.broadcast_to(x, (count, width)) for x in line] for line in a]
            part = [
                jnp.where(inside, jnp.where(lane == first + i, 1.0, 0.0), x)
                for i, x in enumerate(part)
            ]
            for j in range(small):
                root = lax.rsqrt(a[j][j])
                part[j] = part[j] * root
                factors = {i: a[i][j] * root for i in range(j + 1, small)}
                for i in range(j + 1, small):
                    for m in range(j + 1, i + 1):
                        a[i][m] = a[i][m] - factors[i] * factors[m]
                    part[i] = part[i] - factors[i] * part[j]
            for r in range(b0 + small, block):
                row = jnp.where(inside, 0.0, rows[r])
                for j in range(small):
                    row = row - part[j][:, k0 + r : k0 + r + 1] * part[j]
                rows[r] = row
            ready += part
        ready = jnp.swapaxes(jnp.stack(ready), 0, 1)
        for n in range(count):
            rs[pl.ds(n * width + k0, block), :] = ready[n]
        if end < width:
            strip = (block, width)
            strip_lane = lanes(strip)
            own = k0 + rows_of(strip)
            group = min(count, width // block)
            for g in range(0, count, group):
                ahead, use = [], []
                for n in range(g, g + group):
                    done = ready[n]
                    ahead.append(jnp.where(strip_lane >= end, done, 0.0))
                    use.append(
                        jnp.where((strip_lane > own) & (strip_lane < end), 0.0, done)
                    )
                turned = jnp.concatenate(ahead, axis=0).T[end:]
                a_h, a_l = halves(turned)
                both = jnp.concatenate([a_h, a_l], axis=1)
                for n in range(0, group, 2):
                    cells = []
                    for m in (n, n + 1):
                        spread = [jnp.zeros(strip, F32)] * group
                        spread[m] = use[m]
                        cells.append(jnp.concatenate(spread, axis=0))
                    b_h, b_l = halves(jnp.concatenate(cells, axis=1))
                    change = dot(both, jnp.concatenate([b_h, b_h], axis=0)) + dot(a_h, b_l)
                    for m in (n, n + 1):
                        rest = pl.ds((g + m) * width + end, width - end)
                        old = gs[rest, :]
                        gone = lanes(old.shape)
                        old = jnp.where((gone >= k0) & (gone < end), 0.0, old)
                        gs[rest, :] = old - change[:, (m - n) * width : (m - n + 1) * width]

    def weigh(t):
        tile_rank = rank_ref[t]
        picked = listed_ref[t] == 1
        inverse = rs[pl.ds(t * width, width), :]
        inverse = jnp.where(lanes(square) <= rows_of(square), inverse, 0.0)
        inverse = inverse * (scales[t][:1, :1] * (float(order) ** 0.5))
        inv_h, inv_l = halves(inverse)
        weights = jnp.concatenate([vproj_ref[t], xproj], axis=1)
        mixed = dot(inv_h, weights) + dot(inv_l, weights)
        mixed_h, mixed_l = halves(mixed)
        moved_h, moved_l = halves(ts[t])
        coef = dot(inv_h, moved_h) + dot(inv_h, moved_l) + dot(inv_l, moved_h)
        coef = coef * (1.0 / order)
        wide = coef.shape
        col = lanes(wide)
        row = rows_of(wide)
        in_u = col < width
        keep = (col == row) & (col < tile_rank)
        moved_to = (col >= width) & (row == col - width + tile_rank)
        exact_u = jnp.where(keep | moved_to, 1.0, 0.0)
        moved_to = moved_to & (col - width < col_rank_ref[0])
        exact_v = jnp.where(keep, 1.0, jnp.where(moved_to, -1.0, 0.0))
        coef = jnp.where(in_u, jnp.where(col < tile_rank, coef, 0.0), -coef)
        coef = jnp.where(picked, coef, exact_v).astype(BF16)
        mixed_h = jnp.where(picked, mixed_h.astype(F32), exact_u).astype(BF16)
        mixed_l = jnp.where(picked, mixed_l.astype(F32), 0.0).astype(BF16)
        both = jnp.concatenate([mixed_h, mixed_l], axis=0)
        to_mix[t] = both
        to_coef[t] = coef

    for t in range(count):
        weigh(t)
    load_v.wait()

    def finish(t, carry):
        side = jnp.concatenate([u_buf[t], left_buf[t]], axis=1)
        result = dot(side, to_mix[t], 1, 1)
        to_u[t] = (result[:, :width] + result[:, width:]).astype(BF16)
        for k in range(len(spans)):
            send_u(t, k).start()
        side = jnp.concatenate([v_buf[t], x_buf[...]], axis=1)
        to_v[t] = dot(side, to_coef[t], 1, 1).astype(BF16)
        send_v(t).start()
        return carry

    lax.fori_loop(0, count, finish, 0)
    pltpu.make_async_copy(to_u, out_u, sem_out.at[0]).wait()
    pltpu.make_async_copy(to_v, out_v, sem_out.at[1]).wait()


def swap(x, axis, size, mask):
    return lax.ppermute(x, axis, [(c, c ^ mask) for c in range(size)])


def on_device(
    n_row,
    n_col,
    tile_u,
    tile_v,
    tile_rank,
    listed,
    row_u,
    row_v,
    row_rank,
    col_u,
    col_v,
    col_rank,
    sketch,
):
    rows_here, cols_here, order, width = tile_u.shape
    assert cols_here == 1 and width == sketch.shape[1]
    count = rows_here * cols_here
    chunk = row_u.shape[1]
    tile_u = tile_u.reshape(count, order, width)
    tile_v = tile_v.reshape(count, order, width)
    tile_rank = tile_rank.reshape(count)
    listed = listed.reshape(count)
    pos = jnp.stack([lax.axis_index("row"), lax.axis_index("col")]).astype(jnp.int32)
    col_swap = lambda x, mask: swap(x, "col", n_col, mask)
    dims = []
    mask = 2
    while mask < n_col:
        dims.append(mask)
        mask *= 2

    tie = lax.optimization_barrier

    def gather(own, order, found):
        for m in order:
            for r in sorted(found):
                if not r & m and r | m not in found:
                    found[r | m] = col_swap(found[r], m)
        return found

    ring = [(c, (c + 1) % n_row) for c in range(n_row)]
    q = {0: row_v, **{m: col_swap(row_v, m) for m in dims}}
    p = {0: row_u, **{m: col_swap(row_u, m) for m in dims}}
    y = [col_v]
    for _ in range(n_row - 2):
        y.append(lax.ppermute(y[-1], "row", ring))
    turned = sketch.T

    vproj, uu = pl.pallas_call(
        local_kernel,
        in_specs=[SMEM, VMEM, VMEM, VMEM],
        out_specs=[VMEM, VMEM],
        out_shape=[
            jax.ShapeDtypeStruct((count, width, width), BF16),
            jax.ShapeDtypeStruct((count, width, width), F32),
        ],
        compiler_params=pltpu.CompilerParams(vmem_limit_bytes=16 * MIB),
        cost_estimate=pl.CostEstimate(
            flops=4 * count * order * width * width,
            bytes_accessed=4 * count * order * width,
            transcendentals=0,
        ),
        name="local_products",
    )(tile_rank, turned, tile_u, tile_v)

    passed, vproj, x_own, q[dims[0]], p[dims[-1]] = tie(
        (y[-1], vproj, col_u, q[dims[0]], p[dims[-1]])
    )
    y.append(lax.ppermute(passed, "row", ring))
    x = [x_own, lax.ppermute(x_own, "row", ring)]
    q, p, vproj, uu, x = tie((q, p, vproj, uu, x))
    for _ in range(n_row - 2):
        x.append(lax.ppermute(x[-1], "row", ring))
    q = gather(row_v, dims, q)
    p = gather(row_u, dims[::-1], p)
    y_other = col_swap(jnp.concatenate(y, axis=0), 1)
    own_mate = col_swap(row_u, 1)
    masks = tuple(range(0, n_col, 2))
    part_shape = jax.ShapeDtypeStruct((count, width, width), F32)

    def cores(use, before):
        return pl.pallas_call(
            functools.partial(core_kernel, masks=use, pieces=n_row, more=len(before) > 0),
            in_specs=[SMEM] + [VMEM] * (len(use) + n_row + 1 + len(before)),
            out_specs=[VMEM, VMEM],
            out_shape=[part_shape, part_shape],
            compiler_params=pltpu.CompilerParams(vmem_limit_bytes=16 * MIB),
            cost_estimate=pl.CostEstimate(
                flops=4 * len(use) * count * chunk * width * width,
                bytes_accessed=2 * len(use) * count * chunk * width,
                transcendentals=0,
            ),
            name="core_products",
        )(pos, *[q[m] for m in use], *y, y_other, *before)

    parts = cores(masks[:-1], []) if len(masks) > 1 else []
    parts, x = tie((parts, x))
    core_own, core_other = cores(masks[-1:], parts)
    core_got = col_swap(core_other, 1)

    panels = [row_u, own_mate]
    for m in masks[1:]:
        panels += [p[m], col_swap(p[m], 1)]
    out_shape = jax.ShapeDtypeStruct((count, order, width), BF16)
    out_u, out_v = pl.pallas_call(
        functools.partial(
            final_kernel,
            masks=masks,
            block=32,
            pieces=n_row,
        ),
        in_specs=[SMEM] * 5 + [HBM] * 2 + [VMEM] * (5 + n_row + len(panels)),
        out_specs=[HBM, HBM],
        out_shape=[out_shape, out_shape],
        scratch_shapes=[
            pltpu.VMEM((count, order, width), BF16),
            pltpu.VMEM((count, order, width), BF16),
            pltpu.VMEM((count, order, width), BF16),
            pltpu.VMEM((order, width), BF16),
            pltpu.VMEM((count, order, width), BF16),
            pltpu.VMEM((count, order, width), BF16),
            pltpu.VMEM((count * width, width), F32),
            pltpu.VMEM((count * width, width), F32),
            pltpu.VMEM((count, width, 2 * width), F32),
            pltpu.VMEM((count, 8, width), F32),
            pltpu.VMEM((count, 2 * width, 2 * width), BF16),
            pltpu.VMEM((count, width, 2 * width), BF16),
            pltpu.SemaphoreType.DMA((len(panels),)),
            pltpu.SemaphoreType.DMA,
            pltpu.SemaphoreType.DMA((2,)),
        ],
        compiler_params=pltpu.CompilerParams(vmem_limit_bytes=40 * MIB),
        cost_estimate=pl.CostEstimate(
            flops=16 * count * order * width * width,
            bytes_accessed=10 * count * order * width,
            transcendentals=0,
        ),
        name="recompress_store",
    )(
        pos,
        tile_rank,
        listed,
        row_rank,
        col_rank,
        tile_u,
        tile_v,
        uu,
        core_own,
        core_got,
        vproj,
        turned,
        *x,
        *panels,
    )
    shape = (rows_here, cols_here, order, width)
    return out_u.reshape(shape), out_v.reshape(shape)


def solution(mesh):
    return jax.shard_map(
        functools.partial(on_device, mesh.shape["row"], mesh.shape["col"]),
        mesh=mesh,
        in_specs=(
            P("row", "col", None, None),
            P("row", "col", None, None),
            P("row", "col"),
            P("row", "col"),
            P("row", "col", None),
            P("row", "col", None),
            P("row"),
            P("col", "row", None),
            P("col", "row", None),
            P("col"),
            P(),
        ),
        out_specs=(P("row", "col", None, None), P("row", "col", None, None)),
        check_vma=False,
    )
```

time: 354 us -> 73.6 us (0.21)
  other arithmetic: 179 us -> 0.94 us
  matrix products: 71.1 us -> 0 us
  blocking collectives: 33.5 us -> 0 us
  Pallas kernels: 0 us -> 28.4 us
  local copies, waits for them, and re-layouts: 32.8 us -> 7.1 us
  between operations: 14.9 us -> 1.6 us
  starting transfers between devices: 0.08 us -> 12.3 us
    another operation x7 -> x1, other arithmetic: 173 us -> 0.07 us  [on_device(): jnp.stack([lax.axis_index('row'), lax.axis_index('col')]).astype(jnp.int32)]
    dot_general x6 -> x0, matrix products: 60.8 us -> none  [the longest x1 19.3 us: recompress(): jnp.einsum('nbs,nbt->nst', span, span, precision=lax.Precision.HIGHEST)]
    all_gather x2 -> x0, blocking collectives: 33.5 us -> none  [the longest x1 17.3 us: on_device(): lax.all_gather(col_u, 'row', axis=1, tiled=True)]
    pallas_call x0 -> x4, Pallas kernels: none -> 28.4 us  [the longest x1 22.8 us: on_device(): pl.pallas_call(functools.partial(final_kernel, masks=masks, block=32, pie...]
    ppermute x0 -> x18, waiting for transfers between devices: none -> 22.9 us  [the longest x2 12.3 us: on_device(): x.append(lax.ppermute(x[-1], 'row', ring))]
    unnamed x26 -> x29, local copies, waits for them, and re-layouts: 29.9 us -> 7.1 us
    all_gather x2 -> x0, waiting for transfers between devices: 20.6 us -> none  [the longest x1 20.6 us: on_device(): lax.all_gather(row_u, 'col', axis=1, tiled=True)]
    ppermute x0 -> x18, starting transfers between devices: none -> 12.3 us  [the longest x12 7.29 us: swap(): return lax.ppermute(x, axis, [(c, c ^ mask) for c in range(size)])]
  transfers between devices with their start and end apart: 2 -> 18, of which waited for: 1 -> 7; matrix products, arithmetic and copies ran while one was open for 6% -> 3% of each run, Pallas kernels for 0% -> 8%
where the time goes in v2:
time: 73.6 us; the launch traced here: 73.2 us
  Pallas kernels  28.4 us (39%)
  waiting for transfers between devices  22.9 us (31%)
  starting transfers between devices  12.3 us (17%)
  local copies, waits for them, and re-layouts  7.1 us (10%)
  between operations  1.6 us (2%)
  other arithmetic  0.94 us (1%)
    pallas_call x1, Pallas kernels, on_device(): pl.pallas_call(functools.partial(final_kernel, masks=masks, block=32, pie...  22.8 us
    ppermute x2, waiting for transfers between devices, on_device(): x.append(lax.ppermute(x[-1], 'row', ring))  12.3 us
    ppermute x12, starting transfers between devices, swap(): return lax.ppermute(x, axis, [(c, c ^ mask) for c in range(size)])  7.29 us
    unnamed x29, local copies, waits for them, and re-layouts  7.1 us
    ppermute x2, waiting for transfers between devices, on_device(): y.append(lax.ppermute(y[-1], 'row', ring))  4.36 us
    ppermute x1, waiting for transfers between devices, on_device(): y.append(lax.ppermute(passed, 'row', ring))  3.86 us
    pallas_call x1, Pallas kernels, on_device(): pl.pallas_call(local_kernel, in_specs=[SMEM, VMEM, VMEM, VMEM], out_specs...  2.97 us
    pallas_call x2, Pallas kernels, cores(): pl.pallas_call(functools.partial(core_kernel, masks=use, pieces=n_row, mo...  2.6 us
  transfers between devices with their start and end apart: 18, of which 7 were waited for; matrix products, arithmetic and copies ran while one was open for 3% of the time, Pallas kernels for 8%

profile of v2, /device:TPU:0, one launch (start us, length us, event | category | flops | bytes accessed | tf_op | source)
XLA Modules:
  0.0 73.2 jit_solution(6656434029738037371)
XLA Ops:
  0.6 3.0 %collective-permute-start.2 = (bf16[8,256,128]{2,1,0:T(8,128)(2,1)}, bf16[8,256,128]{2,1,0:T(8,128)(2,1)S(1)}, u32[]{:S(2)}, u32[]{:S(2)}) collective-permute-start(bf16[8,256,128]{2,1,0:T(8,128)(2,1)} %refs_0_), channel_id=1, source_target_pairs={{0,2},{1,3},{2,0},{3,1},{4,6},{5,7},{6,4},{7,5},{8,10},{9,11},{10,... | collective-permute-start | bytes 1572872 | tf_op jit(solution)/shard_map/ppermute | solution.py:303
  3.6 1.5 %collective-permute-start.3 = (bf16[8,256,128]{2,1,0:T(8,128)(2,1)}, bf16[8,256,128]{2,1,0:T(8,128)(2,1)S(1)}, u32[]{:S(2)}, u32[]{:S(2)}) collective-permute-start(bf16[8,256,128]{2,1,0:T(8,128)(2,1)} %refs_4_.1), channel_id=1, source_target_pairs={{0,4},{1,5},{2,6},{3,7},{4,0},{5,1},{6,2},{7,3},{8,12},{9,13},{10,... | collective-permute-start | bytes 1572872 | tf_op jit(solution)/shard_map/ppermute | solution.py:303
  5.2 1.6 %collective-permute-start = (bf16[1,512,128]{2,1,0:T(8,128)(2,1)}, bf16[1,512,128]{2,1,0:T(8,128)(2,1)S(1)}, u32[]{:S(2)}, u32[]{:S(2)}) collective-permute-start(bf16[1,512,128]{2,1,0:T(8,128)(2,1)} %refs_1_.1), channel_id=1, source_target_pairs={{0,8},{8,16},{16,24},{24,0},{1,9},{9,17},{17,25},{25,1},{2,10},{10... | collective-permute-start | bytes 393224 | tf_op jit(solution)/shard_map/ppermute | solution.py:351
  6.7 0.5 collective-permute-start.4
  7.2 0.5 collective-permute-start.5
  7.8 4.4 %collective-permute-done.refs_4_.refs_2_ = bf16[1,512,128]{2,1,0:T(8,128)(2,1)S(1)} collective-permute-done((bf16[1,512,128]{2,1,0:T(8,128)(2,1)}, bf16[1,512,128]{2,1,0:T(8,128)(2,1)S(1)}, u32[]{:S(2)}, u32[]{:S(2)}) %collective-permute-start) | collective-permute-done | bytes 131104 | tf_op jit(solution)/shard_map/ppermute | solution.py:351
  12.1 1.2 %copy.13 = bf16[2048,128]{0,1:T(8,128)(2,1)S(1)} copy(bf16[2048,128]{1,0:T(8,128)(2,1)} %param.21) | data formatting | bytes 1048576 | tf_op args[10]
  13.4 0.0 copy-start
  13.4 2.2 %copy-done = bf16[8,1,2048,128]{3,2,1,0:T(8,128)(2,1)S(1)} copy-done((bf16[8,1,2048,128]{3,2,1,0:T(8,128)(2,1)S(1)}, bf16[8,1,2048,128]{3,2,1,0:T(8,128)(2,1)}, u32[]{:S(2)}) %copy-start) | copy-done | bytes 4194328
  15.6 2.2 %copy-done.2 = bf16[8,1,2048,128]{3,2,1,0:T(8,128)(2,1)S(1)} copy-done((bf16[8,1,2048,128]{3,2,1,0:T(8,128)(2,1)S(1)}, bf16[8,1,2048,128]{3,2,1,0:T(8,128)(2,1)}, u32[]{:S(2)}) %copy-start.2) | copy-done | bytes 4194328
  17.8 0.7 copy-done.5
  18.4 3.0 %local_products.1 = (bf16[8,128,128]{2,1,0:T(8,128)(2,1)S(1)}, f32[8,128,128]{2,1,0:T(8,128)S(1)}) custom-call(s32[8]{0:T(128)S(1)} %bitcast.19, bf16[128,2048]{1,0:T(8,128)(2,1)S(1)} %bitcast.17, bf16[8,2048,128]{2,1,0:T(8,128)(2,1)S(1)} %bitcast.13, bf16[8,2048,128]{2,1,0:T(8,128)(2,1)S(1)} %bitcast.16), custom_call_target="tpu_custom_call" | custom-call | flops 1073741824 | bytes 8388608 | tf_op jit(solution)/shard_map/local_products/pallas_call | solution.py:354
  21.4 0.8 %copy-done.9 = f32[8,128,128]{2,1,0:T(8,128)} copy-done((f32[8,128,128]{2,1,0:T(8,128)}, f32[8,128,128]{2,1,0:T(8,128)S(1)}, u32[]{:S(2)}) %copy-start.9) | copy-done | bytes 524312
  22.2 1.4 %collective-permute-start.8 = (bf16[1,512,128]{2,1,0:T(8,128)(2,1)S(1)}, bf16[1,512,128]{2,1,0:T(8,128)(2,1)S(1)}, u32[]{:S(2)}, u32[]{:S(2)}) collective-permute-start(bf16[1,512,128]{2,1,0:T(8,128)(2,1)S(1)} %collective-permute-done.1.refs_5_.refs_3_), channel_id=1, source_target_pairs={{0,8},{8,16},{16,24},{24,0},{1,9},{9,17},{17,25},{25,1},{2,10},{10... | collective-permute-start | bytes 393224 | tf_op jit(solution)/shard_map/ppermute | solution.py:374
  23.6 1.6 %collective-permute-start.6 = (bf16[1,512,128]{2,1,0:T(8,128)(2,1)S(1)}, bf16[1,512,128]{2,1,0:T(8,128)(2,1)}, u32[]{:S(2)}, u32[]{:S(2)}) collective-permute-start(bf16[1,512,128]{2,1,0:T(8,128)(2,1)S(1)} %copy-done.11), channel_id=1, source_target_pairs={{0,8},{8,16},{16,24},{24,0},{1,9},{9,17},{17,25},{25,1},{2,10},{10... | collective-permute-start | bytes 393224 | tf_op jit(solution)/shard_map/ppermute | solution.py:375
  25.2 3.9 %collective-permute-done.8.refs_6_.refs_4_ = bf16[1,512,128]{2,1,0:T(8,128)(2,1)S(1)} collective-permute-done((bf16[1,512,128]{2,1,0:T(8,128)(2,1)S(1)}, bf16[1,512,128]{2,1,0:T(8,128)(2,1)S(1)}, u32[]{:S(2)}, u32[]{:S(2)}) %collective-permute-start.8) | collective-permute-done | bytes 131104 | tf_op jit(solution)/shard_map/ppermute | solution.py:374
  29.1 0.9 %pad_maximum_fusion = bf16[4,512,128]{2,1,0:T(8,128)(2,1)} fusion(bf16[1,512,128]{2,1,0:T(8,128)(2,1)S(1)} %collective-permute-done.8.refs_6_.refs_4_, bf16[1,512,128]{2,1,0:T(8,128)(2,1)S(1)} %collective-permute-done.1.refs_5_.refs_3_, bf16[1,512,128]{2,1,0:T(8,128)(2,1)S(1)} %collective-permute-done.refs_4_.refs_2_, bf16[1,512,128]{2,1,0:T(8,128)(2,1)S(1)} %copy-done.3), kind=kLoop, calls=%fused_computation | loop fusion | flops 786432 | bytes 1048576 | tf_op jit(solution)/shard_map/concatenate | solution.py:381
  30.0 0.6 collective-permute-done.6.refs_1_
  30.6 0.5 collective-permute-start.7
  31.1 0.5 collective-permute-start.16
  31.6 0.5 collective-permute-start.10
  32.1 6.6 %collective-permute-done.10.refs_2_ = bf16[1,512,128]{2,1,0:T(8,128)(2,1)} collective-permute-done((bf16[1,512,128]{2,1,0:T(8,128)(2,1)}, bf16[1,512,128]{2,1,0:T(8,128)(2,1)}, u32[]{:S(2)}, u32[]{:S(2)}) %collective-permute-start.10) | collective-permute-done | bytes 131104 | tf_op jit(solution)/shard_map/ppermute | solution.py:378
  38.7 0.1 pad_add_fusion.pos_ref
  38.8 0.0 collective-permute-start.14
  38.8 1.2 %core_products.2 = (f32[8,128,128]{2,1,0:T(8,128)S(1)}, f32[8,128,128]{2,1,0:T(8,128)S(1)}) custom-call(s32[2]{0:T(128)S(1)} %pad_add_fusion.pos_ref, bf16[8,256,128]{2,1,0:T(8,128)(2,1)S(1)} %copy-done.4, bf16[8,256,128]{2,1,0:T(8,128)(2,1)S(1)} %collective-permute-done.2.refs_1_, bf16[8,256,128]{2,1,0:T(8,128)(2,1)S(1)} %collective-permute-done.4.refs_2_, ...), custom_call_target="tpu_custom_call" | custom-call | flops 402653184 | bytes 1572864 | tf_op jit(solution)/shard_map/core_products/pallas_call | solution.py:387
  40.0 5.7 %collective-permute-done.11.refs_3_ = bf16[1,512,128]{2,1,0:T(8,128)(2,1)S(1)} collective-permute-done((bf16[1,512,128]{2,1,0:T(8,128)(2,1)}, bf16[1,512,128]{2,1,0:T(8,128)(2,1)S(1)}, u32[]{:S(2)}, u32[]{:S(2)}) %collective-permute-start.11) | collective-permute-done | bytes 131104 | tf_op jit(solution)/shard_map/ppermute | solution.py:378
  45.7 1.4 %core_products.3 = (f32[8,128,128]{2,1,0:T(8,128)S(1)}, f32[8,128,128]{2,1,0:T(8,128)S(1)}) custom-call(s32[2]{0:T(128)S(1)} %pad_add_fusion.pos_ref, bf16[8,256,128]{2,1,0:T(8,128)(2,1)} %collective-permute-done.7.refs_0_, bf16[1,512,128]{2,1,0:T(8,128)(2,1)S(1)} %copy-done.3, bf16[1,512,128]{2,1,0:T(8,128)(2,1)S(1)} %collective-permute-done.refs_4_.refs_2_, ...), custom_call_target="tpu_custom_call" | custom-call | flops 134217728 | bytes 524288 | tf_op jit(solution)/shard_map/core_products/pallas_call | solution.py:387
  47.1 0.6 collective-permute-start.12
  47.7 0.1 collective-permute-start.17
  48.5 0.8 %collective-permute-done.12.other_ref = f32[8,128,128]{2,1,0:T(8,128)S(1)} collective-permute-done((f32[8,128,128]{2,1,0:T(8,128)S(1)}, f32[8,128,128]{2,1,0:T(8,128)S(1)}, u32[]{:S(2)}, u32[]{:S(2)}) %collective-permute-start.12) | collective-permute-done | bytes 524320 | tf_op jit(solution)/shard_map/ppermute | solution.py:303
  49.2 1.0 %collective-permute-done.17.refs_11_ = bf16[8,256,128]{2,1,0:T(8,128)(2,1)S(1)} collective-permute-done((bf16[8,256,128]{2,1,0:T(8,128)(2,1)}, bf16[8,256,128]{2,1,0:T(8,128)(2,1)S(1)}, u32[]{:S(2)}, u32[]{:S(2)}) %collective-permute-start.17) | collective-permute-done | bytes 524320 | tf_op jit(solution)/shard_map/ppermute | solution.py:303
  50.2 22.8 %recompress_store.1 = (bf16[8,2048,128]{2,1,0:T(8,128)(2,1)}, bf16[8,2048,128]{2,1,0:T(8,128)(2,1)}) custom-call(s32[2]{0:T(128)S(1)} %pad_add_fusion.pos_ref, s32[8]{0:T(128)S(1)} %bitcast.20, s32[8]{0:T(128)S(1)} %bitcast.21, s32[8]{0:T(128)S(1)} %copy-done.13, s32[1]{0:T(128)S(6)} %copy.16.col_rank_ref, bf16[8,2048,128]{2,1,0:T(8,128)(2,1)S(1)} %bitcast.14, ...), custom_call_target="tpu_custom_call" | custom-call | flops 4294967296 | bytes 20971520 | tf_op jit(solution)/shard_map/recompress_store/pallas_call | solution.py:410
  (39 shorter events, 0.1 us)
Async XLA Ops:
  0.6 21.6 %collective-permute-start.2 = (bf16[8,256,128]{2,1,0:T(8,128)(2,1)}, bf16[8,256,128]{2,1,0:T(8,128)(2,1)S(1)}, u32[]{:S(2)}, u32[]{:S(2)}) collective-permute-start(bf16[8,256,128]{2,1,0:T(8,128)(2,1)} %refs_0_), channel_id=1, source_target_pairs={{0,2},{1,3},{2,0},{3,1},{4,6},{5,7},{6,4},{7,5},{8,10},{9,11},{10,... | collective-permute-start | bytes 1572872 | tf_op jit(solution)/shard_map/ppermute | solution.py:303
  3.6 18.6 %collective-permute-start.3 = (bf16[8,256,128]{2,1,0:T(8,128)(2,1)}, bf16[8,256,128]{2,1,0:T(8,128)(2,1)S(1)}, u32[]{:S(2)}, u32[]{:S(2)}) collective-permute-start(bf16[8,256,128]{2,1,0:T(8,128)(2,1)} %refs_4_.1), channel_id=1, source_target_pairs={{0,4},{1,5},{2,6},{3,7},{4,0},{5,1},{6,2},{7,3},{8,12},{9,13},{10,... | collective-permute-start | bytes 1572872 | tf_op jit(solution)/shard_map/ppermute | solution.py:303
  5.2 7.0 %collective-permute-start = (bf16[1,512,128]{2,1,0:T(8,128)(2,1)}, bf16[1,512,128]{2,1,0:T(8,128)(2,1)S(1)}, u32[]{:S(2)}, u32[]{:S(2)}) collective-permute-start(bf16[1,512,128]{2,1,0:T(8,128)(2,1)} %refs_1_.1), channel_id=1, source_target_pairs={{0,8},{8,16},{16,24},{24,0},{1,9},{9,17},{17,25},{25,1},{2,10},{10... | collective-permute-start | bytes 393224 | tf_op jit(solution)/shard_map/ppermute | solution.py:351
  6.7 23.2 %collective-permute-start.4 = (bf16[8,256,128]{2,1,0:T(8,128)(2,1)}, bf16[8,256,128]{2,1,0:T(8,128)(2,1)S(1)}, u32[]{:S(2)}, u32[]{:S(2)}) collective-permute-start(bf16[8,256,128]{2,1,0:T(8,128)(2,1)} %refs_0_), channel_id=1, source_target_pairs={{0,4},{1,5},{2,6},{3,7},{4,0},{5,1},{6,2},{7,3},{8,12},{9,13},{10,... | collective-permute-start | bytes 1572872 | tf_op jit(solution)/shard_map/ppermute | solution.py:303
  7.2 22.7 %collective-permute-start.5 = (bf16[8,256,128]{2,1,0:T(8,128)(2,1)}, bf16[8,256,128]{2,1,0:T(8,128)(2,1)}, u32[]{:S(2)}, u32[]{:S(2)}) collective-permute-start(bf16[8,256,128]{2,1,0:T(8,128)(2,1)} %refs_4_.1), channel_id=1, source_target_pairs={{0,2},{1,3},{2,0},{3,1},{4,6},{5,7},{6,4},{7,5},{8,10},{9,11},{10,... | collective-permute-start | bytes 1572872 | tf_op jit(solution)/shard_map/ppermute | solution.py:303
  12.1 10.1 %collective-permute-start.1 = (bf16[1,512,128]{2,1,0:T(8,128)(2,1)S(1)}, bf16[1,512,128]{2,1,0:T(8,128)(2,1)S(1)}, u32[]{:S(2)}, u32[]{:S(2)}) collective-permute-start(bf16[1,512,128]{2,1,0:T(8,128)(2,1)S(1)} %collective-permute-done.refs_4_.refs_2_), channel_id=1, source_target_pairs={{0,8},{8,16},{16,24},{24,0},{1,9},{9,17},{17,25},{25,1},{2,10},{10... | collective-permute-start | bytes 393224 | tf_op jit(solution)/shard_map/ppermute | solution.py:351
  13.4 2.2 %copy-start = (bf16[8,1,2048,128]{3,2,1,0:T(8,128)(2,1)S(1)}, bf16[8,1,2048,128]{3,2,1,0:T(8,128)(2,1)}, u32[]{:S(2)}) copy-start(bf16[8,1,2048,128]{3,2,1,0:T(8,128)(2,1)} %param.11) | copy-start | bytes 12582916
  15.6 2.2 %copy-start.2 = (bf16[8,1,2048,128]{3,2,1,0:T(8,128)(2,1)S(1)}, bf16[8,1,2048,128]{3,2,1,0:T(8,128)(2,1)}, u32[]{:S(2)}) copy-start(bf16[8,1,2048,128]{3,2,1,0:T(8,128)(2,1)} %param.12) | copy-start | bytes 12582916
  17.8 0.7 copy-start.5
  18.4 5.2 %copy-start.11 = (bf16[1,512,128]{2,1,0:T(8,128)(2,1)S(1)}, bf16[1,512,128]{2,1,0:T(8,128)(2,1)}, u32[]{:S(2)}) copy-start(bf16[1,512,128]{2,1,0:T(8,128)(2,1)} %refs_0_.1) | copy-start | bytes 393220
  18.4 10.7 %copy-start.3 = (bf16[1,512,128]{2,1,0:T(8,128)(2,1)S(1)}, bf16[1,512,128]{2,1,0:T(8,128)(2,1)}, u32[]{:S(2)}) copy-start(bf16[1,512,128]{2,1,0:T(8,128)(2,1)} %refs_1_.1) | copy-start | bytes 393220
  18.4 20.4 %copy-start.4 = (bf16[8,256,128]{2,1,0:T(8,128)(2,1)S(1)}, bf16[8,256,128]{2,1,0:T(8,128)(2,1)}, u32[]{:S(2)}) copy-start(bf16[8,256,128]{2,1,0:T(8,128)(2,1)} %refs_0_) | copy-start | bytes 1572868
  21.4 0.8 %copy-start.9 = (f32[8,128,128]{2,1,0:T(8,128)}, f32[8,128,128]{2,1,0:T(8,128)S(1)}, u32[]{:S(2)}) copy-start(f32[8,128,128]{2,1,0:T(8,128)S(1)} %get-tuple-element.36.uu_ref) | copy-start | bytes 1572868
  22.2 28.0 %copy-start.6 = (s32[8,1]{0,1:T(1,128)S(1)}, s32[8,1]{0,1:T(1,128)}, u32[]{:S(2)}) copy-start(s32[8,1]{0,1:T(1,128)} %param.13) | copy-start | bytes 100
  22.2 28.0 %copy-start.12 = (s32[8,1]{0,1:T(1,128)S(1)}, s32[8,1]{0,1:T(1,128)}, u32[]{:S(2)}) copy-start(s32[8,1]{0,1:T(1,128)} %param.14) | copy-start | bytes 100
  22.2 28.0 %copy-start.13 = (s32[8]{0:T(128)S(1)}, s32[8]{0:T(128)}, u32[]{:S(2)}) copy-start(s32[8]{0:T(128)} %row_rank_ref.1) | copy-start | bytes 100
  22.2 6.9 %copy-start.7 = (bf16[8,256,128]{2,1,0:T(8,128)(2,1)}, bf16[8,256,128]{2,1,0:T(8,128)(2,1)S(1)}, u32[]{:S(2)}) copy-start(bf16[8,256,128]{2,1,0:T(8,128)(2,1)S(1)} %collective-permute-done.3.refs_8_) | copy-start | bytes 1572868
  22.2 6.8 %collective-permute-start.8 = (bf16[1,512,128]{2,1,0:T(8,128)(2,1)S(1)}, bf16[1,512,128]{2,1,0:T(8,128)(2,1)S(1)}, u32[]{:S(2)}, u32[]{:S(2)}) collective-permute-start(bf16[1,512,128]{2,1,0:T(8,128)(2,1)S(1)} %collective-permute-done.1.refs_5_.refs_3_), channel_id=1, source_target_pairs={{0,8},{8,16},{16,24},{24,0},{1,9},{9,17},{17,25},{25,1},{2,10},{10... | collective-permute-start | bytes 393224 | tf_op jit(solution)/shard_map/ppermute | solution.py:374
  23.6 6.9 %collective-permute-start.6 = (bf16[1,512,128]{2,1,0:T(8,128)(2,1)S(1)}, bf16[1,512,128]{2,1,0:T(8,128)(2,1)}, u32[]{:S(2)}, u32[]{:S(2)}) collective-permute-start(bf16[1,512,128]{2,1,0:T(8,128)(2,1)S(1)} %copy-done.11), channel_id=1, source_target_pairs={{0,8},{8,16},{16,24},{24,0},{1,9},{9,17},{17,25},{25,1},{2,10},{10... | collective-permute-start | bytes 393224 | tf_op jit(solution)/shard_map/ppermute | solution.py:375
  30.0 8.8 %collective-permute-start.9 = (bf16[4,512,128]{2,1,0:T(8,128)(2,1)}, bf16[4,512,128]{2,1,0:T(8,128)(2,1)S(1)}, u32[]{:S(2)}, u32[]{:S(2)}) collective-permute-start(bf16[4,512,128]{2,1,0:T(8,128)(2,1)} %pad_maximum_fusion), channel_id=1, source_target_pairs={{0,1},{1,0},{2,3},{3,2},{4,5},{5,4},{6,7},{7,6},{8,9},{9,8},{10,11... | collective-permute-start | bytes 1572872 | tf_op jit(solution)/shard_map/ppermute | solution.py:303
  30.6 15.1 %collective-permute-start.7 = (bf16[8,256,128]{2,1,0:T(8,128)(2,1)S(1)}, bf16[8,256,128]{2,1,0:T(8,128)(2,1)}, u32[]{:S(2)}, u32[]{:S(2)}) collective-permute-start(bf16[8,256,128]{2,1,0:T(8,128)(2,1)S(1)} %collective-permute-done.4.refs_2_), channel_id=1, source_target_pairs={{0,2},{1,3},{2,0},{3,1},{4,6},{5,7},{6,4},{7,5},{8,10},{9,11},{10,... | collective-permute-start | bytes 1572872 | tf_op jit(solution)/shard_map/ppermute | solution.py:303
  31.1 16.6 %collective-permute-start.16 = (bf16[8,256,128]{2,1,0:T(8,128)(2,1)}, bf16[8,256,128]{2,1,0:T(8,128)(2,1)}, u32[]{:S(2)}, u32[]{:S(2)}) collective-permute-start(bf16[8,256,128]{2,1,0:T(8,128)(2,1)} %collective-permute-done.5.refs_6_), channel_id=1, source_target_pairs={{0,4},{1,5},{2,6},{3,7},{4,0},{5,1},{6,2},{7,3},{8,12},{9,13},{10,... | collective-permute-start | bytes 1572872 | tf_op jit(solution)/shard_map/ppermute | solution.py:303
  31.6 7.1 %collective-permute-start.10 = (bf16[1,512,128]{2,1,0:T(8,128)(2,1)}, bf16[1,512,128]{2,1,0:T(8,128)(2,1)}, u32[]{:S(2)}, u32[]{:S(2)}) collective-permute-start(bf16[1,512,128]{2,1,0:T(8,128)(2,1)} %collective-permute-done.6.refs_1_), channel_id=1, source_target_pairs={{0,8},{8,16},{16,24},{24,0},{1,9},{9,17},{17,25},{25,1},{2,10},{10... | collective-permute-start | bytes 393224 | tf_op jit(solution)/shard_map/ppermute | solution.py:378
  32.1 16.3 %collective-permute-start.13 = (bf16[8,256,128]{2,1,0:T(8,128)(2,1)}, bf16[8,256,128]{2,1,0:T(8,128)(2,1)}, u32[]{:S(2)}, u32[]{:S(2)}) collective-permute-start(bf16[8,256,128]{2,1,0:T(8,128)(2,1)} %refs_4_.1), channel_id=1, source_target_pairs={{0,1},{1,0},{2,3},{3,2},{4,5},{5,4},{6,7},{7,6},{8,9},{9,8},{10,11... | collective-permute-start | bytes 1572872 | tf_op jit(solution)/shard_map/ppermute | solution.py:303
  32.1 18.1 %copy-start.1 = (bf16[8,1,2048,128]{3,2,1,0:T(8,128)(2,1)S(1)}, bf16[8,1,2048,128]{3,2,1,0:T(8,128)(2,1)}, u32[]{:S(2)}) copy-start(bf16[8,1,2048,128]{3,2,1,0:T(8,128)(2,1)} %param.11) | copy-start | bytes 12582916
  32.1 18.1 %copy-start.8 = (bf16[8,256,128]{2,1,0:T(8,128)(2,1)S(1)}, bf16[8,256,128]{2,1,0:T(8,128)(2,1)}, u32[]{:S(2)}) copy-start(bf16[8,256,128]{2,1,0:T(8,128)(2,1)} %copy-done.7) | copy-start | bytes 1572868
  32.1 18.1 %copy-start.10 = (f32[8,128,128]{2,1,0:T(8,128)S(1)}, f32[8,128,128]{2,1,0:T(8,128)}, u32[]{:S(2)}) copy-start(f32[8,128,128]{2,1,0:T(8,128)} %copy-done.9) | copy-start | bytes 1572868
  38.7 7.0 %collective-permute-start.11 = (bf16[1,512,128]{2,1,0:T(8,128)(2,1)}, bf16[1,512,128]{2,1,0:T(8,128)(2,1)S(1)}, u32[]{:S(2)}, u32[]{:S(2)}) collective-permute-start(bf16[1,512,128]{2,1,0:T(8,128)(2,1)} %collective-permute-done.10.refs_2_), channel_id=1, source_target_pairs={{0,8},{8,16},{16,24},{24,0},{1,9},{9,17},{17,25},{25,1},{2,10},{10... | collective-permute-start | bytes 393224 | tf_op jit(solution)/shard_map/ppermute | solution.py:378
  38.8 9.7 %collective-permute-start.14 = (bf16[8,256,128]{2,1,0:T(8,128)(2,1)}, bf16[8,256,128]{2,1,0:T(8,128)(2,1)S(1)}, u32[]{:S(2)}, u32[]{:S(2)}) collective-permute-start(bf16[8,256,128]{2,1,0:T(8,128)(2,1)} %collective-permute-done.5.refs_6_), channel_id=1, source_target_pairs={{0,1},{1,0},{2,3},{3,2},{4,5},{5,4},{6,7},{7,6},{8,9},{9,8},{10,11... | collective-permute-start | bytes 1572872 | tf_op jit(solution)/shard_map/ppermute | solution.py:303
  45.7 2.8 %collective-permute-start.15 = (bf16[8,256,128]{2,1,0:T(8,128)(2,1)}, bf16[8,256,128]{2,1,0:T(8,128)(2,1)S(1)}, u32[]{:S(2)}, u32[]{:S(2)}) collective-permute-start(bf16[8,256,128]{2,1,0:T(8,128)(2,1)} %copy-done.7), channel_id=1, source_target_pairs={{0,1},{1,0},{2,3},{3,2},{4,5},{5,4},{6,7},{7,6},{8,9},{9,8},{10,11... | collective-permute-start | bytes 1572872 | tf_op jit(solution)/shard_map/ppermute | solution.py:303
  47.1 2.1 %collective-permute-start.12 = (f32[8,128,128]{2,1,0:T(8,128)S(1)}, f32[8,128,128]{2,1,0:T(8,128)S(1)}, u32[]{:S(2)}, u32[]{:S(2)}) collective-permute-start(f32[8,128,128]{2,1,0:T(8,128)S(1)} %get-tuple-element.48), channel_id=1, source_target_pairs={{0,1},{1,0},{2,3},{3,2},{4,5},{5,4},{6,7},{7,6},{8,9},{9,8},{10,11... | collective-permute-start | bytes 1572872 | tf_op jit(solution)/shard_map/ppermute | solution.py:303
  47.7 2.5 %collective-permute-start.17 = (bf16[8,256,128]{2,1,0:T(8,128)(2,1)}, bf16[8,256,128]{2,1,0:T(8,128)(2,1)S(1)}, u32[]{:S(2)}, u32[]{:S(2)}) collective-permute-start(bf16[8,256,128]{2,1,0:T(8,128)(2,1)} %collective-permute-done.16.refs_10_), channel_id=1, source_target_pairs={{0,1},{1,0},{2,3},{3,2},{4,5},{5,4},{6,7},{7,6},{8,9},{9,8},{10,11... | collective-permute-start | bytes 1572872 | tf_op jit(solution)/shard_map/ppermute | solution.py:303

commit v3 on v2

--- a/solution.py
+++ b/solution.py
@@ -32,13 +32,17 @@
     return lax.broadcasted_iota(jnp.int32, shape, len(shape) - 2)
 
 
-def local_kernel(rank_ref, st_ref, u_ref, v_ref, proj_ref, uu_ref):
+def gram_kernel(u_ref, uu_ref):
     for t in range(u_ref.shape[0]):
+        u = u_ref[t]
+        uu_ref[t] = dot(u, u, 0, 0)
+
+
+def proj_kernel(rank_ref, st_ref, v_ref, proj_ref):
+    for t in range(v_ref.shape[0]):
         proj = dot(st_ref[...], v_ref[t])
         keep = lanes(proj.shape) < rank_ref[t]
         proj_ref[t] = jnp.where(keep, proj, 0.0).astype(BF16)
-        u = u_ref[t]
-        uu_ref[t] = dot(u, u, 0, 0)
 
 
 def core_kernel(pos_ref, *refs, masks, pieces, more):
@@ -106,6 +110,7 @@
         rs,
         ts,
         scales,
+        mixes,
         to_mix,
         to_coef,
         sem_u,
@@ -154,31 +159,31 @@
     for copy in loads:
         copy.wait()
 
-    def assemble(t):
+    for t in range(count):
         left = left_buf[t]
-        low = dot(left, jnp.concatenate([u_buf[t], left], axis=1), 0, 0)
+        ts[t] = dot(left, jnp.concatenate([u_buf[t], left], axis=1), 0, 0)
+    b = xproj
+    for t in range(count):
+        low = ts[t]
         lu_h, lu_l = halves(low[:, :width])
         ll_h, ll_l = halves(low[:, width:])
         uu_h, uu_l = halves(uu_ref[t])
-        a, b = vproj_ref[t], xproj
+        a = vproj_ref[t]
         left_part = dot(a, uu_h) + dot(a, uu_l) + dot(b, lu_h) + dot(b, lu_l)
         right_part = dot(a, lu_h, 1, 1) + dot(a, lu_l, 1, 1) + dot(b, ll_h) + dot(b, ll_l)
-        moved = jnp.concatenate([left_part, right_part], axis=1)
-        ts[t] = moved
-        moved_h, moved_l = halves(moved)
-        weights = jnp.concatenate([a, b], axis=1)
-        gram = dot(moved_h, weights, 1, 1) + dot(moved_l, weights, 1, 1)
+        ts[t] = jnp.concatenate([left_part, right_part], axis=1)
+    for t in range(count):
+        moved_h, moved_l = halves(ts[t])
+        weights = jnp.concatenate([vproj_ref[t], b], axis=1)
+        gs[pl.ds(t * width, width), :] = dot(moved_h, weights, 1, 1) + dot(moved_l, weights, 1, 1)
+    for t in range(count):
+        at = pl.ds(t * width, width)
+        gram = gs[at, :]
         diag = jnp.where(eye, gram, 0.0)
         trace = jnp.sum(jnp.sum(diag, axis=1, keepdims=True), axis=0, keepdims=True)
         scale = trace / width + 0.0001
-        inverse = 1.0 / scale
-        gs[pl.ds(t * width, width), :] = gram * inverse + jnp.where(
-            eye, 0.01, 0.0
-        )
+        gs[at, :] = gram * (1.0 / scale) + jnp.where(eye, 0.01, 0.0)
         scales[t] = jnp.broadcast_to(lax.rsqrt(scale), scales.shape[1:])
-
-    for t in range(count):
-        assemble(t)
 
     lane = lanes((count, width))
     small = 8
@@ -223,44 +228,45 @@
             strip_lane = lanes(strip)
             own = k0 + rows_of(strip)
             group = min(count, width // block)
+            ahead, use = [], []
+            for n in range(count):
+                done = ready[n]
+                ahead.append(jnp.where(strip_lane >= end, done, 0.0))
+                use.append(jnp.where((strip_lane > own) & (strip_lane < end), 0.0, done))
+            changes = []
             for g in range(0, count, group):
-                ahead, use = [], []
-                for n in range(g, g + group):
-                    done = ready[n]
-                    ahead.append(jnp.where(strip_lane >= end, done, 0.0))
-                    use.append(
-                        jnp.where((strip_lane > own) & (strip_lane < end), 0.0, done)
-                    )
-                turned = jnp.concatenate(ahead, axis=0).T[end:]
-                a_h, a_l = halves(turned)
+                a_h, a_l = halves(jnp.concatenate(ahead[g : g + group], axis=0).T[end:])
                 both = jnp.concatenate([a_h, a_l], axis=1)
                 for n in range(0, group, 2):
                     cells = []
                     for m in (n, n + 1):
                         spread = [jnp.zeros(strip, F32)] * group
-                        spread[m] = use[m]
+                        spread[m] = use[g + m]
                         cells.append(jnp.concatenate(spread, axis=0))
                     b_h, b_l = halves(jnp.concatenate(cells, axis=1))
                     change = dot(both, jnp.concatenate([b_h, b_h], axis=0)) + dot(a_h, b_l)
-                    for m in (n, n + 1):
-                        rest = pl.ds((g + m) * width + end, width - end)
-                        old = gs[rest, :]
-                        gone = lanes(old.shape)
-                        old = jnp.where((gone >= k0) & (gone < end), 0.0, old)
-                        gs[rest, :] = old - change[:, (m - n) * width : (m - n + 1) * width]
-
-    def weigh(t):
+                    changes += [change[:, :width], change[:, width:]]
+            for n in range(count):
+                rest = pl.ds(n * width + end, width - end)
+                old = gs[rest, :]
+                gone = lanes(old.shape)
+                gs[rest, :] = jnp.where((gone >= k0) & (gone < end), 0.0, old) - changes[n]
+
+    for t in range(count):
+        at = pl.ds(t * width, width)
+        inverse = jnp.where(lanes(square) <= rows_of(square), rs[at, :], 0.0)
+        rs[at, :] = inverse * (scales[t][:1, :1] * (float(order) ** 0.5))
+    for t in range(count):
+        inv_h, inv_l = halves(rs[pl.ds(t * width, width), :])
+        weights = jnp.concatenate([vproj_ref[t], b], axis=1)
+        mixes[t] = dot(inv_h, weights) + dot(inv_l, weights)
+        moved_h, moved_l = halves(ts[t])
+        ts[t] = dot(inv_h, moved_h) + dot(inv_h, moved_l) + dot(inv_l, moved_h)
+    for t in range(count):
         tile_rank = rank_ref[t]
         picked = listed_ref[t] == 1
-        inverse = rs[pl.ds(t * width, width), :]
-        inverse = jnp.where(lanes(square) <= rows_of(square), inverse, 0.0)
-        inverse = inverse * (scales[t][:1, :1] * (float(order) ** 0.5))
-        inv_h, inv_l = halves(inverse)
-        weights = jnp.concatenate([vproj_ref[t], xproj], axis=1)
-        mixed = dot(inv_h, weights) + dot(inv_l, weights)
-        mixed_h, mixed_l = halves(mixed)
-        moved_h, moved_l = halves(ts[t])
-        coef = dot(inv_h, moved_h) + dot(inv_h, moved_l) + dot(inv_l, moved_h)
+        mixed_h, mixed_l = halves(mixes[t])
+        coef = ts[t]
         coef = coef * (1.0 / order)
         wide = coef.shape
         col = lanes(wide)
@@ -279,11 +285,9 @@
         to_mix[t] = both
         to_coef[t] = coef
 
-    for t in range(count):
-        weigh(t)
     load_v.wait()
 
-    def finish(t, carry):
+    def finish(t):
         side = jnp.concatenate([u_buf[t], left_buf[t]], axis=1)
         result = dot(side, to_mix[t], 1, 1)
         to_u[t] = (result[:, :width] + result[:, width:]).astype(BF16)
@@ -292,9 +296,9 @@
         side = jnp.concatenate([v_buf[t], x_buf[...]], axis=1)
         to_v[t] = dot(side, to_coef[t], 1, 1).astype(BF16)
         send_v(t).start()
-        return carry
-
-    lax.fori_loop(0, count, finish, 0)
+
+    for t in range(count):
+        finish(t)
     pltpu.make_async_copy(to_u, out_u, sem_out.at[0]).wait()
     pltpu.make_async_copy(to_v, out_v, sem_out.at[1]).wait()
 
@@ -343,39 +347,48 @@
                     found[r | m] = col_swap(found[r], m)
         return found
 
-    ring = [(c, (c + 1) % n_row) for c in range(n_row)]
+    def shift(v, step):
+        return lax.ppermute(v, "row", [(c, (c + step) % n_row) for c in range(n_row)])
+
     q = {0: row_v, **{m: col_swap(row_v, m) for m in dims}}
     p = {0: row_u, **{m: col_swap(row_u, m) for m in dims}}
     y = [col_v]
     for _ in range(n_row - 2):
-        y.append(lax.ppermute(y[-1], "row", ring))
+        y.append(shift(y[-1], 1))
+    cost = pl.CostEstimate(
+        flops=2 * count * order * width * width,
+        bytes_accessed=2 * count * order * width,
+        transcendentals=0,
+    )
+    uu = pl.pallas_call(
+        gram_kernel,
+        in_specs=[VMEM],
+        out_specs=VMEM,
+        out_shape=jax.ShapeDtypeStruct((count, width, width), F32),
+        compiler_params=pltpu.CompilerParams(vmem_limit_bytes=16 * MIB),
+        cost_estimate=cost,
+        name="gram_products",
+    )(tile_u)
+    y[-1], x_own, q[dims[0]], p[dims[-1]], uu = tie(
+        (y[-1], col_u, q[dims[0]], p[dims[-1]], uu)
+    )
+    y.append(shift(y[-1], 1))
+    x = [x_own, shift(x_own, 1)]
+    q, p, x, tile_v, sketch = tie((q, p, x, tile_v, sketch))
     turned = sketch.T
-
-    vproj, uu = pl.pallas_call(
-        local_kernel,
-        in_specs=[SMEM, VMEM, VMEM, VMEM],
-        out_specs=[VMEM, VMEM],
-        out_shape=[
-            jax.ShapeDtypeStruct((count, width, width), BF16),
-            jax.ShapeDtypeStruct((count, width, width), F32),
-        ],
+    vproj = pl.pallas_call(
+        proj_kernel,
+        in_specs=[SMEM, VMEM, VMEM],
+        out_specs=VMEM,
+        out_shape=jax.ShapeDtypeStruct((count, width, width), BF16),
         compiler_params=pltpu.CompilerParams(vmem_limit_bytes=16 * MIB),
-        cost_estimate=pl.CostEstimate(
-            flops=4 * count * order * width * width,
-            bytes_accessed=4 * count * order * width,
-            transcendentals=0,
-        ),
-        name="local_products",
-    )(tile_rank, turned, tile_u, tile_v)
-
-    passed, vproj, x_own, q[dims[0]], p[dims[-1]] = tie(
-        (y[-1], vproj, col_u, q[dims[0]], p[dims[-1]])
-    )
-    y.append(lax.ppermute(passed, "row", ring))
-    x = [x_own, lax.ppermute(x_own, "row", ring)]
-    q, p, vproj, uu, x = tie((q, p, vproj, uu, x))
-    for _ in range(n_row - 2):
-        x.append(lax.ppermute(x[-1], "row", ring))
+        cost_estimate=cost,
+        name="sketch_products",
+    )(tile_rank, turned, tile_v)
+    back = shift(x[0], -1)
+    for _ in range(n_row - 3):
+        x.append(shift(x[-1], 1))
+    x.append(back)
     q = gather(row_v, dims, q)
     p = gather(row_u, dims[::-1], p)
     y_other = col_swap(jnp.concatenate(y, axis=0), 1)
@@ -399,7 +412,7 @@
         )(pos, *[q[m] for m in use], *y, y_other, *before)
 
     parts = cores(masks[:-1], []) if len(masks) > 1 else []
-    parts, x = tie((parts, x))
+    parts, x, vproj = tie((parts, x, vproj))
     core_own, core_other = cores(masks[-1:], parts)
     core_got = col_swap(core_other, 1)
 
@@ -428,6 +441,7 @@
             pltpu.VMEM((count * width, width), F32),
             pltpu.VMEM((count, width, 2 * width), F32),
             pltpu.VMEM((count, 8, width), F32),
+            pltpu.VMEM((count, width, 2 * width), F32),
             pltpu.VMEM((count, 2 * width, 2 * width), BF16),
             pltpu.VMEM((count, width, 2 * width), BF16),
             pltpu.SemaphoreType.DMA((len(panels),)),

time: 73.6 us -> 64.2 us (0.87)
  waiting for transfers between devices: 22.9 us -> 15.1 us
  Pallas kernels: 28.4 us -> 23.4 us
  starting transfers between devices: 12.3 us -> 17.1 us
  local copies, waits for them, and re-layouts: 7.1 us -> 5.67 us
    ppermute x6, waiting for transfers between devices: 21.1 us -> 11.5 us  [shift(): lax.ppermute(v, 'row', [(c, (c + step) % n_row) for c in range(n_row)])]
    pallas_call x1, Pallas kernels: 22.8 us -> 17.7 us  [on_device(): pl.pallas_call(functools.partial(final_kernel, masks=masks, block=32, pie...]
    ppermute x6, starting transfers between devices: 5.03 us -> 8.11 us  [shift(): lax.ppermute(v, 'row', [(c, (c + step) % n_row) for c in range(n_row)])]
    unnamed x29 -> x28, local copies, waits for them, and re-layouts: 7.1 us -> 4.42 us
    ppermute x12, waiting for transfers between devices: 1.75 us -> 3.6 us  [swap(): return lax.ppermute(x, axis, [(c, c ^ mask) for c in range(size)])]
    ppermute x12, starting transfers between devices: 7.29 us -> 8.97 us  [swap(): return lax.ppermute(x, axis, [(c, c ^ mask) for c in range(size)])]
    optimization_barrier x0 -> x1, local copies, waits for them, and re-layouts: none -> 1.24 us  [on_device(): q, p, x, tile_v, sketch = tie((q, p, x, tile_v, sketch))]
    pallas_call x1 -> x2, Pallas kernels: 2.97 us -> 3.13 us  [the longest x1 1.83 us: on_device(): pl.pallas_call(proj_kernel, in_specs=[SMEM, VMEM, VMEM], out_specs=VMEM,...]
  transfers between devices with their start and end apart: 18 -> 18, of which waited for: 7 -> 6; matrix products, arithmetic and copies ran while one was open for 3% -> 3% of each run, Pallas kernels for 8% -> 9%
where the time goes in v3:
time: 64.2 us; the launch traced here: 63.8 us
  Pallas kernels  23.4 us (36%)
  starting transfers between devices  17.1 us (27%)
  waiting for transfers between devices  15.1 us (24%)
  local copies, waits for them, and re-layouts  5.67 us (9%)
  between operations  1.64 us (3%)
  other arithmetic  0.94 us (1%)
    pallas_call x1, Pallas kernels, on_device(): pl.pallas_call(functools.partial(final_kernel, masks=masks, block=32, pie...  17.7 us
    ppermute x6, waiting for transfers between devices, shift(): lax.ppermute(v, 'row', [(c, (c + step) % n_row) for c in range(n_row)])  11.5 us
    ppermute x12, starting transfers between devices, swap(): return lax.ppermute(x, axis, [(c, c ^ mask) for c in range(size)])  8.97 us
    ppermute x6, starting transfers between devices, shift(): lax.ppermute(v, 'row', [(c, (c + step) % n_row) for c in range(n_row)])  8.11 us
    unnamed x28, local copies, waits for them, and re-layouts  4.42 us
    ppermute x12, waiting for transfers between devices, swap(): return lax.ppermute(x, axis, [(c, c ^ mask) for c in range(size)])  3.6 us
    pallas_call x2, Pallas kernels, cores(): pl.pallas_call(functools.partial(core_kernel, masks=use, pieces=n_row, mo...  2.6 us
    pallas_call x1, Pallas kernels, on_device(): pl.pallas_call(proj_kernel, in_specs=[SMEM, VMEM, VMEM], out_specs=VMEM,...  1.83 us
  transfers between devices with their start and end apart: 18, of which 6 were waited for; matrix products, arithmetic and copies ran while one was open for 3% of the time, Pallas kernels for 9%

profile of v3, /device:TPU:0, one launch (start us, length us, event | category | flops | bytes accessed | tf_op | source)
XLA Modules:
  0.0 63.8 jit_solution(10527704547015205921)
XLA Ops:
  0.6 3.0 %collective-permute-start.2 = (bf16[8,256,128]{2,1,0:T(8,128)(2,1)}, bf16[8,256,128]{2,1,0:T(8,128)(2,1)S(1)}, u32[]{:S(2)}, u32[]{:S(2)}) collective-permute-start(bf16[8,256,128]{2,1,0:T(8,128)(2,1)} %refs_0_), channel_id=1, source_target_pairs={{0,2},{1,3},{2,0},{3,1},{4,6},{5,7},{6,4},{7,5},{8,10},{9,11},{10,... | collective-permute-start | bytes 1572872 | tf_op jit(solution)/shard_map/ppermute | solution.py:307
  3.6 1.5 %collective-permute-start.3 = (bf16[8,256,128]{2,1,0:T(8,128)(2,1)}, bf16[8,256,128]{2,1,0:T(8,128)(2,1)S(1)}, u32[]{:S(2)}, u32[]{:S(2)}) collective-permute-start(bf16[8,256,128]{2,1,0:T(8,128)(2,1)} %refs_4_.1), channel_id=1, source_target_pairs={{0,4},{1,5},{2,6},{3,7},{4,0},{5,1},{6,2},{7,3},{8,12},{9,13},{10,... | collective-permute-start | bytes 1572872 | tf_op jit(solution)/shard_map/ppermute | solution.py:307
  5.2 1.6 %collective-permute-start = (bf16[1,512,128]{2,1,0:T(8,128)(2,1)}, bf16[1,512,128]{2,1,0:T(8,128)(2,1)S(1)}, u32[]{:S(2)}, u32[]{:S(2)}) collective-permute-start(bf16[1,512,128]{2,1,0:T(8,128)(2,1)} %refs_1_.1), channel_id=1, source_target_pairs={{0,8},{8,16},{16,24},{24,0},{1,9},{9,17},{17,25},{25,1},{2,10},{10... | collective-permute-start | bytes 393224 | tf_op jit(solution)/shard_map/ppermute | solution.py:351
  6.7 0.5 collective-permute-start.4
  7.2 0.5 collective-permute-start.5
  7.8 4.4 %collective-permute-done.refs_4_.refs_2_ = bf16[1,512,128]{2,1,0:T(8,128)(2,1)S(1)} collective-permute-done((bf16[1,512,128]{2,1,0:T(8,128)(2,1)}, bf16[1,512,128]{2,1,0:T(8,128)(2,1)S(1)}, u32[]{:S(2)}, u32[]{:S(2)}) %collective-permute-start) | collective-permute-done | bytes 131104 | tf_op jit(solution)/shard_map/ppermute | solution.py:351
  12.1 2.2 %copy-done.1 = bf16[8,1,2048,128]{3,2,1,0:T(8,128)(2,1)S(1)} copy-done((bf16[8,1,2048,128]{3,2,1,0:T(8,128)(2,1)S(1)}, bf16[8,1,2048,128]{3,2,1,0:T(8,128)(2,1)}, u32[]{:S(2)}) %copy-start.1) | copy-done | bytes 4194328
  14.3 1.3 %gram_products.1.uu_ref = f32[8,128,128]{2,1,0:T(8,128)S(1)} custom-call(bf16[8,2048,128]{2,1,0:T(8,128)(2,1)S(1)} %bitcast.15), custom_call_target="tpu_custom_call" | custom-call | flops 536870912 | bytes 4194304 | tf_op jit(solution)/shard_map/gram_products/pallas_call | solution.py:363
  15.6 0.0 copy-start.4
  15.6 3.3 %collective-permute-done.1.refs_5_.refs_3_ = bf16[1,512,128]{2,1,0:T(8,128)(2,1)S(1)} collective-permute-done((bf16[1,512,128]{2,1,0:T(8,128)(2,1)S(1)}, bf16[1,512,128]{2,1,0:T(8,128)(2,1)S(1)}, u32[]{:S(2)}, u32[]{:S(2)}) %collective-permute-start.1) | collective-permute-done | bytes 131104 | tf_op jit(solution)/shard_map/ppermute | solution.py:351
  18.9 1.4 %collective-permute-start.8 = (bf16[1,512,128]{2,1,0:T(8,128)(2,1)S(1)}, bf16[1,512,128]{2,1,0:T(8,128)(2,1)S(1)}, u32[]{:S(2)}, u32[]{:S(2)}) collective-permute-start(bf16[1,512,128]{2,1,0:T(8,128)(2,1)S(1)} %collective-permute-done.1.refs_5_.refs_3_), channel_id=1, source_target_pairs={{0,8},{8,16},{16,24},{24,0},{1,9},{9,17},{17,25},{25,1},{2,10},{10... | collective-permute-start | bytes 393224 | tf_op jit(solution)/shard_map/ppermute | solution.py:351
  20.3 1.6 %collective-permute-start.6 = (bf16[1,512,128]{2,1,0:T(8,128)(2,1)S(1)}, bf16[1,512,128]{2,1,0:T(8,128)(2,1)S(1)}, u32[]{:S(2)}, u32[]{:S(2)}) collective-permute-start(bf16[1,512,128]{2,1,0:T(8,128)(2,1)S(1)} %copy-done.11), channel_id=1, source_target_pairs={{0,8},{8,16},{16,24},{24,0},{1,9},{9,17},{17,25},{25,1},{2,10},{10... | collective-permute-start | bytes 393224 | tf_op jit(solution)/shard_map/ppermute | solution.py:351
  21.9 3.9 %collective-permute-done.8.refs_6_.refs_4_ = bf16[1,512,128]{2,1,0:T(8,128)(2,1)S(1)} collective-permute-done((bf16[1,512,128]{2,1,0:T(8,128)(2,1)S(1)}, bf16[1,512,128]{2,1,0:T(8,128)(2,1)S(1)}, u32[]{:S(2)}, u32[]{:S(2)}) %collective-permute-start.8) | collective-permute-done | bytes 131104 | tf_op jit(solution)/shard_map/ppermute | solution.py:351
  25.8 0.9 %pad_maximum_fusion = bf16[4,512,128]{2,1,0:T(8,128)(2,1)} fusion(bf16[1,512,128]{2,1,0:T(8,128)(2,1)S(1)} %collective-permute-done.8.refs_6_.refs_4_, bf16[1,512,128]{2,1,0:T(8,128)(2,1)S(1)} %collective-permute-done.1.refs_5_.refs_3_, bf16[1,512,128]{2,1,0:T(8,128)(2,1)S(1)} %collective-permute-done.refs_4_.refs_2_, bf16[1,512,128]{2,1,0:T(8,128)(2,1)S(1)} %copy-done.3), kind=kLoop, calls=%fused_computation | loop fusion | flops 786432 | bytes 1048576 | tf_op jit(solution)/shard_map/concatenate | solution.py:394
  26.6 1.9 %collective-permute-done.4.refs_2_ = bf16[8,256,128]{2,1,0:T(8,128)(2,1)S(1)} collective-permute-done((bf16[8,256,128]{2,1,0:T(8,128)(2,1)}, bf16[8,256,128]{2,1,0:T(8,128)(2,1)S(1)}, u32[]{:S(2)}, u32[]{:S(2)}) %collective-permute-start.4) | collective-permute-done | bytes 524320 | tf_op jit(solution)/shard_map/ppermute | solution.py:307
  28.5 0.4 collective-permute-start.7
  28.9 1.7 %collective-permute-start.16 = (bf16[8,256,128]{2,1,0:T(8,128)(2,1)}, bf16[8,256,128]{2,1,0:T(8,128)(2,1)}, u32[]{:S(2)}, u32[]{:S(2)}) collective-permute-start(bf16[8,256,128]{2,1,0:T(8,128)(2,1)} %collective-permute-done.5.refs_6_), channel_id=1, source_target_pairs={{0,4},{1,5},{2,6},{3,7},{4,0},{5,1},{6,2},{7,3},{8,12},{9,13},{10,... | collective-permute-start | bytes 1572872 | tf_op jit(solution)/shard_map/ppermute | solution.py:307
  30.6 3.6 %collective-permute-start.11 = (bf16[1,512,128]{2,1,0:T(8,128)(2,1)S(1)}, bf16[1,512,128]{2,1,0:T(8,128)(2,1)S(1)}, u32[]{:S(2)}, u32[]{:S(2)}) collective-permute-start(bf16[1,512,128]{2,1,0:T(8,128)(2,1)S(1)} %copy-done.11), channel_id=1, source_target_pairs={{0,24},{8,0},{16,8},{24,16},{1,25},{9,1},{17,9},{25,17},{2,26},{10... | collective-permute-start | bytes 393224 | tf_op jit(solution)/shard_map/ppermute | solution.py:351
  34.2 0.1 pad_add_fusion.pos_ref
  34.3 1.2 %copy.13 = bf16[2048,128]{0,1:T(8,128)(2,1)S(1)} copy(bf16[2048,128]{1,0:T(8,128)(2,1)} %param.21) | data formatting | bytes 1048576 | tf_op jit(solution)/shard_map/optimization_barrier | solution.py:377
  35.6 2.2 %copy-done = bf16[8,1,2048,128]{3,2,1,0:T(8,128)(2,1)S(1)} copy-done((bf16[8,1,2048,128]{3,2,1,0:T(8,128)(2,1)S(1)}, bf16[8,1,2048,128]{3,2,1,0:T(8,128)(2,1)}, u32[]{:S(2)}) %copy-start) | copy-done | bytes 4194328
  37.8 1.8 %sketch_products.1.vproj_ref = bf16[8,128,128]{2,1,0:T(8,128)(2,1)S(1)} custom-call(s32[8]{0:T(128)S(1)} %bitcast.19, bf16[128,2048]{1,0:T(8,128)(2,1)S(1)} %bitcast.17, bf16[8,2048,128]{2,1,0:T(8,128)(2,1)S(1)} %bitcast.14), custom_call_target="tpu_custom_call" | custom-call | flops 536870912 | bytes 4194304 | tf_op jit(solution)/shard_map/sketch_products/pallas_call | solution.py:379
  39.6 0.1 collective-permute-start.13
  39.7 1.2 %core_products.2 = (f32[8,128,128]{2,1,0:T(8,128)S(1)}, f32[8,128,128]{2,1,0:T(8,128)S(1)}) custom-call(s32[2]{0:T(128)S(1)} %pad_add_fusion.pos_ref, bf16[8,256,128]{2,1,0:T(8,128)(2,1)S(1)} %copy-done.4, bf16[8,256,128]{2,1,0:T(8,128)(2,1)S(1)} %copy-done.6, bf16[8,256,128]{2,1,0:T(8,128)(2,1)S(1)} %collective-permute-done.4.refs_2_, ...), custom_call_target="tpu_custom_call" | custom-call | flops 402653184 | bytes 1572864 | tf_op jit(solution)/shard_map/core_products/pallas_call | solution.py:400
  40.9 0.5 collective-permute-start.14
  41.5 0.1 collective-permute-start.15
  41.6 1.4 %core_products.3 = (f32[8,128,128]{2,1,0:T(8,128)S(1)}, f32[8,128,128]{2,1,0:T(8,128)S(1)}) custom-call(s32[2]{0:T(128)S(1)} %pad_add_fusion.pos_ref, bf16[8,256,128]{2,1,0:T(8,128)(2,1)} %collective-permute-done.7.refs_0_, bf16[1,512,128]{2,1,0:T(8,128)(2,1)S(1)} %copy-done.3, bf16[1,512,128]{2,1,0:T(8,128)(2,1)S(1)} %collective-permute-done.refs_4_.refs_2_, ...), custom_call_target="tpu_custom_call" | custom-call | flops 134217728 | bytes 524288 | tf_op jit(solution)/shard_map/core_products/pallas_call | solution.py:400
  43.0 0.5 collective-permute-start.12
  43.5 0.1 collective-permute-start.17
  44.3 0.8 %collective-permute-done.12.other_ref = f32[8,128,128]{2,1,0:T(8,128)S(1)} collective-permute-done((f32[8,128,128]{2,1,0:T(8,128)S(1)}, f32[8,128,128]{2,1,0:T(8,128)S(1)}, u32[]{:S(2)}, u32[]{:S(2)}) %collective-permute-start.12) | collective-permute-done | bytes 524320 | tf_op jit(solution)/shard_map/ppermute | solution.py:307
  45.0 1.0 %collective-permute-done.17.refs_11_ = bf16[8,256,128]{2,1,0:T(8,128)(2,1)S(1)} collective-permute-done((bf16[8,256,128]{2,1,0:T(8,128)(2,1)}, bf16[8,256,128]{2,1,0:T(8,128)(2,1)S(1)}, u32[]{:S(2)}, u32[]{:S(2)}) %collective-permute-start.17) | collective-permute-done | bytes 524320 | tf_op jit(solution)/shard_map/ppermute | solution.py:307
  46.0 17.7 %recompress_store.1 = (bf16[8,2048,128]{2,1,0:T(8,128)(2,1)}, bf16[8,2048,128]{2,1,0:T(8,128)(2,1)}) custom-call(s32[2]{0:T(128)S(1)} %pad_add_fusion.pos_ref, s32[8]{0:T(128)S(1)} %bitcast.20, s32[8]{0:T(128)S(1)} %bitcast.21, s32[8]{0:T(128)S(1)} %copy-done.13, s32[1]{0:T(128)S(6)} %copy.16.col_rank_ref, bf16[8,2048,128]{2,1,0:T(8,128)(2,1)S(1)} %bitcast.16, ...), custom_call_target="tpu_custom_call" | custom-call | flops 4294967296 | bytes 20971520 | tf_op jit(solution)/shard_map/recompress_store/pallas_call | solution.py:423
  (40 shorter events, 0.1 us)
Async XLA Ops:
  0.6 34.9 %copy-start.7 = (s32[8,1]{0,1:T(1,128)S(1)}, s32[8,1]{0,1:T(1,128)}, u32[]{:S(2)}) copy-start(s32[8,1]{0,1:T(1,128)} %param.13) | copy-start | bytes 100
  0.6 18.3 %collective-permute-start.2 = (bf16[8,256,128]{2,1,0:T(8,128)(2,1)}, bf16[8,256,128]{2,1,0:T(8,128)(2,1)S(1)}, u32[]{:S(2)}, u32[]{:S(2)}) collective-permute-start(bf16[8,256,128]{2,1,0:T(8,128)(2,1)} %refs_0_), channel_id=1, source_target_pairs={{0,2},{1,3},{2,0},{3,1},{4,6},{5,7},{6,4},{7,5},{8,10},{9,11},{10,... | collective-permute-start | bytes 1572872 | tf_op jit(solution)/shard_map/ppermute | solution.py:307
  3.6 15.3 %collective-permute-start.3 = (bf16[8,256,128]{2,1,0:T(8,128)(2,1)}, bf16[8,256,128]{2,1,0:T(8,128)(2,1)S(1)}, u32[]{:S(2)}, u32[]{:S(2)}) collective-permute-start(bf16[8,256,128]{2,1,0:T(8,128)(2,1)} %refs_4_.1), channel_id=1, source_target_pairs={{0,4},{1,5},{2,6},{3,7},{4,0},{5,1},{6,2},{7,3},{8,12},{9,13},{10,... | collective-permute-start | bytes 1572872 | tf_op jit(solution)/shard_map/ppermute | solution.py:307
  5.2 7.0 %collective-permute-start = (bf16[1,512,128]{2,1,0:T(8,128)(2,1)}, bf16[1,512,128]{2,1,0:T(8,128)(2,1)S(1)}, u32[]{:S(2)}, u32[]{:S(2)}) collective-permute-start(bf16[1,512,128]{2,1,0:T(8,128)(2,1)} %refs_1_.1), channel_id=1, source_target_pairs={{0,8},{8,16},{16,24},{24,0},{1,9},{9,17},{17,25},{25,1},{2,10},{10... | collective-permute-start | bytes 393224 | tf_op jit(solution)/shard_map/ppermute | solution.py:351
  6.7 21.7 %collective-permute-start.4 = (bf16[8,256,128]{2,1,0:T(8,128)(2,1)}, bf16[8,256,128]{2,1,0:T(8,128)(2,1)S(1)}, u32[]{:S(2)}, u32[]{:S(2)}) collective-permute-start(bf16[8,256,128]{2,1,0:T(8,128)(2,1)} %refs_0_), channel_id=1, source_target_pairs={{0,4},{1,5},{2,6},{3,7},{4,0},{5,1},{6,2},{7,3},{8,12},{9,13},{10,... | collective-permute-start | bytes 1572872 | tf_op jit(solution)/shard_map/ppermute | solution.py:307
  7.2 21.2 %collective-permute-start.5 = (bf16[8,256,128]{2,1,0:T(8,128)(2,1)}, bf16[8,256,128]{2,1,0:T(8,128)(2,1)}, u32[]{:S(2)}, u32[]{:S(2)}) collective-permute-start(bf16[8,256,128]{2,1,0:T(8,128)(2,1)} %refs_4_.1), channel_id=1, source_target_pairs={{0,2},{1,3},{2,0},{3,1},{4,6},{5,7},{6,4},{7,5},{8,10},{9,11},{10,... | collective-permute-start | bytes 1572872 | tf_op jit(solution)/shard_map/ppermute | solution.py:307
  12.1 6.8 %collective-permute-start.1 = (bf16[1,512,128]{2,1,0:T(8,128)(2,1)S(1)}, bf16[1,512,128]{2,1,0:T(8,128)(2,1)S(1)}, u32[]{:S(2)}, u32[]{:S(2)}) collective-permute-start(bf16[1,512,128]{2,1,0:T(8,128)(2,1)S(1)} %collective-permute-done.refs_4_.refs_2_), channel_id=1, source_target_pairs={{0,8},{8,16},{16,24},{24,0},{1,9},{9,17},{17,25},{25,1},{2,10},{10... | collective-permute-start | bytes 393224 | tf_op jit(solution)/shard_map/ppermute | solution.py:351
  12.1 2.2 %copy-start.1 = (bf16[8,1,2048,128]{3,2,1,0:T(8,128)(2,1)S(1)}, bf16[8,1,2048,128]{3,2,1,0:T(8,128)(2,1)}, u32[]{:S(2)}) copy-start(bf16[8,1,2048,128]{3,2,1,0:T(8,128)(2,1)} %param.11) | copy-start | bytes 12582916
  14.3 6.0 %copy-start.11 = (bf16[1,512,128]{2,1,0:T(8,128)(2,1)S(1)}, bf16[1,512,128]{2,1,0:T(8,128)(2,1)}, u32[]{:S(2)}) copy-start(bf16[1,512,128]{2,1,0:T(8,128)(2,1)} %refs_0_.1) | copy-start | bytes 393220
  14.3 11.4 %copy-start.3 = (bf16[1,512,128]{2,1,0:T(8,128)(2,1)S(1)}, bf16[1,512,128]{2,1,0:T(8,128)(2,1)}, u32[]{:S(2)}) copy-start(bf16[1,512,128]{2,1,0:T(8,128)(2,1)} %refs_1_.1) | copy-start | bytes 393220
  15.6 24.1 %copy-start.4 = (bf16[8,256,128]{2,1,0:T(8,128)(2,1)S(1)}, bf16[8,256,128]{2,1,0:T(8,128)(2,1)}, u32[]{:S(2)}) copy-start(bf16[8,256,128]{2,1,0:T(8,128)(2,1)} %refs_0_) | copy-start | bytes 1572868
  18.9 9.6 %copy-start.5 = (bf16[8,256,128]{2,1,0:T(8,128)(2,1)}, bf16[8,256,128]{2,1,0:T(8,128)(2,1)S(1)}, u32[]{:S(2)}) copy-start(bf16[8,256,128]{2,1,0:T(8,128)(2,1)S(1)} %collective-permute-done.2.refs_1_) | copy-start | bytes 1572868
  18.9 9.6 %copy-start.9 = (bf16[8,256,128]{2,1,0:T(8,128)(2,1)}, bf16[8,256,128]{2,1,0:T(8,128)(2,1)S(1)}, u32[]{:S(2)}) copy-start(bf16[8,256,128]{2,1,0:T(8,128)(2,1)S(1)} %collective-permute-done.3.refs_8_) | copy-start | bytes 1572868
  18.9 6.8 %collective-permute-start.8 = (bf16[1,512,128]{2,1,0:T(8,128)(2,1)S(1)}, bf16[1,512,128]{2,1,0:T(8,128)(2,1)S(1)}, u32[]{:S(2)}, u32[]{:S(2)}) collective-permute-start(bf16[1,512,128]{2,1,0:T(8,128)(2,1)S(1)} %collective-permute-done.1.refs_5_.refs_3_), channel_id=1, source_target_pairs={{0,8},{8,16},{16,24},{24,0},{1,9},{9,17},{17,25},{25,1},{2,10},{10... | collective-permute-start | bytes 393224 | tf_op jit(solution)/shard_map/ppermute | solution.py:351
  20.3 8.2 %collective-permute-start.6 = (bf16[1,512,128]{2,1,0:T(8,128)(2,1)S(1)}, bf16[1,512,128]{2,1,0:T(8,128)(2,1)S(1)}, u32[]{:S(2)}, u32[]{:S(2)}) collective-permute-start(bf16[1,512,128]{2,1,0:T(8,128)(2,1)S(1)} %copy-done.11), channel_id=1, source_target_pairs={{0,8},{8,16},{16,24},{24,0},{1,9},{9,17},{17,25},{25,1},{2,10},{10... | collective-permute-start | bytes 393224 | tf_op jit(solution)/shard_map/ppermute | solution.py:351
  26.6 13.0 %collective-permute-start.9 = (bf16[4,512,128]{2,1,0:T(8,128)(2,1)}, bf16[4,512,128]{2,1,0:T(8,128)(2,1)S(1)}, u32[]{:S(2)}, u32[]{:S(2)}) collective-permute-start(bf16[4,512,128]{2,1,0:T(8,128)(2,1)} %pad_maximum_fusion), channel_id=1, source_target_pairs={{0,1},{1,0},{2,3},{3,2},{4,5},{5,4},{6,7},{7,6},{8,9},{9,8},{10,11... | collective-permute-start | bytes 1572872 | tf_op jit(solution)/shard_map/ppermute | solution.py:307
  28.5 13.1 %collective-permute-start.7 = (bf16[8,256,128]{2,1,0:T(8,128)(2,1)S(1)}, bf16[8,256,128]{2,1,0:T(8,128)(2,1)}, u32[]{:S(2)}, u32[]{:S(2)}) collective-permute-start(bf16[8,256,128]{2,1,0:T(8,128)(2,1)S(1)} %collective-permute-done.4.refs_2_), channel_id=1, source_target_pairs={{0,2},{1,3},{2,0},{3,1},{4,6},{5,7},{6,4},{7,5},{8,10},{9,11},{10,... | collective-permute-start | bytes 1572872 | tf_op jit(solution)/shard_map/ppermute | solution.py:307
  28.9 14.6 %collective-permute-start.16 = (bf16[8,256,128]{2,1,0:T(8,128)(2,1)}, bf16[8,256,128]{2,1,0:T(8,128)(2,1)}, u32[]{:S(2)}, u32[]{:S(2)}) collective-permute-start(bf16[8,256,128]{2,1,0:T(8,128)(2,1)} %collective-permute-done.5.refs_6_), channel_id=1, source_target_pairs={{0,4},{1,5},{2,6},{3,7},{4,0},{5,1},{6,2},{7,3},{8,12},{9,13},{10,... | collective-permute-start | bytes 1572872 | tf_op jit(solution)/shard_map/ppermute | solution.py:307
  30.6 10.3 %collective-permute-start.11 = (bf16[1,512,128]{2,1,0:T(8,128)(2,1)S(1)}, bf16[1,512,128]{2,1,0:T(8,128)(2,1)S(1)}, u32[]{:S(2)}, u32[]{:S(2)}) collective-permute-start(bf16[1,512,128]{2,1,0:T(8,128)(2,1)S(1)} %copy-done.11), channel_id=1, source_target_pairs={{0,24},{8,0},{16,8},{24,16},{1,25},{9,1},{17,9},{25,17},{2,26},{10... | collective-permute-start | bytes 393224 | tf_op jit(solution)/shard_map/ppermute | solution.py:351
  34.2 7.3 %collective-permute-start.10 = (bf16[1,512,128]{2,1,0:T(8,128)(2,1)S(1)}, bf16[1,512,128]{2,1,0:T(8,128)(2,1)}, u32[]{:S(2)}, u32[]{:S(2)}) collective-permute-start(bf16[1,512,128]{2,1,0:T(8,128)(2,1)S(1)} %collective-permute-done.6.refs_1_), channel_id=1, source_target_pairs={{0,8},{8,16},{16,24},{24,0},{1,9},{9,17},{17,25},{25,1},{2,10},{10... | collective-permute-start | bytes 393224 | tf_op jit(solution)/shard_map/ppermute | solution.py:351
  35.6 2.2 %copy-start = (bf16[8,1,2048,128]{3,2,1,0:T(8,128)(2,1)S(1)}, bf16[8,1,2048,128]{3,2,1,0:T(8,128)(2,1)}, u32[]{:S(2)}) copy-start(bf16[8,1,2048,128]{3,2,1,0:T(8,128)(2,1)} %param.12) | copy-start | bytes 12582916
  37.8 2.0 %copy-start.6 = (bf16[8,256,128]{2,1,0:T(8,128)(2,1)S(1)}, bf16[8,256,128]{2,1,0:T(8,128)(2,1)}, u32[]{:S(2)}) copy-start(bf16[8,256,128]{2,1,0:T(8,128)(2,1)} %copy-done.5) | copy-start | bytes 1572868
  37.8 3.7 %copy-start.10 = (bf16[8,256,128]{2,1,0:T(8,128)(2,1)S(1)}, bf16[8,256,128]{2,1,0:T(8,128)(2,1)}, u32[]{:S(2)}) copy-start(bf16[8,256,128]{2,1,0:T(8,128)(2,1)} %copy-done.9) | copy-start | bytes 1572868
  37.8 8.2 %copy-start.2 = (bf16[8,1,2048,128]{3,2,1,0:T(8,128)(2,1)S(1)}, bf16[8,1,2048,128]{3,2,1,0:T(8,128)(2,1)}, u32[]{:S(2)}) copy-start(bf16[8,1,2048,128]{3,2,1,0:T(8,128)(2,1)} %param.11) | copy-start | bytes 12582916
  37.8 8.2 %copy-start.8 = (bf16[8,256,128]{2,1,0:T(8,128)(2,1)S(1)}, bf16[8,256,128]{2,1,0:T(8,128)(2,1)}, u32[]{:S(2)}) copy-start(bf16[8,256,128]{2,1,0:T(8,128)(2,1)} %refs_4_.1) | copy-start | bytes 1572868
  37.8 8.2 %copy-start.12 = (s32[8,1]{0,1:T(1,128)S(1)}, s32[8,1]{0,1:T(1,128)}, u32[]{:S(2)}) copy-start(s32[8,1]{0,1:T(1,128)} %param.14) | copy-start | bytes 100
  37.8 8.2 %copy-start.13 = (s32[8]{0:T(128)S(1)}, s32[8]{0:T(128)}, u32[]{:S(2)}) copy-start(s32[8]{0:T(128)} %row_rank_ref.1) | copy-start | bytes 100
  39.6 4.6 %collective-permute-start.13 = (bf16[8,256,128]{2,1,0:T(8,128)(2,1)}, bf16[8,256,128]{2,1,0:T(8,128)(2,1)S(1)}, u32[]{:S(2)}, u32[]{:S(2)}) collective-permute-start(bf16[8,256,128]{2,1,0:T(8,128)(2,1)} %refs_4_.1), channel_id=1, source_target_pairs={{0,1},{1,0},{2,3},{3,2},{4,5},{5,4},{6,7},{7,6},{8,9},{9,8},{10,11... | collective-permute-start | bytes 1572872 | tf_op jit(solution)/shard_map/ppermute | solution.py:307
  40.9 3.3 %collective-permute-start.14 = (bf16[8,256,128]{2,1,0:T(8,128)(2,1)}, bf16[8,256,128]{2,1,0:T(8,128)(2,1)S(1)}, u32[]{:S(2)}, u32[]{:S(2)}) collective-permute-start(bf16[8,256,128]{2,1,0:T(8,128)(2,1)} %collective-permute-done.5.refs_6_), channel_id=1, source_target_pairs={{0,1},{1,0},{2,3},{3,2},{4,5},{5,4},{6,7},{7,6},{8,9},{9,8},{10,11... | collective-permute-start | bytes 1572872 | tf_op jit(solution)/shard_map/ppermute | solution.py:307
  41.5 2.8 %collective-permute-start.15 = (bf16[8,256,128]{2,1,0:T(8,128)(2,1)S(1)}, bf16[8,256,128]{2,1,0:T(8,128)(2,1)S(1)}, u32[]{:S(2)}, u32[]{:S(2)}) collective-permute-start(bf16[8,256,128]{2,1,0:T(8,128)(2,1)S(1)} %copy-done.10), channel_id=1, source_target_pairs={{0,1},{1,0},{2,3},{3,2},{4,5},{5,4},{6,7},{7,6},{8,9},{9,8},{10,11... | collective-permute-start | bytes 1572872 | tf_op jit(solution)/shard_map/ppermute | solution.py:307
  43.0 2.0 %collective-permute-start.12 = (f32[8,128,128]{2,1,0:T(8,128)S(1)}, f32[8,128,128]{2,1,0:T(8,128)S(1)}, u32[]{:S(2)}, u32[]{:S(2)}) collective-permute-start(f32[8,128,128]{2,1,0:T(8,128)S(1)} %get-tuple-element.46), channel_id=1, source_target_pairs={{0,1},{1,0},{2,3},{3,2},{4,5},{5,4},{6,7},{7,6},{8,9},{9,8},{10,11... | collective-permute-start | bytes 1572872 | tf_op jit(solution)/shard_map/ppermute | solution.py:307
  43.5 2.5 %collective-permute-start.17 = (bf16[8,256,128]{2,1,0:T(8,128)(2,1)}, bf16[8,256,128]{2,1,0:T(8,128)(2,1)S(1)}, u32[]{:S(2)}, u32[]{:S(2)}) collective-permute-start(bf16[8,256,128]{2,1,0:T(8,128)(2,1)} %collective-permute-done.16.refs_10_), channel_id=1, source_target_pairs={{0,1},{1,0},{2,3},{3,2},{4,5},{5,4},{6,7},{7,6},{8,9},{9,8},{10,11... | collective-permute-start | bytes 1572872 | tf_op jit(solution)/shard_map/ppermute | solution.py:307

commit v4 on v3

--- a/solution.py
+++ b/solution.py
@@ -45,11 +45,11 @@
         proj_ref[t] = jnp.where(keep, proj, 0.0).astype(BF16)
 
 
-def core_kernel(pos_ref, *refs, masks, pieces, more):
+def core_kernel(pos_ref, *refs, masks, pieces, more, outs):
     q_refs, refs = refs[: len(masks)], refs[len(masks) :]
     mine_refs, refs = refs[:pieces], refs[pieces:]
     other_ref, refs = refs[0], refs[1:]
-    before, (own_out, other_out) = refs[:-2], refs[-2:]
+    before, out_refs = refs[: -len(outs)], refs[-len(outs) :]
     count, chunk, width = q_refs[0].shape
     depth = other_ref.shape[1]
     sides = []
@@ -61,6 +61,7 @@
         for k in range(1, pieces):
             mine = jnp.where(piece == k, mine_refs[k][0, pl.ds(inner, chunk), :], mine)
         both = [mine, other_ref[piece, pl.ds(inner, chunk), :]]
+        both = [both[k] for k in outs]
         sides.append(jnp.concatenate(both, axis=1).astype(F32).T.astype(BF16))
     for t in range(0, count, 2):
         total = None
@@ -70,11 +71,9 @@
             total = part if total is None else total + part
         for k in range(2):
             block = total[:, k * width : (k + 1) * width]
-            own, other = block[:width], block[width:]
-            if more:
-                own, other = own + before[0][t + k], other + before[1][t + k]
-            own_out[t + k] = own
-            other_out[t + k] = other
+            for n, out_ref in enumerate(out_refs):
+                share = block[n * width : (n + 1) * width]
+                out_ref[t + k] = share + before[n][t + k] if more else share
 
 
 def final_kernel(
@@ -396,12 +395,14 @@
     masks = tuple(range(0, n_col, 2))
     part_shape = jax.ShapeDtypeStruct((count, width, width), F32)
 
-    def cores(use, before):
+    def cores(use, before, outs=(0, 1)):
         return pl.pallas_call(
-            functools.partial(core_kernel, masks=use, pieces=n_row, more=len(before) > 0),
+            functools.partial(
+                core_kernel, masks=use, pieces=n_row, more=len(before) > 0, outs=outs
+            ),
             in_specs=[SMEM] + [VMEM] * (len(use) + n_row + 1 + len(before)),
-            out_specs=[VMEM, VMEM],
-            out_shape=[part_shape, part_shape],
+            out_specs=[VMEM] * len(outs),
+            out_shape=[part_shape] * len(outs),
             compiler_params=pltpu.CompilerParams(vmem_limit_bytes=16 * MIB),
             cost_estimate=pl.CostEstimate(
                 flops=4 * len(use) * count * chunk * width * width,
@@ -413,8 +414,9 @@
 
     parts = cores(masks[:-1], []) if len(masks) > 1 else []
     parts, x, vproj = tie((parts, x, vproj))
-    core_own, core_other = cores(masks[-1:], parts)
+    (core_other,) = cores(masks[-1:], parts[1:], (1,))
     core_got = col_swap(core_other, 1)
+    (core_own,) = cores(masks[-1:], parts[:1], (0,))
 
     panels = [row_u, own_mate]
     for m in masks[1:]:

time: 64.2 us -> 64.3 us (level)
  Pallas kernels: 23.4 us -> 24.3 us
  starting transfers between devices: 17.1 us -> 16.2 us
  local copies, waits for them, and re-layouts: 5.67 us -> 6.46 us
  waiting for transfers between devices: 15.1 us -> 14.4 us
    ppermute x12, waiting for transfers between devices: 3.6 us -> 2.16 us  [swap(): return lax.ppermute(x, axis, [(c, c ^ mask) for c in range(size)])]
    pallas_call x2 -> x3, Pallas kernels: 2.6 us -> 3.52 us  [cores(): pl.pallas_call(functools.partial(core_kernel, masks=use, pieces=n_row, mo...]
    unnamed x28, local copies, waits for them, and re-layouts: 4.42 us -> 5.22 us
    ppermute x6, starting transfers between devices: 8.11 us -> 7.33 us  [shift(): lax.ppermute(v, 'row', [(c, (c + step) % n_row) for c in range(n_row)])]
    ppermute x6, waiting for transfers between devices: 11.5 us -> 12.2 us  [shift(): lax.ppermute(v, 'row', [(c, (c + step) % n_row) for c in range(n_row)])]
  transfers between devices with their start and end apart: 18 -> 18, of which waited for: 6 -> 5; matrix products, arithmetic and copies ran while one was open for 3% -> 3% of each run, Pallas kernels for 9% -> 10%
where the time goes in v4:
time: 64.3 us; the launch traced here: 64 us
  Pallas kernels  24.3 us (38%)
  starting transfers between devices  16.2 us (25%)
  waiting for transfers between devices  14.4 us (22%)
  local copies, waits for them, and re-layouts  6.46 us (10%)
  between operations  1.65 us (3%)
  other arithmetic  0.94 us (1%)
    pallas_call x1, Pallas kernels, on_device(): pl.pallas_call(functools.partial(final_kernel, masks=masks, block=32, pie...  17.7 us
    ppermute x6, waiting for transfers between devices, shift(): lax.ppermute(v, 'row', [(c, (c + step) % n_row) for c in range(n_row)])  12.2 us
    ppermute x12, starting transfers between devices, swap(): return lax.ppermute(x, axis, [(c, c ^ mask) for c in range(size)])  8.91 us
    ppermute x6, starting transfers between devices, shift(): lax.ppermute(v, 'row', [(c, (c + step) % n_row) for c in range(n_row)])  7.33 us
    unnamed x28, local copies, waits for them, and re-layouts  5.22 us
    pallas_call x3, Pallas kernels, cores(): pl.pallas_call(functools.partial(core_kernel, masks=use, pieces=n_row, mo...  3.52 us
    ppermute x12, waiting for transfers between devices, swap(): return lax.ppermute(x, axis, [(c, c ^ mask) for c in range(size)])  2.16 us
    pallas_call x1, Pallas kernels, on_device(): pl.pallas_call(proj_kernel, in_specs=[SMEM, VMEM, VMEM], out_specs=VMEM,...  1.84 us
  transfers between devices with their start and end apart: 18, of which 5 were waited for; matrix products, arithmetic and copies ran while one was open for 3% of the time, Pallas kernels for 10%

profile of v4, /device:TPU:0, one launch (start us, length us, event | category | flops | bytes accessed | tf_op | source)
XLA Modules:
  0.0 64.0 jit_solution(8763665982382995166)
XLA Ops:
  0.6 3.0 %collective-permute-start.2 = (bf16[8,256,128]{2,1,0:T(8,128)(2,1)}, bf16[8,256,128]{2,1,0:T(8,128)(2,1)S(1)}, u32[]{:S(2)}, u32[]{:S(2)}) collective-permute-start(bf16[8,256,128]{2,1,0:T(8,128)(2,1)} %refs_0_), channel_id=1, source_target_pairs={{0,2},{1,3},{2,0},{3,1},{4,6},{5,7},{6,4},{7,5},{8,10},{9,11},{10,... | collective-permute-start | bytes 1572872 | tf_op jit(solution)/shard_map/ppermute | solution.py:306
  3.6 1.5 %collective-permute-start.3 = (bf16[8,256,128]{2,1,0:T(8,128)(2,1)}, bf16[8,256,128]{2,1,0:T(8,128)(2,1)S(1)}, u32[]{:S(2)}, u32[]{:S(2)}) collective-permute-start(bf16[8,256,128]{2,1,0:T(8,128)(2,1)} %refs_4_.1), channel_id=1, source_target_pairs={{0,4},{1,5},{2,6},{3,7},{4,0},{5,1},{6,2},{7,3},{8,12},{9,13},{10,... | collective-permute-start | bytes 1572872 | tf_op jit(solution)/shard_map/ppermute | solution.py:306
  5.2 1.6 %collective-permute-start = (bf16[1,512,128]{2,1,0:T(8,128)(2,1)}, bf16[1,512,128]{2,1,0:T(8,128)(2,1)S(1)}, u32[]{:S(2)}, u32[]{:S(2)}) collective-permute-start(bf16[1,512,128]{2,1,0:T(8,128)(2,1)} %refs_1_.3), channel_id=1, source_target_pairs={{0,8},{8,16},{16,24},{24,0},{1,9},{9,17},{17,25},{25,1},{2,10},{10... | collective-permute-start | bytes 393224 | tf_op jit(solution)/shard_map/ppermute | solution.py:350
  6.7 0.5 collective-permute-start.4
  7.2 0.5 collective-permute-start.5
  7.8 4.4 %collective-permute-done.refs_4_.refs_2_ = bf16[1,512,128]{2,1,0:T(8,128)(2,1)S(1)} collective-permute-done((bf16[1,512,128]{2,1,0:T(8,128)(2,1)}, bf16[1,512,128]{2,1,0:T(8,128)(2,1)S(1)}, u32[]{:S(2)}, u32[]{:S(2)}) %collective-permute-start) | collective-permute-done | bytes 131104 | tf_op jit(solution)/shard_map/ppermute | solution.py:350
  12.1 2.2 %copy-done.1 = bf16[8,1,2048,128]{3,2,1,0:T(8,128)(2,1)S(1)} copy-done((bf16[8,1,2048,128]{3,2,1,0:T(8,128)(2,1)S(1)}, bf16[8,1,2048,128]{3,2,1,0:T(8,128)(2,1)}, u32[]{:S(2)}) %copy-start.1) | copy-done | bytes 4194328
  14.3 1.3 %gram_products.1.uu_ref = f32[8,128,128]{2,1,0:T(8,128)S(1)} custom-call(bf16[8,2048,128]{2,1,0:T(8,128)(2,1)S(1)} %bitcast.15), custom_call_target="tpu_custom_call" | custom-call | flops 536870912 | bytes 4194304 | tf_op jit(solution)/shard_map/gram_products/pallas_call | solution.py:362
  15.6 3.3 %collective-permute-done.1.refs_5_.refs_3_ = bf16[1,512,128]{2,1,0:T(8,128)(2,1)S(1)} collective-permute-done((bf16[1,512,128]{2,1,0:T(8,128)(2,1)S(1)}, bf16[1,512,128]{2,1,0:T(8,128)(2,1)S(1)}, u32[]{:S(2)}, u32[]{:S(2)}) %collective-permute-start.1) | collective-permute-done | bytes 131104 | tf_op jit(solution)/shard_map/ppermute | solution.py:350
  18.9 0.8 %copy-done.5 = bf16[8,256,128]{2,1,0:T(8,128)(2,1)} copy-done((bf16[8,256,128]{2,1,0:T(8,128)(2,1)}, bf16[8,256,128]{2,1,0:T(8,128)(2,1)S(1)}, u32[]{:S(2)}) %copy-start.5) | copy-done | bytes 524312
  19.7 0.6 collective-permute-start.8
  20.3 1.6 %collective-permute-start.6 = (bf16[1,512,128]{2,1,0:T(8,128)(2,1)S(1)}, bf16[1,512,128]{2,1,0:T(8,128)(2,1)S(1)}, u32[]{:S(2)}, u32[]{:S(2)}) collective-permute-start(bf16[1,512,128]{2,1,0:T(8,128)(2,1)S(1)} %copy-done.11), channel_id=1, source_target_pairs={{0,8},{8,16},{16,24},{24,0},{1,9},{9,17},{17,25},{25,1},{2,10},{10... | collective-permute-start | bytes 393224 | tf_op jit(solution)/shard_map/ppermute | solution.py:350
  21.9 4.6 %collective-permute-done.8.refs_6_.refs_4_ = bf16[1,512,128]{2,1,0:T(8,128)(2,1)S(1)} collective-permute-done((bf16[1,512,128]{2,1,0:T(8,128)(2,1)S(1)}, bf16[1,512,128]{2,1,0:T(8,128)(2,1)S(1)}, u32[]{:S(2)}, u32[]{:S(2)}) %collective-permute-start.8) | collective-permute-done | bytes 131104 | tf_op jit(solution)/shard_map/ppermute | solution.py:350
  26.5 0.9 %pad_maximum_fusion = bf16[4,512,128]{2,1,0:T(8,128)(2,1)} fusion(bf16[1,512,128]{2,1,0:T(8,128)(2,1)S(1)} %collective-permute-done.8.refs_6_.refs_4_, bf16[1,512,128]{2,1,0:T(8,128)(2,1)S(1)} %collective-permute-done.1.refs_5_.refs_3_, bf16[1,512,128]{2,1,0:T(8,128)(2,1)S(1)} %collective-permute-done.refs_4_.refs_2_, bf16[1,512,128]{2,1,0:T(8,128)(2,1)S(1)} %copy-done.3), kind=kLoop, calls=%fused_computation | loop fusion | flops 786432 | bytes 1048576 | tf_op jit(solution)/shard_map/concatenate | solution.py:393
  27.3 1.2 %collective-permute-done.4.refs_2_ = bf16[8,256,128]{2,1,0:T(8,128)(2,1)} collective-permute-done((bf16[8,256,128]{2,1,0:T(8,128)(2,1)}, bf16[8,256,128]{2,1,0:T(8,128)(2,1)}, u32[]{:S(2)}, u32[]{:S(2)}) %collective-permute-start.4) | collective-permute-done | bytes 524320 | tf_op jit(solution)/shard_map/ppermute | solution.py:306
  28.6 0.4 collective-permute-start.7
  29.0 1.7 %collective-permute-start.16 = (bf16[8,256,128]{2,1,0:T(8,128)(2,1)}, bf16[8,256,128]{2,1,0:T(8,128)(2,1)}, u32[]{:S(2)}, u32[]{:S(2)}) collective-permute-start(bf16[8,256,128]{2,1,0:T(8,128)(2,1)} %collective-permute-done.5.refs_6_), channel_id=1, source_target_pairs={{0,4},{1,5},{2,6},{3,7},{4,0},{5,1},{6,2},{7,3},{8,12},{9,13},{10,... | collective-permute-start | bytes 1572872 | tf_op jit(solution)/shard_map/ppermute | solution.py:306
  30.7 3.6 %collective-permute-start.11 = (bf16[1,512,128]{2,1,0:T(8,128)(2,1)S(1)}, bf16[1,512,128]{2,1,0:T(8,128)(2,1)S(1)}, u32[]{:S(2)}, u32[]{:S(2)}) collective-permute-start(bf16[1,512,128]{2,1,0:T(8,128)(2,1)S(1)} %copy-done.11), channel_id=1, source_target_pairs={{0,24},{8,0},{16,8},{24,16},{1,25},{9,1},{17,9},{25,17},{2,26},{10... | collective-permute-start | bytes 393224 | tf_op jit(solution)/shard_map/ppermute | solution.py:350
  34.3 0.1 pad_add_fusion.pos_ref
  34.4 1.2 %copy.13 = bf16[2048,128]{0,1:T(8,128)(2,1)S(1)} copy(bf16[2048,128]{1,0:T(8,128)(2,1)} %param.21) | data formatting | bytes 1048576 | tf_op jit(solution)/shard_map/optimization_barrier | solution.py:376
  35.7 2.2 %copy-done = bf16[8,1,2048,128]{3,2,1,0:T(8,128)(2,1)S(1)} copy-done((bf16[8,1,2048,128]{3,2,1,0:T(8,128)(2,1)S(1)}, bf16[8,1,2048,128]{3,2,1,0:T(8,128)(2,1)}, u32[]{:S(2)}) %copy-start) | copy-done | bytes 4194328
  37.9 1.8 %sketch_products.1.vproj_ref = bf16[8,128,128]{2,1,0:T(8,128)(2,1)S(1)} custom-call(s32[8]{0:T(128)S(1)} %bitcast.19, bf16[128,2048]{1,0:T(8,128)(2,1)S(1)} %bitcast.17, bf16[8,2048,128]{2,1,0:T(8,128)(2,1)S(1)} %bitcast.14), custom_call_target="tpu_custom_call" | custom-call | flops 536870912 | bytes 4194304 | tf_op jit(solution)/shard_map/sketch_products/pallas_call | solution.py:378
  39.8 0.1 collective-permute-start.13
  39.9 1.9 %core_products.3 = (f32[8,128,128]{2,1,0:T(8,128)S(1)}, f32[8,128,128]{2,1,0:T(8,128)S(1)}) custom-call(s32[2]{0:T(128)S(1)} %pad_add_fusion.pos_ref, bf16[8,256,128]{2,1,0:T(8,128)(2,1)S(1)} %copy-done.4, bf16[8,256,128]{2,1,0:T(8,128)(2,1)S(1)} %copy-done.6, bf16[8,256,128]{2,1,0:T(8,128)(2,1)} %collective-permute-done.4.refs_2_, ...), custom_call_target="tpu_custom_call" | custom-call | flops 402653184 | bytes 1572864 | tf_op jit(solution)/shard_map/core_products/pallas_call | solution.py:399
  41.7 0.4 collective-permute-start.14
  42.1 0.2 collective-permute-start.15
  42.3 0.8 %core_products.5 = f32[8,128,128]{2,1,0:T(8,128)S(1)} custom-call(s32[2]{0:T(128)S(1)} %pad_add_fusion.pos_ref, bf16[8,256,128]{2,1,0:T(8,128)(2,1)S(1)} %collective-permute-done.7.refs_0_, bf16[1,512,128]{2,1,0:T(8,128)(2,1)S(1)} %copy-done.3, bf16[1,512,128]{2,1,0:T(8,128)(2,1)S(1)} %collective-permute-done.refs_4_.refs_2_, ...), custom_call_target="tpu_custom_call" | custom-call | flops 134217728 | bytes 524288 | tf_op jit(solution)/shard_map/core_products/pallas_call | solution.py:399
  43.2 0.4 collective-permute-start.12
  43.5 0.2 collective-permute-start.17
  44.4 0.8 %core_products.4.own_ref = f32[8,128,128]{2,1,0:T(8,128)S(1)} custom-call(s32[2]{0:T(128)S(1)} %pad_add_fusion.pos_ref, bf16[8,256,128]{2,1,0:T(8,128)(2,1)S(1)} %collective-permute-done.7.refs_0_, bf16[1,512,128]{2,1,0:T(8,128)(2,1)S(1)} %copy-done.3, bf16[1,512,128]{2,1,0:T(8,128)(2,1)S(1)} %collective-permute-done.refs_4_.refs_2_, ...), custom_call_target="tpu_custom_call" | custom-call | flops 134217728 | bytes 524288 | tf_op jit(solution)/shard_map/core_products/pallas_call | solution.py:399
  45.3 0.9 %collective-permute-done.17.refs_11_ = bf16[8,256,128]{2,1,0:T(8,128)(2,1)S(1)} collective-permute-done((bf16[8,256,128]{2,1,0:T(8,128)(2,1)}, bf16[8,256,128]{2,1,0:T(8,128)(2,1)S(1)}, u32[]{:S(2)}, u32[]{:S(2)}) %collective-permute-start.17) | collective-permute-done | bytes 524320 | tf_op jit(solution)/shard_map/ppermute | solution.py:306
  46.2 17.7 %recompress_store.1 = (bf16[8,2048,128]{2,1,0:T(8,128)(2,1)}, bf16[8,2048,128]{2,1,0:T(8,128)(2,1)}) custom-call(s32[2]{0:T(128)S(1)} %pad_add_fusion.pos_ref, s32[8]{0:T(128)S(1)} %bitcast.20, s32[8]{0:T(128)S(1)} %bitcast.21, s32[8]{0:T(128)S(1)} %copy-done.13, s32[1]{0:T(128)S(6)} %copy.16.col_rank_ref, bf16[8,2048,128]{2,1,0:T(8,128)(2,1)S(1)} %bitcast.16, ...), custom_call_target="tpu_custom_call" | custom-call | flops 4294967296 | bytes 20971520 | tf_op jit(solution)/shard_map/recompress_store/pallas_call | solution.py:425
  (41 shorter events, 0.1 us)
Async XLA Ops:
  0.6 35.0 %copy-start.7 = (s32[8,1]{0,1:T(1,128)S(1)}, s32[8,1]{0,1:T(1,128)}, u32[]{:S(2)}) copy-start(s32[8,1]{0,1:T(1,128)} %param.13) | copy-start | bytes 100
  0.6 18.3 %collective-permute-start.2 = (bf16[8,256,128]{2,1,0:T(8,128)(2,1)}, bf16[8,256,128]{2,1,0:T(8,128)(2,1)S(1)}, u32[]{:S(2)}, u32[]{:S(2)}) collective-permute-start(bf16[8,256,128]{2,1,0:T(8,128)(2,1)} %refs_0_), channel_id=1, source_target_pairs={{0,2},{1,3},{2,0},{3,1},{4,6},{5,7},{6,4},{7,5},{8,10},{9,11},{10,... | collective-permute-start | bytes 1572872 | tf_op jit(solution)/shard_map/ppermute | solution.py:306
  3.6 16.1 %collective-permute-start.3 = (bf16[8,256,128]{2,1,0:T(8,128)(2,1)}, bf16[8,256,128]{2,1,0:T(8,128)(2,1)S(1)}, u32[]{:S(2)}, u32[]{:S(2)}) collective-permute-start(bf16[8,256,128]{2,1,0:T(8,128)(2,1)} %refs_4_.1), channel_id=1, source_target_pairs={{0,4},{1,5},{2,6},{3,7},{4,0},{5,1},{6,2},{7,3},{8,12},{9,13},{10,... | collective-permute-start | bytes 1572872 | tf_op jit(solution)/shard_map/ppermute | solution.py:306
  5.2 7.0 %collective-permute-start = (bf16[1,512,128]{2,1,0:T(8,128)(2,1)}, bf16[1,512,128]{2,1,0:T(8,128)(2,1)S(1)}, u32[]{:S(2)}, u32[]{:S(2)}) collective-permute-start(bf16[1,512,128]{2,1,0:T(8,128)(2,1)} %refs_1_.3), channel_id=1, source_target_pairs={{0,8},{8,16},{16,24},{24,0},{1,9},{9,17},{17,25},{25,1},{2,10},{10... | collective-permute-start | bytes 393224 | tf_op jit(solution)/shard_map/ppermute | solution.py:350
  6.7 21.8 %collective-permute-start.4 = (bf16[8,256,128]{2,1,0:T(8,128)(2,1)}, bf16[8,256,128]{2,1,0:T(8,128)(2,1)}, u32[]{:S(2)}, u32[]{:S(2)}) collective-permute-start(bf16[8,256,128]{2,1,0:T(8,128)(2,1)} %refs_0_), channel_id=1, source_target_pairs={{0,4},{1,5},{2,6},{3,7},{4,0},{5,1},{6,2},{7,3},{8,12},{9,13},{10,... | collective-permute-start | bytes 1572872 | tf_op jit(solution)/shard_map/ppermute | solution.py:306
  7.2 21.3 %collective-permute-start.5 = (bf16[8,256,128]{2,1,0:T(8,128)(2,1)}, bf16[8,256,128]{2,1,0:T(8,128)(2,1)}, u32[]{:S(2)}, u32[]{:S(2)}) collective-permute-start(bf16[8,256,128]{2,1,0:T(8,128)(2,1)} %refs_4_.1), channel_id=1, source_target_pairs={{0,2},{1,3},{2,0},{3,1},{4,6},{5,7},{6,4},{7,5},{8,10},{9,11},{10,... | collective-permute-start | bytes 1572872 | tf_op jit(solution)/shard_map/ppermute | solution.py:306
  12.1 6.8 %collective-permute-start.1 = (bf16[1,512,128]{2,1,0:T(8,128)(2,1)S(1)}, bf16[1,512,128]{2,1,0:T(8,128)(2,1)S(1)}, u32[]{:S(2)}, u32[]{:S(2)}) collective-permute-start(bf16[1,512,128]{2,1,0:T(8,128)(2,1)S(1)} %collective-permute-done.refs_4_.refs_2_), channel_id=1, source_target_pairs={{0,8},{8,16},{16,24},{24,0},{1,9},{9,17},{17,25},{25,1},{2,10},{10... | collective-permute-start | bytes 393224 | tf_op jit(solution)/shard_map/ppermute | solution.py:350
  12.1 2.2 %copy-start.1 = (bf16[8,1,2048,128]{3,2,1,0:T(8,128)(2,1)S(1)}, bf16[8,1,2048,128]{3,2,1,0:T(8,128)(2,1)}, u32[]{:S(2)}) copy-start(bf16[8,1,2048,128]{3,2,1,0:T(8,128)(2,1)} %param.11) | copy-start | bytes 12582916
  14.3 6.0 %copy-start.11 = (bf16[1,512,128]{2,1,0:T(8,128)(2,1)S(1)}, bf16[1,512,128]{2,1,0:T(8,128)(2,1)}, u32[]{:S(2)}) copy-start(bf16[1,512,128]{2,1,0:T(8,128)(2,1)} %refs_0_.1) | copy-start | bytes 393220
  14.3 12.1 %copy-start.3 = (bf16[1,512,128]{2,1,0:T(8,128)(2,1)S(1)}, bf16[1,512,128]{2,1,0:T(8,128)(2,1)}, u32[]{:S(2)}) copy-start(bf16[1,512,128]{2,1,0:T(8,128)(2,1)} %refs_1_.3) | copy-start | bytes 393220
  15.6 24.2 %copy-start.4 = (bf16[8,256,128]{2,1,0:T(8,128)(2,1)S(1)}, bf16[8,256,128]{2,1,0:T(8,128)(2,1)}, u32[]{:S(2)}) copy-start(bf16[8,256,128]{2,1,0:T(8,128)(2,1)} %refs_0_) | copy-start | bytes 1572868
  18.9 0.8 %copy-start.5 = (bf16[8,256,128]{2,1,0:T(8,128)(2,1)}, bf16[8,256,128]{2,1,0:T(8,128)(2,1)S(1)}, u32[]{:S(2)}) copy-start(bf16[8,256,128]{2,1,0:T(8,128)(2,1)S(1)} %collective-permute-done.2.refs_1_) | copy-start | bytes 1572868
  19.7 8.9 %copy-start.9 = (bf16[8,256,128]{2,1,0:T(8,128)(2,1)}, bf16[8,256,128]{2,1,0:T(8,128)(2,1)S(1)}, u32[]{:S(2)}) copy-start(bf16[8,256,128]{2,1,0:T(8,128)(2,1)S(1)} %collective-permute-done.3.refs_8_) | copy-start | bytes 1572868
  19.7 6.8 %collective-permute-start.8 = (bf16[1,512,128]{2,1,0:T(8,128)(2,1)S(1)}, bf16[1,512,128]{2,1,0:T(8,128)(2,1)S(1)}, u32[]{:S(2)}, u32[]{:S(2)}) collective-permute-start(bf16[1,512,128]{2,1,0:T(8,128)(2,1)S(1)} %collective-permute-done.1.refs_5_.refs_3_), channel_id=1, source_target_pairs={{0,8},{8,16},{16,24},{24,0},{1,9},{9,17},{17,25},{25,1},{2,10},{10... | collective-permute-start | bytes 393224 | tf_op jit(solution)/shard_map/ppermute | solution.py:350
  20.3 8.3 %collective-permute-start.6 = (bf16[1,512,128]{2,1,0:T(8,128)(2,1)S(1)}, bf16[1,512,128]{2,1,0:T(8,128)(2,1)S(1)}, u32[]{:S(2)}, u32[]{:S(2)}) collective-permute-start(bf16[1,512,128]{2,1,0:T(8,128)(2,1)S(1)} %copy-done.11), channel_id=1, source_target_pairs={{0,8},{8,16},{16,24},{24,0},{1,9},{9,17},{17,25},{25,1},{2,10},{10... | collective-permute-start | bytes 393224 | tf_op jit(solution)/shard_map/ppermute | solution.py:350
  27.3 12.4 %collective-permute-start.9 = (bf16[4,512,128]{2,1,0:T(8,128)(2,1)}, bf16[4,512,128]{2,1,0:T(8,128)(2,1)S(1)}, u32[]{:S(2)}, u32[]{:S(2)}) collective-permute-start(bf16[4,512,128]{2,1,0:T(8,128)(2,1)} %pad_maximum_fusion), channel_id=1, source_target_pairs={{0,1},{1,0},{2,3},{3,2},{4,5},{5,4},{6,7},{7,6},{8,9},{9,8},{10,11... | collective-permute-start | bytes 1572872 | tf_op jit(solution)/shard_map/ppermute | solution.py:306
  28.6 13.7 %collective-permute-start.7 = (bf16[8,256,128]{2,1,0:T(8,128)(2,1)}, bf16[8,256,128]{2,1,0:T(8,128)(2,1)S(1)}, u32[]{:S(2)}, u32[]{:S(2)}) collective-permute-start(bf16[8,256,128]{2,1,0:T(8,128)(2,1)} %collective-permute-done.4.refs_2_), channel_id=1, source_target_pairs={{0,2},{1,3},{2,0},{3,1},{4,6},{5,7},{6,4},{7,5},{8,10},{9,11},{10,... | collective-permute-start | bytes 1572872 | tf_op jit(solution)/shard_map/ppermute | solution.py:306
  29.0 14.5 %collective-permute-start.16 = (bf16[8,256,128]{2,1,0:T(8,128)(2,1)}, bf16[8,256,128]{2,1,0:T(8,128)(2,1)}, u32[]{:S(2)}, u32[]{:S(2)}) collective-permute-start(bf16[8,256,128]{2,1,0:T(8,128)(2,1)} %collective-permute-done.5.refs_6_), channel_id=1, source_target_pairs={{0,4},{1,5},{2,6},{3,7},{4,0},{5,1},{6,2},{7,3},{8,12},{9,13},{10,... | collective-permute-start | bytes 1572872 | tf_op jit(solution)/shard_map/ppermute | solution.py:306
  30.7 11.0 %collective-permute-start.11 = (bf16[1,512,128]{2,1,0:T(8,128)(2,1)S(1)}, bf16[1,512,128]{2,1,0:T(8,128)(2,1)S(1)}, u32[]{:S(2)}, u32[]{:S(2)}) collective-permute-start(bf16[1,512,128]{2,1,0:T(8,128)(2,1)S(1)} %copy-done.11), channel_id=1, source_target_pairs={{0,24},{8,0},{16,8},{24,16},{1,25},{9,1},{17,9},{25,17},{2,26},{10... | collective-permute-start | bytes 393224 | tf_op jit(solution)/shard_map/ppermute | solution.py:350
  34.3 7.8 %collective-permute-start.10 = (bf16[1,512,128]{2,1,0:T(8,128)(2,1)S(1)}, bf16[1,512,128]{2,1,0:T(8,128)(2,1)}, u32[]{:S(2)}, u32[]{:S(2)}) collective-permute-start(bf16[1,512,128]{2,1,0:T(8,128)(2,1)S(1)} %collective-permute-done.6.refs_1_), channel_id=1, source_target_pairs={{0,8},{8,16},{16,24},{24,0},{1,9},{9,17},{17,25},{25,1},{2,10},{10... | collective-permute-start | bytes 393224 | tf_op jit(solution)/shard_map/ppermute | solution.py:350
  35.7 2.2 %copy-start = (bf16[8,1,2048,128]{3,2,1,0:T(8,128)(2,1)S(1)}, bf16[8,1,2048,128]{3,2,1,0:T(8,128)(2,1)}, u32[]{:S(2)}) copy-start(bf16[8,1,2048,128]{3,2,1,0:T(8,128)(2,1)} %param.12) | copy-start | bytes 12582916
  37.8 1.9 %copy-start.8 = (bf16[8,256,128]{2,1,0:T(8,128)(2,1)S(1)}, bf16[8,256,128]{2,1,0:T(8,128)(2,1)}, u32[]{:S(2)}) copy-start(bf16[8,256,128]{2,1,0:T(8,128)(2,1)} %refs_4_.1) | copy-start | bytes 1572868
  37.8 2.0 %copy-start.6 = (bf16[8,256,128]{2,1,0:T(8,128)(2,1)S(1)}, bf16[8,256,128]{2,1,0:T(8,128)(2,1)}, u32[]{:S(2)}) copy-start(bf16[8,256,128]{2,1,0:T(8,128)(2,1)} %copy-done.5) | copy-start | bytes 1572868
  37.8 4.3 %copy-start.10 = (bf16[8,256,128]{2,1,0:T(8,128)(2,1)S(1)}, bf16[8,256,128]{2,1,0:T(8,128)(2,1)}, u32[]{:S(2)}) copy-start(bf16[8,256,128]{2,1,0:T(8,128)(2,1)} %copy-done.9) | copy-start | bytes 1572868
  39.7 6.5 %copy-start.2 = (bf16[8,1,2048,128]{3,2,1,0:T(8,128)(2,1)S(1)}, bf16[8,1,2048,128]{3,2,1,0:T(8,128)(2,1)}, u32[]{:S(2)}) copy-start(bf16[8,1,2048,128]{3,2,1,0:T(8,128)(2,1)} %param.11) | copy-start | bytes 12582916
  39.7 6.5 %copy-start.12 = (s32[8,1]{0,1:T(1,128)S(1)}, s32[8,1]{0,1:T(1,128)}, u32[]{:S(2)}) copy-start(s32[8,1]{0,1:T(1,128)} %param.14) | copy-start | bytes 100
  39.7 6.4 %copy-start.13 = (s32[8]{0:T(128)S(1)}, s32[8]{0:T(128)}, u32[]{:S(2)}) copy-start(s32[8]{0:T(128)} %row_rank_ref.1) | copy-start | bytes 100
  39.8 5.5 %collective-permute-start.13 = (bf16[8,256,128]{2,1,0:T(8,128)(2,1)S(1)}, bf16[8,256,128]{2,1,0:T(8,128)(2,1)S(1)}, u32[]{:S(2)}, u32[]{:S(2)}) collective-permute-start(bf16[8,256,128]{2,1,0:T(8,128)(2,1)S(1)} %copy-done.8), channel_id=1, source_target_pairs={{0,1},{1,0},{2,3},{3,2},{4,5},{5,4},{6,7},{7,6},{8,9},{9,8},{10,11... | collective-permute-start | bytes 1572872 | tf_op jit(solution)/shard_map/ppermute | solution.py:306
  41.7 3.5 %collective-permute-start.14 = (bf16[8,256,128]{2,1,0:T(8,128)(2,1)}, bf16[8,256,128]{2,1,0:T(8,128)(2,1)S(1)}, u32[]{:S(2)}, u32[]{:S(2)}) collective-permute-start(bf16[8,256,128]{2,1,0:T(8,128)(2,1)} %collective-permute-done.5.refs_6_), channel_id=1, source_target_pairs={{0,1},{1,0},{2,3},{3,2},{4,5},{5,4},{6,7},{7,6},{8,9},{9,8},{10,11... | collective-permute-start | bytes 1572872 | tf_op jit(solution)/shard_map/ppermute | solution.py:306
  42.1 3.1 %collective-permute-start.15 = (bf16[8,256,128]{2,1,0:T(8,128)(2,1)S(1)}, bf16[8,256,128]{2,1,0:T(8,128)(2,1)S(1)}, u32[]{:S(2)}, u32[]{:S(2)}) collective-permute-start(bf16[8,256,128]{2,1,0:T(8,128)(2,1)S(1)} %copy-done.10), channel_id=1, source_target_pairs={{0,1},{1,0},{2,3},{3,2},{4,5},{5,4},{6,7},{7,6},{8,9},{9,8},{10,11... | collective-permute-start | bytes 1572872 | tf_op jit(solution)/shard_map/ppermute | solution.py:306
  43.2 2.1 %collective-permute-start.12 = (f32[8,128,128]{2,1,0:T(8,128)S(1)}, f32[8,128,128]{2,1,0:T(8,128)S(1)}, u32[]{:S(2)}, u32[]{:S(2)}) collective-permute-start(f32[8,128,128]{2,1,0:T(8,128)S(1)} %core_products.5), channel_id=1, source_target_pairs={{0,1},{1,0},{2,3},{3,2},{4,5},{5,4},{6,7},{7,6},{8,9},{9,8},{10,11... | collective-permute-start | bytes 1572872 | tf_op jit(solution)/shard_map/ppermute | solution.py:306
  43.5 2.6 %collective-permute-start.17 = (bf16[8,256,128]{2,1,0:T(8,128)(2,1)}, bf16[8,256,128]{2,1,0:T(8,128)(2,1)S(1)}, u32[]{:S(2)}, u32[]{:S(2)}) collective-permute-start(bf16[8,256,128]{2,1,0:T(8,128)(2,1)} %collective-permute-done.16.refs_10_), channel_id=1, source_target_pairs={{0,1},{1,0},{2,3},{3,2},{4,5},{5,4},{6,7},{7,6},{8,9},{9,8},{10,11... | collective-permute-start | bytes 1572872 | tf_op jit(solution)/shard_map/ppermute | solution.py:306
